TPU v7x, 128 devices: a whole 4x4x4 slice. The times are simulated.
128 devices in a mesh: tok: 8 (over z, core), exp: 16 (over x, y).
Axes of the slice: x: 4, y: 4, z: 4, core: 2. Of those that a mesh axis runs over, the one named last changes fastest.
Arguments:
- tokens: bfloat16 [8192, 4096], P('tok', 'exp'), may hold values from -6 to 6
- cotangent: bfloat16 [8192, 4096], P('tok', 'exp'), may hold values from -1.5 to 1.5
- gates: float32 [8192, 16], P('tok'), may hold values from 0.05 to 1
- picks: int32 [8, 16], replicated, may hold values from 0 to 8, as said below
- w_in: bfloat16 [16, 4096, 8192], P('exp', None, 'tok'), may hold values from -0.09375 to 0.09375
- w_out: bfloat16 [16, 8192, 4096], P('exp', 'tok'), may hold values from -0.0625 to 0.0625
Outputs:
- mixed: bfloat16 [8192, 4096], P('tok', 'exp')
- d_tokens: bfloat16 [8192, 4096], P('tok', 'exp')
- d_gates: float32 [8192, 16], P('tok')
Inputs may be any that keep to these rules, and one draw needn't show every extreme that they name: `picks`: each column has exactly 6 entries below 8; the value 8 means that the expert takes no block of that tile.
All inputs are finite; a program needn't handle non-finite values.
Results may differ from a plain program's by a relative error of at most 0.0069.
Values may be sent and summed in bfloat16 or wider, within the bound.
No kernel may reach another device: no remote copies, remote signals or barrier semaphores. Data moves between devices by JAX's collectives and lax.ppermute only.
A program may use at most 128 MiB of HBM per device.

v0:
```python
import jax
import jax.numpy as jnp
from jax import lax
from jax.sharding import PartitionSpec as P

D = 4096
BLK = 128


def gelu_tanh(value):
    return jax.nn.gelu(value, approximate=True)


def on_device(tokens, cotangent, gates, picks, w_in, w_out):
    tok_count = lax.axis_size("tok")
    exp_count = lax.axis_size("exp")
    my_tile = lax.axis_index("tok")
    my_expert = lax.axis_index("exp")
    capacity = 3 * tok_count // 4
    blocks = tokens.shape[0] // BLK
    slice_width = tokens.shape[1]
    experts = gates.shape[1]
    tile_picks = lax.dynamic_slice_in_dim(picks, my_tile, 1, 0)[0]
    onehot = (tile_picks[:, None] == jnp.arange(blocks, dtype=jnp.int32)[None, :]).astype(
        jnp.float32
    )
    onehot_low = onehot.astype(jnp.bfloat16)
    tok_three = tokens.reshape(blocks, BLK, slice_width)
    cot_three = cotangent.reshape(blocks, BLK, slice_width)
    gate_three = gates.reshape(blocks, BLK, experts)
    x_slot = jnp.einsum(
        "eb,brc->rec", onehot_low, tok_three, preferred_element_type=jnp.float32
    ).astype(jnp.bfloat16)
    dy_slot = jnp.einsum("eb,brc->rec", onehot_low, cot_three, preferred_element_type=jnp.float32)
    gate_slot = jnp.einsum("eb,bre->re", onehot, gate_three, precision=lax.Precision.HIGHEST)
    g_slot = (gate_slot[:, :, None] * dy_slot).astype(jnp.bfloat16)
    send_x = x_slot.reshape(BLK, experts * slice_width)
    send_g = g_slot.reshape(BLK, experts * slice_width)
    wide_x = jnp.broadcast_to(send_x[:, None, :], (BLK, tok_count, experts * slice_width)).reshape(
        BLK, tok_count * experts * slice_width
    )
    wide_g = jnp.broadcast_to(send_g[:, None, :], (BLK, tok_count, experts * slice_width)).reshape(
        BLK, tok_count * experts * slice_width
    )
    rows_x, rows_g = (
        lax.all_to_all(wide_x, ("tok", "exp"), split_axis=1, concat_axis=1, tiled=True),
        lax.all_to_all(wide_g, ("tok", "exp"), split_axis=1, concat_axis=1, tiled=True),
    )
    rows_x = rows_x.reshape(BLK, tok_count, D)
    rows_g = rows_g.reshape(BLK, tok_count, D)
    column = lax.dynamic_slice_in_dim(picks, my_expert, 1, 1)[:, 0]
    taken_tiles = jnp.argsort((column >= blocks).astype(jnp.int32), stable=True)[:capacity]
    chosen_x = jnp.take(rows_x, taken_tiles, axis=1).reshape(BLK * capacity, D)
    chosen_g = jnp.take(rows_g, taken_tiles, axis=1).reshape(BLK * capacity, D)
    hidden = jnp.dot(chosen_x, w_in[0], preferred_element_type=jnp.float32)
    act, gelu_back = jax.vjp(gelu_tanh, hidden)
    forward_part = jnp.dot(act.astype(jnp.bfloat16), w_out[0], preferred_element_type=jnp.float32)
    act_grad = lax.dot_general(
        chosen_g, w_out[0], (((1,), (1,)), ((), ())), preferred_element_type=jnp.float32
    )
    hidden_grad = gelu_back(act_grad)[0].astype(jnp.bfloat16)
    back_part = lax.dot_general(
        hidden_grad, w_in[0], (((1,), (1,)), ((), ())), preferred_element_type=jnp.float32
    )

    def spread(part_rows):
        empty = jnp.zeros((BLK, tok_count, D), jnp.bfloat16)
        return empty.at[:, taken_tiles].set(
            part_rows.astype(jnp.bfloat16).reshape(BLK, capacity, D)
        )

    out_send = spread(forward_part).reshape(BLK, tok_count * D)
    grad_send = spread(back_part).reshape(BLK, tok_count * D)
    out_recv, grad_recv = (
        lax.all_to_all(out_send, ("tok", "exp"), split_axis=1, concat_axis=1, tiled=True),
        lax.all_to_all(grad_send, ("tok", "exp"), split_axis=1, concat_axis=1, tiled=True),
    )
    expert_out = jnp.sum(
        out_recv.reshape(BLK, tok_count, exp_count, slice_width).astype(jnp.float32), axis=1
    ).astype(jnp.bfloat16)
    expert_grad = jnp.sum(
        grad_recv.reshape(BLK, tok_count, exp_count, slice_width).astype(jnp.float32), axis=1
    ).astype(jnp.bfloat16)
    out_float = expert_out.astype(jnp.float32)
    mixed = jnp.einsum(
        "eb,rec->brc", onehot, gate_slot[:, :, None] * out_float, precision=lax.Precision.HIGHEST
    )
    d_tokens = jnp.einsum(
        "eb,rec->brc", onehot, expert_grad.astype(jnp.float32), precision=lax.Precision.HIGHEST
    )
    partial_gate = jnp.sum(dy_slot * out_float, axis=2)
    local_grad = jnp.einsum("eb,re->bre", onehot, partial_gate, precision=lax.Precision.HIGHEST)
    d_gates = lax.psum(local_grad, "exp")
    return (
        mixed.reshape(blocks * BLK, slice_width).astype(jnp.bfloat16),
        d_tokens.reshape(blocks * BLK, slice_width).astype(jnp.bfloat16),
        d_gates.reshape(blocks * BLK, experts),
    )


def solution(mesh):
    return jax.shard_map(
        on_device,
        mesh=mesh,
        in_specs=(
            P("tok", "exp"),
            P("tok", "exp"),
            P("tok", None),
            P(),
            P("exp", None, "tok"),
            P("exp", "tok", None),
        ),
        out_specs=(P("tok", "exp"), P("tok", "exp"), P("tok", None)),
        check_vma=False,
    )
```

profile of v0, /device:TPU:0, one launch (start us, length us, event | category | flops | bytes accessed | tf_op | source)
XLA Modules:
  0.0 730.1 jit_solution(1939612881902488900)
XLA Ops:
  10.5 4.3 broadcast_in_dim.32
  14.8 12.1 %all-to-all-start = ((bf16[128,128,256]{0,2,1:T(8,128)(2,1)}), bf16[128,128,256]{0,2,1:T(8,128)(2,1)}, u32[]{:S(2)}, u32[]{:S(2)}) async-start(bf16[128,128,256]{0,2,1:T(8,128)(2,1)} %bitcast.79), calls=%async_computation | async-start | bytes 16777216 | tf_op jit(solution)/shard_map/all_to_all | solution.py:46
  28.1 98.3 %all-to-all-done = bf16[128,128,256]{0,2,1:T(8,128)(2,1)} async-done(((bf16[128,128,256]{0,2,1:T(8,128)(2,1)}), bf16[128,128,256]{0,2,1:T(8,128)(2,1)}, u32[]{:S(2)}, u32[]{:S(2)}) %all-to-all-start) | async-done | bytes 8388640 | tf_op jit(solution)/shard_map/all_to_all | solution.py:46
  126.4 11.7 %copy.42 = bf16[128,8,4096]{2,0,1:T(8,128)(2,1)} copy(bf16[128,8,4096]{0,2,1:T(8,128)(2,1)} %bitcast.9) | data formatting | bytes 16777216 | tf_op jit(solution)/shard_map/reshape | solution.py:49
  138.1 7.5 %gather_fusion = bf16[6,128,4096]{2,1,0:T(8,128)(2,1)} fusion(bf16[128,8,4096]{2,0,1:T(8,128)(2,1)} %copy.42, s32[1024]{0:T(1024)S(1)} %pad_clamp_fusion), kind=kCustom, calls=%fused_computation.clone | custom fusion | bytes 12582936 | tf_op jit(solution)/shard_map/jit(_take)/gather | solution.py:53
  149.1 6.7 copy.43
  155.8 10.2 %reshape.82 = bf16[768,4096]{1,0:T(8,128)(2,1)} reshape(bf16[128,6,4096]{2,1,0:T(8,128)(2,1)} %copy.43) | data formatting | bytes 12582912 | tf_op jit(solution)/shard_map/reshape | solution.py:53
  166.0 10.9 %fusion.6 = f32[768,1024]{1,0:T(8,128)S(1)} fusion(bf16[768,4096]{1,0:T(8,128)(2,1)} %reshape.82, bf16[1,4096,1024]{2,1,0:T(8,128)(2,1)} %param.12), kind=kOutput, calls=%fused_computation.10 | convolution fusion | flops 6442450944 | bytes 17825792 | tf_op jit(solution)/shard_map/dot_general | solution.py:55
  178.6 12.2 %fusion.11 = bf16[768,4096]{1,0:T(8,128)(2,1)} fusion(bf16[1,1024,4096]{2,1,0:T(8,128)(2,1)} %param.13, f32[768,1024]{1,0:T(8,128)S(1)} %fusion.6), kind=kOutput, calls=%fused_computation.13 | convolution fusion | flops 6452674560 | bytes 17825792 | tf_op jit(solution)/shard_map/dot_general | solution.py:57
  190.8 10.3 %reshape.109 = bf16[128,6,4096]{2,1,0:T(8,128)(2,1)} reshape(bf16[768,4096]{1,0:T(8,128)(2,1)} %fusion.11) | data formatting | bytes 12582912 | tf_op jit(solution)/shard_map/reshape | solution.py:69
  201.1 9.6 %copy.44 = bf16[6,128,4096]{2,1,0:T(8,128)(2,1)} copy(bf16[6,128,4096]{2,0,1:T(8,128)(2,1)} %bitcast.77) | data formatting | bytes 12582912 | tf_op jit(solution)/shard_map/reshape | solution.py:69
  210.6 4.4 broadcast.43.clone
  215.1 16.2 %scatter_fusion = bf16[128,8,4096]{2,0,1:T(8,128)(2,1)} fusion(bf16[128,8,4096]{2,0,1:T(8,128)(2,1)} %broadcast.43.clone, s32[6]{0:T(128)S(1)} %get-tuple-element.7, bf16[6,128,4096]{2,1,0:T(8,128)(2,1)} %copy.44), kind=kCustom, calls=%fused_computation.2 | custom fusion | bytes 18874392 | tf_op jit(solution)/shard_map/scatter | solution.py:68
  231.2 12.0 %copy.45 = bf16[128,8,4096]{0,2,1:T(8,128)(2,1)} copy(bf16[128,8,4096]{2,0,1:T(8,128)(2,1)} %scatter_fusion) | data formatting | bytes 16777216 | tf_op jit(solution)/shard_map/scatter | solution.py:68
  243.3 10.9 %all-to-all-start.1 = ((bf16[128,128,256]{0,2,1:T(8,128)(2,1)}), bf16[128,128,256]{0,2,1:T(8,128)(2,1)}, u32[]{:S(2)}, u32[]{:S(2)}) async-start(bf16[128,128,256]{0,2,1:T(8,128)(2,1)} %bitcast.81), calls=%async_computation.1 | async-start | bytes 16777216 | tf_op jit(solution)/shard_map/all_to_all | solution.py:75
  254.4 98.8 %all-to-all-done.1 = bf16[128,128,256]{0,2,1:T(8,128)(2,1)} async-done(((bf16[128,128,256]{0,2,1:T(8,128)(2,1)}), bf16[128,128,256]{0,2,1:T(8,128)(2,1)}, u32[]{:S(2)}, u32[]{:S(2)}) %all-to-all-start.1) | async-done | bytes 8388640 | tf_op jit(solution)/shard_map/all_to_all | solution.py:75
  353.3 5.0 reduce_sum.35
  363.9 108.0 %all_to_all.36 = bf16[128,128,256]{0,2,1:T(8,128)(2,1)} all-to-all(bf16[128,128,256]{0,2,1:T(8,128)(2,1)S(1)} %bitcast.82), channel_id=1, replica_groups=mesh['tok'=8,'exp'=16] {'tok','exp'}, dimensions={1} | all-to-all | bytes 16777216 | tf_op jit(solution)/shard_map/all_to_all | solution.py:47
  471.9 11.4 %copy.50 = bf16[128,8,4096]{2,0,1:T(8,128)(2,1)} copy(bf16[128,8,4096]{0,2,1:T(8,128)(2,1)} %bitcast.83) | data formatting | bytes 16777216 | tf_op jit(solution)/shard_map/reshape | solution.py:50
  483.3 7.6 %gather_fusion.1 = bf16[6,128,4096]{2,1,0:T(8,128)(2,1)} fusion(bf16[128,8,4096]{2,0,1:T(8,128)(2,1)} %copy.50, s32[1024]{0:T(1024)S(1)} %pad_clamp_fusion), kind=kCustom, calls=%fused_computation.1.clone | custom fusion | bytes 12582936 | tf_op jit(solution)/shard_map/jit(_take)/gather | solution.py:54
  494.3 6.8 copy.51
  501.1 10.3 %reshape.87 = bf16[768,4096]{1,0:T(8,128)(2,1)} reshape(bf16[128,6,4096]{2,1,0:T(8,128)(2,1)} %copy.51) | data formatting | bytes 12582912 | tf_op jit(solution)/shard_map/reshape | solution.py:54
  511.4 13.3 %fusion.20 = bf16[768,1024]{1,0:T(8,128)(2,1)S(1)} fusion(f32[768,1024]{1,0:T(8,128)} %copy-done.4, bf16[768,4096]{1,0:T(8,128)(2,1)} %reshape.87, bf16[1,1024,4096]{2,1,0:T(8,128)(2,1)} %param.13), kind=kOutput, calls=%fused_computation.24 | convolution fusion | flops 6458179584 | bytes 19398656 | tf_op jit(solution)/shard_map/dot_general | solution.py:58
  524.7 12.4 %fusion.8 = bf16[768,4096]{1,0:T(8,128)(2,1)} fusion(bf16[768,1024]{1,0:T(8,128)(2,1)S(1)} %fusion.20, bf16[1,4096,1024]{2,1,0:T(8,128)(2,1)} %param.12), kind=kOutput, calls=%fused_computation.12 | convolution fusion | flops 6445596672 | bytes 16252928 | tf_op jit(solution)/shard_map/dot_general | solution.py:62
  537.1 10.1 %reshape.117 = bf16[128,6,4096]{2,1,0:T(8,128)(2,1)} reshape(bf16[768,4096]{1,0:T(8,128)(2,1)} %fusion.8) | data formatting | bytes 12582912 | tf_op jit(solution)/shard_map/reshape | solution.py:69
  547.3 9.5 %copy.52 = bf16[6,128,4096]{2,1,0:T(8,128)(2,1)} copy(bf16[6,128,4096]{2,0,1:T(8,128)(2,1)} %bitcast.78) | data formatting | bytes 12582912 | tf_op jit(solution)/shard_map/reshape | solution.py:69
  561.1 16.2 %scatter_fusion.1 = bf16[128,8,4096]{2,0,1:T(8,128)(2,1)} fusion(bf16[128,8,4096]{2,0,1:T(8,128)(2,1)} %broadcast.43, s32[6]{0:T(128)S(1)} %get-tuple-element.7, bf16[6,128,4096]{2,1,0:T(8,128)(2,1)} %copy.52), kind=kCustom, calls=%fused_computation.3 | custom fusion | bytes 18874392 | tf_op jit(solution)/shard_map/scatter | solution.py:68
  577.2 11.9 %copy.53 = bf16[128,8,4096]{0,2,1:T(8,128)(2,1)} copy(bf16[128,8,4096]{2,0,1:T(8,128)(2,1)} %scatter_fusion.1) | data formatting | bytes 16777216 | tf_op jit(solution)/shard_map/scatter | solution.py:68
  589.2 5.9 all-to-all-start.3
  597.9 96.8 %all-to-all-done.3 = bf16[128,128,256]{0,2,1:T(8,128)(2,1)} async-done(((bf16[128,128,256]{0,2,1:T(8,128)(2,1)}), bf16[128,128,256]{0,2,1:T(8,128)(2,1)}, u32[]{:S(2)}, u32[]{:S(2)}) %all-to-all-start.3) | async-done | bytes 8388640 | tf_op jit(solution)/shard_map/all_to_all | solution.py:76
  694.7 5.0 reduce_sum.36
  701.8 19.7 %all-reduce.2.cloned.1.call-done = f32[1024,16]{0,1:T(8,128)} async-done(((f32[1024,16]{0,1:T(8,128)}), f32[1024,16]{0,1:T(8,128)}) %all-reduce.2.cloned.1.call-update) | async-done | bytes 65552 | tf_op jit(solution)/shard_map/psum | solution.py:93
  (41 shorter events, 29.5 us)
Async XLA Ops:
  7.2 352.0 %copy-start = (bf16[1024,256]{1,0:T(8,128)(2,1)S(1)}, bf16[1024,256]{1,0:T(8,128)(2,1)}, u32[]{:S(2)}) copy-start(bf16[1024,256]{1,0:T(8,128)(2,1)} %param.9) | copy-start | bytes 1572868
  14.8 12.2 %copy-start.3 = (s32[8,16]{1,0:T(8,128)S(1)}, s32[8,16]{1,0:T(8,128)}, u32[]{:S(2)}) copy-start(s32[8,16]{1,0:T(8,128)} %param.11) | copy-start | bytes 1540
  14.8 111.6 %all-to-all-start = ((bf16[128,128,256]{0,2,1:T(8,128)(2,1)}), bf16[128,128,256]{0,2,1:T(8,128)(2,1)}, u32[]{:S(2)}, u32[]{:S(2)}) async-start(bf16[128,128,256]{0,2,1:T(8,128)(2,1)} %bitcast.79), calls=%async_computation | async-start | bytes 16777216 | tf_op jit(solution)/shard_map/all_to_all | solution.py:46
  176.9 1.7 copy-start.4
  243.3 11.0 %copy-start.2 = (f32[1024,16]{0,1:T(8,128)S(1)}, f32[1024,16]{0,1:T(8,128)}, u32[]{:S(2)}) copy-start(f32[1024,16]{0,1:T(8,128)} %param.10) | copy-start | bytes 196612
  243.3 110.0 %all-to-all-start.1 = ((bf16[128,128,256]{0,2,1:T(8,128)(2,1)}), bf16[128,128,256]{0,2,1:T(8,128)(2,1)}, u32[]{:S(2)}, u32[]{:S(2)}) async-start(bf16[128,128,256]{0,2,1:T(8,128)(2,1)} %bitcast.81), calls=%async_computation.1 | async-start | bytes 16777216 | tf_op jit(solution)/shard_map/all_to_all | solution.py:75
  589.2 105.5 %all-to-all-start.3 = ((bf16[128,128,256]{0,2,1:T(8,128)(2,1)}), bf16[128,128,256]{0,2,1:T(8,128)(2,1)}, u32[]{:S(2)}, u32[]{:S(2)}) async-start(bf16[128,128,256]{0,2,1:T(8,128)(2,1)} %bitcast.80), calls=%async_computation.3 | async-start | bytes 16777216 | tf_op jit(solution)/shard_map/all_to_all | solution.py:76
  595.1 126.4 %all-reduce.2.cloned.1.call-start = ((), (), s32[]{:S(2)}) async-start(), calls=%async_computation.4 | async-start | bytes 131072 | tf_op jit(solution)/shard_map/psum | solution.py:93
  694.7 28.3 %copy-start.1 = (bf16[1024,256]{1,0:T(8,128)(2,1)S(1)}, bf16[1024,256]{1,0:T(8,128)(2,1)}, u32[]{:S(2)}) copy-start(bf16[1024,256]{1,0:T(8,128)(2,1)} %param.9) | copy-start | bytes 1572868
Sparse Core Ops, SparseCore 0:
  599.7 121.7 all-reduce.1
where the time goes:
time: 736 us; the launch traced here: 730 us
  waiting for transfers between devices  314 us (43%)
  local copies, waits for them, and re-layouts  193 us (26%)
  blocking collectives  108 us (15%)
  matrix products  53.3 us (7%)
  starting transfers between devices  29 us (4%)
  other arithmetic  18.2 us (2%)
  between operations  14.5 us (2%)
    all_to_all x1, blocking collectives, on_device(): lax.all_to_all(wide_g, ('tok', 'exp'), split_axis=1, concat_axis=1, tiled...  108 us
    all_to_all x1, waiting for transfers between devices, on_device(): lax.all_to_all(out_send, ('tok', 'exp'), split_axis=1, concat_axis=1, til...  98.8 us
    all_to_all x1, waiting for transfers between devices, on_device(): lax.all_to_all(wide_x, ('tok', 'exp'), split_axis=1, concat_axis=1, tiled...  98.3 us
    all_to_all x1, waiting for transfers between devices, on_device(): lax.all_to_all(grad_send, ('tok', 'exp'), split_axis=1, concat_axis=1, ti...  96.8 us
    scatter x4, local copies, waits for them, and re-layouts, spread(): empty.at[:, taken_tiles]  56.3 us
    reshape x4, local copies, waits for them, and re-layouts, spread(): part_rows.astype(jnp.bfloat16).reshape(BLK, capacity, D)  39.5 us
    psum x1, waiting for transfers between devices, on_device(): d_gates = lax.psum(local_grad, 'exp')  19.7 us
  transfers between devices with their start and end apart: 4, of which 4 were waited for; matrix products, arithmetic and copies ran while one was open for 2% of the time, Pallas kernels for 0%

commit v1 on v0

v1 whole, which is shorter than its diff:
```python
import functools

import jax
import jax.numpy as jnp
from jax import lax
from jax.experimental import pallas as pl
from jax.experimental.pallas import tpu as pltpu
from jax.sharding import PartitionSpec as P

D = 4096
BLK = 128
WIDTH = 256
SLICES = D // WIDTH
CAP = 6
OWN = CAP // 2
ROWS = OWN * BLK
UNITS = 1024
GELU_C = 0.7978845608028654
GELU_K = 0.044715
MIB = 1024 * 1024
ANY = pl.BlockSpec(memory_space=pl.ANY)
SMEM = pl.BlockSpec(memory_space=pltpu.SMEM)
VMEM = pl.BlockSpec(memory_space=pltpu.VMEM)


def params(mib=56):
    return pltpu.CompilerParams(vmem_limit_bytes=mib * MIB)


def cost(flops, nbytes):
    return pl.CostEstimate(flops=flops, bytes_accessed=nbytes, transcendentals=0)


def pick_body(count, ids, src, out, sems):
    copies = [
        pltpu.make_async_copy(src.at[ids[i]], out.at[i], sems.at[i]) for i in range(count)
    ]
    for copy in copies:
        copy.start()
    for copy in copies:
        copy.wait()


def pick_blocks(src, ids):
    count = ids.shape[0]
    return pl.pallas_call(
        functools.partial(pick_body, count),
        out_shape=jax.ShapeDtypeStruct((count, BLK, WIDTH), src.dtype),
        in_specs=[SMEM, ANY],
        out_specs=ANY,
        scratch_shapes=[pltpu.SemaphoreType.DMA((count,))],
        cost_estimate=cost(0, 2 * count * BLK * WIDTH * 2),
        name="pick_blocks",
    )(ids, src)


def hidden_body(tiles, x_all, wa, wb, act_a, act_b, der_a, der_b, x_v, sems):
    @pl.when(pl.program_id(0) == 0)
    def _():
        copies = [
            pltpu.make_async_copy(
                x_all.at[tiles[s], f],
                x_v.at[pl.ds(s * BLK, BLK), pl.ds(f * WIDTH, WIDTH)],
                sems.at[s, f],
            )
            for s in range(OWN)
            for f in range(SLICES)
        ]
        for copy in copies:
            copy.start()
        for copy in copies:
            copy.wait()

    for w, act, der in ((wa, act_a, der_a), (wb, act_b, der_b)):
        h = jnp.dot(x_v[...], w[...], preferred_element_type=jnp.float32)
        sq = h * h
        t = jnp.tanh(GELU_C * h * (1.0 + GELU_K * sq))
        half = 0.5 * (1.0 + t)
        act[...] = (h * half).astype(act.dtype)
        der[...] = half + (0.5 * GELU_C) * h * (1.0 - t * t) * (1.0 + (3.0 * GELU_K) * sq)


def hidden(tiles, x_all, w_in, w_in_other):
    cols = 256
    w_spec = pl.BlockSpec((D, cols), lambda i: (0, i))
    o_spec = pl.BlockSpec((ROWS, cols), lambda i: (0, i))
    act = jax.ShapeDtypeStruct((ROWS, UNITS), jnp.bfloat16)
    der = jax.ShapeDtypeStruct((ROWS, UNITS), jnp.float32)
    return pl.pallas_call(
        hidden_body,
        grid=(UNITS // cols,),
        out_shape=(act, act, der, der),
        in_specs=[SMEM, ANY, w_spec, w_spec],
        out_specs=(o_spec, o_spec, o_spec, o_spec),
        scratch_shapes=[
            pltpu.VMEM((ROWS, D), jnp.bfloat16),
            pltpu.SemaphoreType.DMA((OWN, SLICES)),
        ],
        compiler_params=params(),
        cost_estimate=cost(2 * ROWS * D * 2 * UNITS, 24 * MIB),
        name="hidden",
    )(tiles, x_all, w_in, w_in_other)


def back_body(dy, wa, wb, act_a, act_b, der_a, der_b, gate, dh_a, dh_b, dgate, dy_v, sems):
    step = pl.program_id(0)

    @pl.when(step == 0)
    def _():
        copies = [
            pltpu.make_async_copy(dy.at[f], dy_v.at[:, pl.ds(f * WIDTH, WIDTH)], sems.at[f])
            for f in range(SLICES)
        ]
        for copy in copies:
            copy.start()
        for copy in copies:
            copy.wait()
        dgate[...] = jnp.zeros_like(dgate)

    scale = gate[...]
    total = dgate[...]
    for w, act, der, dh in ((wa, act_a, der_a, dh_a), (wb, act_b, der_b, dh_b)):
        u = lax.dot_general(
            dy_v[...], w[...], (((1,), (1,)), ((), ())), preferred_element_type=jnp.float32
        )
        dh[...] = (scale * u * der[...]).astype(dh.dtype)
        total += jnp.sum(act[...].astype(jnp.float32) * u, axis=1, keepdims=True)
    dgate[...] = total


def back(dy, w_out, w_out_other, acts, ders, gate):
    cols = 256
    w_spec = pl.BlockSpec((cols, D), lambda i: (i, 0))
    o_spec = pl.BlockSpec((ROWS, cols), lambda i: (0, i))
    g_spec = pl.BlockSpec((ROWS, 1), lambda i: (0, 0))
    dh = jax.ShapeDtypeStruct((ROWS, UNITS), jnp.bfloat16)
    return pl.pallas_call(
        back_body,
        grid=(UNITS // cols,),
        out_shape=(dh, dh, jax.ShapeDtypeStruct((ROWS, 1), jnp.float32)),
        in_specs=[ANY, w_spec, w_spec, o_spec, o_spec, o_spec, o_spec, g_spec],
        out_specs=(o_spec, o_spec, g_spec),
        scratch_shapes=[
            pltpu.VMEM((ROWS, D), jnp.bfloat16),
            pltpu.SemaphoreType.DMA((SLICES,)),
        ],
        compiler_params=params(),
        cost_estimate=cost(2 * ROWS * D * 2 * UNITS, 24 * MIB),
        name="back",
    )(dy, w_out, w_out_other, *acts, *ders, gate)


def rows_out_body(act_a, act_b, wa, wb, gate, out):
    o = jnp.dot(act_a[...], wa[...], preferred_element_type=jnp.float32)
    o += jnp.dot(act_b[...], wb[...], preferred_element_type=jnp.float32)
    o = (o * gate[...]).astype(out.dtype)
    for f in range(out.shape[0]):
        out[f] = o[:, f * WIDTH : (f + 1) * WIDTH]


def rows_out(acts, w_out, w_out_other, gate):
    per = 2
    a_spec = pl.BlockSpec((ROWS, UNITS), lambda i: (0, 0))
    w_spec = pl.BlockSpec((UNITS, per * WIDTH), lambda i: (0, i))
    return pl.pallas_call(
        rows_out_body,
        grid=(SLICES // per,),
        out_shape=jax.ShapeDtypeStruct((SLICES, ROWS, WIDTH), jnp.bfloat16),
        in_specs=[a_spec, a_spec, w_spec, w_spec, pl.BlockSpec((ROWS, 1), lambda i: (0, 0))],
        out_specs=pl.BlockSpec((per, ROWS, WIDTH), lambda i: (i, 0, 0)),
        compiler_params=params(),
        cost_estimate=cost(2 * ROWS * D * 2 * UNITS, 21 * MIB),
        name="rows_out",
    )(*acts, w_out, w_out_other, gate)


def rows_grad_body(tiles, dh_a, dh_b, wa, wb, out):
    dims = (((1,), (1,)), ((), ()))
    r = lax.dot_general(dh_a[...], wa[...], dims, preferred_element_type=jnp.float32)
    r += lax.dot_general(dh_b[...], wb[...], dims, preferred_element_type=jnp.float32)
    r = r.astype(out.dtype)
    out[...] = jnp.zeros_like(out)
    for s in range(OWN):
        for f in range(out.shape[1]):
            out[tiles[s], f] = r[s * BLK : (s + 1) * BLK, f * WIDTH : (f + 1) * WIDTH]


def rows_grad(tiles, dhs, w_in, w_in_other, tile_count):
    per = 2
    a_spec = pl.BlockSpec((ROWS, UNITS), lambda i: (0, 0))
    w_spec = pl.BlockSpec((per * WIDTH, UNITS), lambda i: (i, 0))
    return pl.pallas_call(
        rows_grad_body,
        grid=(SLICES // per,),
        out_shape=jax.ShapeDtypeStruct((tile_count, SLICES, BLK, WIDTH), jnp.bfloat16),
        in_specs=[SMEM, a_spec, a_spec, w_spec, w_spec],
        out_specs=pl.BlockSpec((tile_count, per, BLK, WIDTH), lambda i: (0, i, 0, 0)),
        compiler_params=params(),
        cost_estimate=cost(2 * ROWS * D * 2 * UNITS, 27 * MIB),
        name="rows_grad",
    )(tiles, *dhs, w_in, w_in_other)


def merge_body(count, ids, parts, out, total):
    total[...] = jnp.zeros_like(total)

    def step(i, carry):
        total[ids[i]] += parts[i].astype(jnp.float32)
        return carry

    lax.fori_loop(0, count, step, 0)
    out[...] = total[: out.shape[0]].astype(out.dtype)


def merge(parts, ids, blocks):
    count = parts.shape[0]
    return pl.pallas_call(
        functools.partial(merge_body, count),
        out_shape=jax.ShapeDtypeStruct((blocks, BLK, WIDTH), jnp.bfloat16),
        in_specs=[SMEM, VMEM],
        out_specs=VMEM,
        scratch_shapes=[pltpu.VMEM((blocks + 1, BLK, WIDTH), jnp.float32)],
        compiler_params=params(),
        cost_estimate=cost(0, (count + blocks) * BLK * WIDTH * 2 * 2),
        name="merge",
    )(ids, parts)


def exchange(value):
    return lax.all_to_all(value, "exp", split_axis=0, concat_axis=0, tiled=True)


def on_device(tokens, cotangent, gates, picks, w_in, w_out):
    tile_count = lax.axis_size("tok")
    my_tile = lax.axis_index("tok")
    my_expert = lax.axis_index("exp")
    core = my_tile % 2
    blocks = tokens.shape[0] // BLK
    experts = gates.shape[1]
    w_in, w_out = w_in[0], w_out[0]
    pairs = [(i, i ^ 1) for i in range(tile_count)]
    w_in_other = lax.ppermute(w_in, "tok", pairs)
    w_out_other = lax.ppermute(w_out, "tok", pairs)

    chosen = picks < blocks
    order = jnp.arange(tile_count, dtype=jnp.int32)
    rank = jnp.sum(
        jnp.where((order[None, :] < order[:, None])[:, :, None], chosen[None], False).astype(
            jnp.int32
        ),
        axis=1,
    )
    slot = jnp.arange(CAP, dtype=jnp.int32)
    at_slot = (chosen & (rank >= 0))[:, :, None] & (rank[:, :, None] == slot)
    slot_tile = jnp.sum(jnp.where(at_slot, order[:, None, None], 0), axis=0)
    slot_block = jnp.sum(jnp.where(at_slot, picks[:, :, None], 0), axis=0)
    slot_row = slot_tile * blocks + slot_block
    own_rows = lax.dynamic_slice_in_dim(slot_row, core * OWN, OWN, 1)
    own_tiles = lax.dynamic_slice(slot_tile, (my_expert, core * OWN), (1, OWN))[0]
    my_rows = lax.dynamic_index_in_dim(own_rows, my_expert, 0, False)
    tile_picks = lax.dynamic_index_in_dim(picks, my_tile, 0, False)

    cot_all = lax.all_gather(cotangent.reshape(blocks, BLK, WIDTH), "tok", tiled=True)
    gate_mine = lax.dynamic_index_in_dim(gates, my_expert, 1, False).reshape(blocks, BLK)
    gate_all = lax.all_gather(gate_mine, "tok", tiled=True)
    gate = jnp.take(gate_all, my_rows, axis=0, mode="clip").reshape(ROWS, 1)
    dy = exchange(pick_blocks(cot_all, own_rows.reshape(-1)).reshape(experts, ROWS, WIDTH))

    x_slot = pick_blocks(tokens.reshape(blocks, BLK, WIDTH), jnp.minimum(tile_picks, blocks - 1))
    x_all = lax.all_gather(exchange(x_slot), "tok")

    act_a, act_b, der_a, der_b = hidden(own_tiles, x_all, w_in, w_in_other)
    dh_a, dh_b, dgate = back(dy, w_out, w_out_other, (act_a, act_b), (der_a, der_b), gate)
    dx_all = rows_grad(own_tiles, (dh_a, dh_b), w_in, w_in_other, tile_count)
    out_rows = rows_out((act_a, act_b), w_out, w_out_other, gate)

    dx = lax.psum_scatter(dx_all, "tok", scatter_dimension=0)
    d_tokens = merge(exchange(dx), tile_picks, blocks)

    parts = exchange(out_rows).reshape(experts * OWN, BLK, WIDTH)
    mixed_all = merge(parts, own_rows.reshape(-1), tile_count * blocks)
    mixed = lax.psum_scatter(
        mixed_all.reshape(tile_count, blocks * BLK, WIDTH), "tok", scatter_dimension=0
    )

    spread = jnp.zeros((experts, CAP, BLK), jnp.float32)
    spread = lax.dynamic_update_slice(
        spread, dgate.reshape(1, OWN, BLK), (my_expert, core * OWN, jnp.int32(0))
    )
    grads = lax.psum(spread, ("tok", "exp"))
    here = slot_tile == my_tile
    here &= slot[None, :] < CAP
    taken = lax.dynamic_index_in_dim(chosen, my_tile, 0, False)
    mine = jnp.sum(jnp.where((here & taken[:, None])[:, :, None], grads, 0.0), axis=1)
    at_block = tile_picks[None, :] == jnp.arange(blocks, dtype=jnp.int32)[:, None]
    d_gates = jnp.where(at_block[:, None, :], mine.T[None], 0.0)
    return (
        mixed,
        d_tokens.reshape(blocks * BLK, WIDTH),
        d_gates.reshape(blocks * BLK, experts),
    )


def solution(mesh):
    return jax.shard_map(
        on_device,
        mesh=mesh,
        in_specs=(
            P("tok", "exp"),
            P("tok", "exp"),
            P("tok", None),
            P(),
            P("exp", None, "tok"),
            P("exp", "tok", None),
        ),
        out_specs=(P("tok", "exp"), P("tok", "exp"), P("tok", None)),
        check_vma=False,
    )
```

time: 736 us -> 401 us (0.54)
  waiting for transfers between devices: 314 us -> 11.7 us
  Pallas kernels: 0 us -> 197 us
  local copies, waits for them, and re-layouts: 193 us -> 6.56 us
  matrix products: 53.3 us -> 0 us
  blocking collectives: 108 us -> 159 us
  starting transfers between devices: 29 us -> 8.77 us
  other arithmetic: 18.2 us -> 1.83 us
    all_to_all x3 -> x2, waiting for transfers between devices: 294 us -> 10.9 us  [exchange(): return lax.all_to_all(value, 'exp', split_axis=0, concat_axis=0, tiled=True)]
    pallas_call x0 -> x8, Pallas kernels: none -> 197 us  [the longest x2 131 us: pick_blocks(): pl.pallas_call(functools.partial(pick_body, count), out_shape=jax.ShapeDt...]
    reshape x8 -> x1, local copies, waits for them, and re-layouts: 83.1 us -> 0.6 us  [on_device(): mixed_all = merge(parts, own_rows.reshape(-1), tile_count * blocks)]
    psum x0 -> x1, blocking collectives: none -> 71.3 us  [on_device(): grads = lax.psum(spread, ('tok', 'exp'))]
    scatter x4 -> x0, local copies, waits for them, and re-layouts: 56.3 us -> none  [spread(): empty.at[:, taken_tiles]]
    dot_general x8 -> x0, matrix products: 53.3 us -> none  [the longest x1 13.3 us: on_device(): lax.dot_general(chosen_g, w_out[0], (((1,), (1,)), ((), ())), preferred_e...]
    all_to_all x1 -> x2, blocking collectives: 108 us -> 73.5 us  [exchange(): return lax.all_to_all(value, 'exp', split_axis=0, concat_axis=0, tiled=True)]
    all_to_all x3 -> x2, starting transfers between devices: 28.9 us -> 8.03 us  [exchange(): return lax.all_to_all(value, 'exp', split_axis=0, concat_axis=0, tiled=True)]
  transfers between devices with their start and end apart: 4 -> 8, of which waited for: 4 -> 1; matrix products, arithmetic and copies ran while one was open for 2% -> 1% of each run, Pallas kernels for 0% -> 42%
where the time goes in v1:
time: 401 us; the launch traced here: 399 us
  Pallas kernels  197 us (49%)
  blocking collectives  159 us (40%)
  between operations  14 us (3%)
  waiting for transfers between devices  11.7 us (3%)
  starting transfers between devices  8.77 us (2%)
  local copies, waits for them, and re-layouts  6.56 us (2%)
    pallas_call x2, Pallas kernels, pick_blocks(): pl.pallas_call(functools.partial(pick_body, count), out_shape=jax.ShapeDt...  131 us
    all_to_all x2, blocking collectives, exchange(): return lax.all_to_all(value, 'exp', split_axis=0, concat_axis=0, tiled=True)  73.5 us
    psum x1, blocking collectives, on_device(): grads = lax.psum(spread, ('tok', 'exp'))  71.3 us
    pallas_call x1, Pallas kernels, hidden(): pl.pallas_call(hidden_body, grid=(UNITS // cols,), out_shape=(act, act, d...  15.3 us
    pallas_call x1, Pallas kernels, back(): pl.pallas_call(back_body, grid=(UNITS // cols,), out_shape=(dh, dh, jax.S...  15.1 us
    pallas_call x1, Pallas kernels, rows_grad(): pl.pallas_call(rows_grad_body, grid=(SLICES // per,), out_shape=jax.Shape...  14.4 us
    all_gather x1, blocking collectives, on_device(): gate_all = lax.all_gather(gate_mine, 'tok', tiled=True)  14 us
    pallas_call x1, Pallas kernels, rows_out(): pl.pallas_call(rows_out_body, grid=(SLICES // per,), out_shape=jax.ShapeD...  13.3 us
  transfers between devices with their start and end apart: 8, of which 1 were waited for; matrix products, arithmetic and copies ran while one was open for 1% of the time, Pallas kernels for 42%

profile of v1, /device:TPU:0, one launch (start us, length us, event | category | flops | bytes accessed | tf_op | source)
XLA Modules:
  0.0 398.8 jit_solution(17558581404414385849)
XLA Ops:
  7.2 0.7 all-gather.4.cloned.1.call-update
  8.0 1.2 broadcast_minimum_fusion
  9.2 33.7 %pick_blocks.2 = bf16[16,128,256]{2,1,0:T(8,128)(2,1)} custom-call(s32[16]{0:T(128)} %get-tuple-element.19.ids, bf16[8,128,256]{2,1,0:T(8,128)(2,1)} %bitcast.44), custom_call_target="tpu_custom_call" | custom-call | bytes 2097152 | tf_op jit(solution)/shard_map/pick_blocks/pallas_call | solution.py:46
  42.9 24.1 %all_to_all.20 = bf16[16,128,256]{2,1,0:T(8,128)(2,1)} all-to-all(bf16[16,128,256]{2,1,0:T(8,128)(2,1)} %pick_blocks.2), channel_id=1, replica_groups=mesh['tok'=8,'exp'=16] {'exp'}, dimensions={0} | all-to-all | bytes 2097152 | tf_op jit(solution)/shard_map/all_to_all | solution.py:230
  67.0 0.1 collective-permute-start
  67.1 0.5 collective-permute-start.1
  67.6 0.1 convert_reduce_fusion
  67.8 0.6 reshape.120.ids
  68.4 97.5 %pick_blocks.3 = bf16[48,128,256]{2,1,0:T(8,128)(2,1)} custom-call(s32[48]{0:T(128)} %reshape.120.ids, bf16[64,128,256]{2,1,0:T(8,128)(2,1)} %all-gather.4.cloned.1.call-done.src), custom_call_target="tpu_custom_call" | custom-call | bytes 6291456 | tf_op jit(solution)/shard_map/pick_blocks/pallas_call | solution.py:46
  166.0 3.9 all-to-all-start.2
  169.9 0.7 dynamic-slice_reduce_fusion.1.tiles
  170.6 0.2 dynamic-slice_reduce_fusion
  170.8 14.0 %all_gather.14 = f32[64,128]{1,0:T(8,128)S(1)} all-gather(f32[8,128]{1,0:T(8,128)S(1)} %bitcast.50), channel_id=1, replica_groups=mesh['tok'=8,'exp'=16] {'tok'}, dimensions={0}, use_global_device_ids=true | all-gather | bytes 36864 | tf_op jit(solution)/shard_map/all_gather | solution.py:265
  184.9 0.6 gather_fusion
  185.4 0.8 copy.22
  186.3 15.3 %hidden.1 = (bf16[384,1024]{1,0:T(8,128)(2,1)}, bf16[384,1024]{1,0:T(8,128)(2,1)}, f32[384,1024]{1,0:T(8,128)}, f32[384,1024]{1,0:T(8,128)}) custom-call(s32[3]{0:T(128)} %dynamic-slice_reduce_fusion.1.tiles, bf16[8,16,128,256]{3,2,1,0:T(8,128)(2,1)} %bitcast.40, bf16[4096,1024]{1,0:T(8,128)(2,1)} %bitcast.32, bf16[4096,1024]{1,0:T(8,128)(2,1)} %collective-permute-done.wb), custom_call_target="tpu_custom_call" | custom-call | flops 6442450944 | bytes 25165824 | tf_op jit(solution)/shard_map/hidden/pallas_call | solution.py:89
  201.5 10.9 %all-to-all-done.2.dy = bf16[16,384,256]{2,1,0:T(8,128)(2,1)S(1)} async-done(((bf16[16,384,256]{2,1,0:T(8,128)(2,1)}), bf16[16,384,256]{2,1,0:T(8,128)(2,1)S(1)}, u32[]{:S(2)}, u32[]{:S(2)}) %all-to-all-start.2) | async-done | bytes 3145760 | tf_op jit(solution)/shard_map/all_to_all | solution.py:230
  212.5 1.7 copy-done.2
  214.1 15.1 %back.1 = (bf16[384,1024]{1,0:T(8,128)(2,1)}, bf16[384,1024]{1,0:T(8,128)(2,1)}, f32[384,1]{1,0:T(8,128)}) custom-call(bf16[16,384,256]{2,1,0:T(8,128)(2,1)} %copy-done.2, bf16[1024,4096]{1,0:T(8,128)(2,1)} %bitcast.38, bf16[1024,4096]{1,0:T(8,128)(2,1)} %collective-permute-done.1.wb, bf16[384,1024]{1,0:T(8,128)(2,1)} %get-tuple-element.10.act_a, ...), custom_call_target="tpu_custom_call" | custom-call | flops 6442450944 | bytes 25165824 | tf_op jit(solution)/shard_map/back/pallas_call | solution.py:137
  229.3 14.4 %rows_grad.1 = bf16[8,16,128,256]{3,2,1,0:T(8,128)(2,1)} custom-call(s32[3]{0:T(128)} %dynamic-slice_reduce_fusion.1.tiles, bf16[384,1024]{1,0:T(8,128)(2,1)} %get-tuple-element.14.dh_a, bf16[384,1024]{1,0:T(8,128)(2,1)} %get-tuple-element.15.dh_b, bf16[4096,1024]{1,0:T(8,128)(2,1)} %bitcast.33, bf16[4096,1024]{1,0:T(8,128)(2,1)} %collective-permute-done.wb), custom_call_target="tpu_custom_call" | custom-call | flops 6442450944 | bytes 28311552 | tf_op jit(solution)/shard_map/rows_grad/pallas_call | solution.py:192
  243.8 13.3 %rows_out.1 = bf16[16,384,256]{2,1,0:T(8,128)(2,1)} custom-call(bf16[384,1024]{1,0:T(8,128)(2,1)} %get-tuple-element.10.act_a, bf16[384,1024]{1,0:T(8,128)(2,1)} %get-tuple-element.11.act_b, bf16[1024,4096]{1,0:T(8,128)(2,1)} %bitcast.39, bf16[1024,4096]{1,0:T(8,128)(2,1)} %collective-permute-done.1.wb, f32[384,1]{1,0:T(8,128)} %bitcast.43), custom_call_target="tpu_custom_call" | custom-call | flops 6442450944 | bytes 22020096 | tf_op jit(solution)/shard_map/rows_out/pallas_call | solution.py:165
  257.0 49.4 %all_to_all.21 = bf16[16,384,256]{2,1,0:T(8,128)(2,1)} all-to-all(bf16[16,384,256]{2,1,0:T(8,128)(2,1)} %rows_out.1), channel_id=1, replica_groups=mesh['tok'=8,'exp'=16] {'exp'}, dimensions={0} | all-to-all | bytes 6291456 | tf_op jit(solution)/shard_map/all_to_all | solution.py:230
  306.5 5.5 %merge.2 = bf16[64,128,256]{2,1,0:T(8,128)(2,1)} custom-call(s32[48]{0:T(128)} %reshape.120.ids, bf16[48,128,256]{2,1,0:T(8,128)(2,1)} %bitcast.36), custom_call_target="tpu_custom_call" | custom-call | bytes 14680064 | tf_op jit(solution)/shard_map/merge/pallas_call | solution.py:217
  312.0 4.2 %all-to-all-start.3 = ((bf16[16,128,256]{2,1,0:T(8,128)(2,1)}), bf16[16,128,256]{2,1,0:T(8,128)(2,1)S(1)}, u32[]{:S(2)}, u32[]{:S(2)}) async-start(bf16[16,128,256]{2,1,0:T(8,128)(2,1)} %bitcast.41), calls=%async_computation.5 | async-start | bytes 2097152 | tf_op jit(solution)/shard_map/all_to_all | solution.py:230
  316.3 0.1 copy.20
  316.5 0.1 reduce.2
  316.6 0.1 dynamic_update_slice.3
  316.8 71.3 %psum.7 = f32[16,6,128]{2,1,0:T(8,128)S(1)} all-reduce(f32[16,6,128]{2,1,0:T(8,128)S(1)} %dynamic_update_slice.3), channel_id=1, replica_groups=mesh['tok'=8,'exp'=16] {'tok','exp'}, use_global_device_ids=true, to_apply=%region_5.6 | all-reduce | flops 12288 | bytes 98304 | tf_op jit(solution)/shard_map/psum | solution.py:290
  388.1 0.1 select_reduce_fusion
  388.3 0.6 copy.26
  388.9 1.0 copy-done.3
  389.9 2.4 merge.3
  (42 shorter events, 0.7 us)
Async XLA Ops:
  7.2 163.6 %copy-start = (f32[1024,16]{0,1:T(8,128)S(1)}, f32[1024,16]{0,1:T(8,128)}, u32[]{:S(2)}) copy-start(f32[1024,16]{0,1:T(8,128)} %param.8) | copy-start | bytes 196612
  7.2 60.4 %copy-start.5 = (s32[8,16]{1,0:T(8,128)S(1)}, s32[8,16]{1,0:T(8,128)}, u32[]{:S(2)}) copy-start(s32[8,16]{1,0:T(8,128)} %param.9) | copy-start | bytes 1540
  7.2 61.2 %all-gather.4.cloned.1.call-start = ((), (), s32[]{:S(2)}) async-start(), calls=%async_computation.7 | async-start | bytes 4718592 | tf_op jit(solution)/shard_map/all_gather | solution.py:263
  7.9 178.3 %all-gather.6.cloned.1.call-start = ((), (), s32[]{:S(2)}) async-start(), calls=%async_computation.9 | async-start | bytes 9437184 | tf_op jit(solution)/shard_map/all_gather | solution.py:270
  9.2 307.2 %copy-start.6 = (s32[16]{0:T(128)}, s32[16]{0:T(128)S(1)}, u32[]{:S(2)}) copy-start(s32[16]{0:T(128)S(1)} %get-tuple-element.20.ids) | copy-start | bytes 196
  67.0 119.3 %collective-permute-start = (bf16[4096,1024]{1,0:T(8,128)(2,1)}, bf16[4096,1024]{1,0:T(8,128)(2,1)}, u32[]{:S(2)}, u32[]{:S(2)}) collective-permute-start(bf16[4096,1024]{1,0:T(8,128)(2,1)} %bitcast.31), channel_id=1, source_target_pairs={{0,16},{16,0},{32,48},{48,32},{64,80},{80,64},{96,112},{112,96},{1... | collective-permute-start | bytes 25165832 | tf_op jit(solution)/shard_map/ppermute | solution.py:242
  67.1 134.4 %collective-permute-start.1 = (bf16[1024,4096]{1,0:T(8,128)(2,1)}, bf16[1024,4096]{1,0:T(8,128)(2,1)}, u32[]{:S(2)}, u32[]{:S(2)}) collective-permute-start(bf16[1024,4096]{1,0:T(8,128)(2,1)} %bitcast.37), channel_id=1, source_target_pairs={{0,16},{16,0},{32,48},{48,32},{64,80},{80,64},{96,112},{112,96},{1... | collective-permute-start | bytes 25165832 | tf_op jit(solution)/shard_map/ppermute | solution.py:243
  166.0 46.5 %all-to-all-start.2 = ((bf16[16,384,256]{2,1,0:T(8,128)(2,1)}), bf16[16,384,256]{2,1,0:T(8,128)(2,1)S(1)}, u32[]{:S(2)}, u32[]{:S(2)}) async-start(bf16[16,384,256]{2,1,0:T(8,128)(2,1)} %bitcast.35), calls=%async_computation.3 | async-start | bytes 6291456 | tf_op jit(solution)/shard_map/all_to_all | solution.py:230
  169.8 142.2 %reduce-scatter.5.cloned.1.call-start = ((), (), s32[]{:S(2)}) async-start(), calls=%async_computation.8 | async-start | bytes 9437184 | tf_op jit(solution)/shard_map/reduce_scatter | solution.py:277
  212.5 1.7 copy-start.2
  243.7 148.6 %reduce-scatter.3.cloned.1.call-start = ((), (), s32[]{:S(2)}) async-start(), calls=%async_computation.6 | async-start | bytes 4718592 | tf_op jit(solution)/shard_map/reduce_scatter | solution.py:282
  312.0 4.5 %copy-start.4 = (f32[384,1]{1,0:T(8,128)S(1)}, f32[384,1]{1,0:T(8,128)}, u32[]{:S(2)}) copy-start(f32[384,1]{1,0:T(8,128)} %get-tuple-element.16) | copy-start | bytes 4612
  312.0 80.4 %copy-start.1 = (f32[1024,16]{0,1:T(8,128)S(1)}, f32[1024,16]{0,1:T(8,128)}, u32[]{:S(2)}) copy-start(f32[1024,16]{0,1:T(8,128)} %param.8) | copy-start | bytes 196612
  312.0 76.9 %all-to-all-start.3 = ((bf16[16,128,256]{2,1,0:T(8,128)(2,1)}), bf16[16,128,256]{2,1,0:T(8,128)(2,1)S(1)}, u32[]{:S(2)}, u32[]{:S(2)}) async-start(bf16[16,128,256]{2,1,0:T(8,128)(2,1)} %bitcast.41), calls=%async_computation.5 | async-start | bytes 2097152 | tf_op jit(solution)/shard_map/all_to_all | solution.py:230
  388.9 1.0 copy-start.3
Sparse Core Ops, SparseCore 0:
  9.7 34.7 all-gather.3
  67.1 49.1 all-gather.5
  243.8 58.6 reduce-scatter.4
  312.1 38.1 reduce-scatter.2

commit v2 on v1

v2 whole, which is shorter than its diff:
```python
import functools

import jax
import jax.numpy as jnp
from jax import lax
from jax.experimental import pallas as pl
from jax.experimental.pallas import tpu as pltpu
from jax.sharding import PartitionSpec as P

D = 4096
BLK = 128
WIDTH = 256
SLICES = D // WIDTH
CAP = 6
OWN = CAP // 2
ROWS = OWN * BLK
UNITS = 1024
GELU_C = 0.7978845608028654
GELU_K = 0.044715
MIB = 1024 * 1024
PICK_MIB, HID_MIB, BACK_MIB, OUT_MIB, MERGE_MIB = 60, 60, 60, 60, 60
ANY = pl.BlockSpec(memory_space=pl.ANY)
SMEM = pl.BlockSpec(memory_space=pltpu.SMEM)
VMEM = pl.BlockSpec(memory_space=pltpu.VMEM)


def params(mib):
    return pltpu.CompilerParams(vmem_limit_bytes=mib * MIB)


def cost(flops, nbytes):
    return pl.CostEstimate(flops=flops, bytes_accessed=nbytes, transcendentals=0)


def pick_body(count, ids, src, out, sems):
    copies = [
        pltpu.make_async_copy(src.at[ids[i]], out.at[i], sems.at[i]) for i in range(count)
    ]
    for copy in copies:
        copy.start()
    for copy in copies:
        copy.wait()


def pick_blocks(src, ids):
    count = ids.shape[0]
    return pl.pallas_call(
        functools.partial(pick_body, count),
        out_shape=jax.ShapeDtypeStruct((count, BLK, WIDTH), src.dtype),
        in_specs=[SMEM, ANY],
        out_specs=VMEM,
        scratch_shapes=[pltpu.SemaphoreType.DMA((count,))],
        compiler_params=params(PICK_MIB),
        cost_estimate=cost(0, 2 * count * BLK * WIDTH * 2),
        name="pick_blocks",
    )(ids, src)


def hidden_body(tiles, x_all, wa, wb, act_a, act_b, der_a, der_b, x_raw, x_v, sems):
    @pl.when(pl.program_id(0) == 0)
    def _():
        copies = [
            pltpu.make_async_copy(x_all.at[tiles[s]], x_raw.at[s], sems.at[s]) for s in range(OWN)
        ]
        for copy in copies:
            copy.start()
        for s in range(OWN):
            copies[s].wait()
            for f in range(SLICES):
                x_v[s * BLK : (s + 1) * BLK, f * WIDTH : (f + 1) * WIDTH] = x_raw[s, f]

    for w, act, der in ((wa, act_a, der_a), (wb, act_b, der_b)):
        h = jnp.dot(x_v[...], w[...], preferred_element_type=jnp.float32)
        sq = h * h
        t = jnp.tanh(h * (GELU_C + (GELU_C * GELU_K) * sq))
        half = 0.5 + 0.5 * t
        act[...] = (h * half).astype(act.dtype)
        slope = 0.5 * GELU_C + (1.5 * GELU_C * GELU_K) * sq
        der[...] = half + (h * slope) * (1.0 - t * t)


def hidden(tiles, x_all, w_in, w_in_other):
    cols = 256
    w_spec = pl.BlockSpec((D, cols), lambda i: (0, i))
    o_spec = pl.BlockSpec((ROWS, cols), lambda i: (0, i))
    act = jax.ShapeDtypeStruct((ROWS, UNITS), jnp.bfloat16)
    der = jax.ShapeDtypeStruct((ROWS, UNITS), jnp.float32)
    return pl.pallas_call(
        hidden_body,
        grid=(UNITS // cols,),
        out_shape=(act, act, der, der),
        in_specs=[SMEM, ANY, w_spec, w_spec],
        out_specs=(o_spec, o_spec, o_spec, o_spec),
        scratch_shapes=[
            pltpu.VMEM((OWN, SLICES, BLK, WIDTH), jnp.bfloat16),
            pltpu.VMEM((ROWS, D), jnp.bfloat16),
            pltpu.SemaphoreType.DMA((OWN,)),
        ],
        compiler_params=params(HID_MIB),
        cost_estimate=cost(2 * ROWS * D * 2 * UNITS, 24 * MIB),
        name="hidden",
    )(tiles, x_all, w_in, w_in_other)


def back_body(
    first, tiles, dy, oa, ob, ia, ib, act_a, act_b, der_a, der_b, gate, out, dgate, g_v, dh_a, dh_b
):
    step = pl.program_id(0)
    dims = (((1,), (1,)), ((), ()))

    @pl.when(step == 0)
    def _():
        scale = gate[...]
        for f in range(SLICES):
            g = scale * dy[f].astype(jnp.float32)
            g_v[:, f * WIDTH : (f + 1) * WIDTH] = g.astype(g_v.dtype)
        dgate[...] = jnp.zeros_like(dgate)

    @pl.when(step < first)
    def _():
        total = dgate[...]
        cols = oa.shape[0]
        here = pl.ds(pl.multiple_of(step * cols, cols), cols)
        for w, act, der, dh in ((oa, act_a, der_a, dh_a), (ob, act_b, der_b, dh_b)):
            u = lax.dot_general(g_v[...], w[...], dims, preferred_element_type=jnp.float32)
            dh[:, here] = (u * der[...]).astype(dh.dtype)
            total += jnp.sum(act[...].astype(jnp.float32) * u, axis=1, keepdims=True)
        dgate[...] = jnp.where(step == first - 1, total / gate[...], total)

    @pl.when(step >= first)
    def _():
        r = lax.dot_general(dh_a[...], ia[...], dims, preferred_element_type=jnp.float32)
        r += lax.dot_general(dh_b[...], ib[...], dims, preferred_element_type=jnp.float32)
        r = r.astype(out.dtype)
        out[...] = jnp.zeros_like(out)
        for s in range(OWN):
            for f in range(out.shape[1]):
                out[tiles[s], f] = r[s * BLK : (s + 1) * BLK, f * WIDTH : (f + 1) * WIDTH]


def back(tiles, dy, w_out, w_out_other, w_in, w_in_other, acts, ders, gate, tile_count):
    cols, per = 256, 4
    first, second = UNITS // cols, SLICES // per
    early = lambda i: jnp.minimum(i, first - 1)
    late = lambda i: jnp.maximum(i - first, 0)
    wo_spec = pl.BlockSpec((cols, D), lambda i: (early(i), 0))
    wi_spec = pl.BlockSpec((per * WIDTH, UNITS), lambda i: (late(i), 0))
    h_spec = pl.BlockSpec((ROWS, cols), lambda i: (0, early(i)))
    g_spec = pl.BlockSpec((ROWS, 1), lambda i: (0, 0))
    dy_spec = pl.BlockSpec((SLICES, ROWS, WIDTH), lambda i: (0, 0, 0))
    return pl.pallas_call(
        functools.partial(back_body, first),
        grid=(first + second,),
        out_shape=(
            jax.ShapeDtypeStruct((tile_count, SLICES, BLK, WIDTH), jnp.bfloat16),
            jax.ShapeDtypeStruct((ROWS, 1), jnp.float32),
        ),
        in_specs=[SMEM, dy_spec, wo_spec, wo_spec, wi_spec, wi_spec]
        + [h_spec] * 4
        + [g_spec],
        out_specs=(
            pl.BlockSpec((tile_count, per, BLK, WIDTH), lambda i: (0, late(i), 0, 0)),
            g_spec,
        ),
        scratch_shapes=[
            pltpu.VMEM((ROWS, D), jnp.bfloat16),
            pltpu.VMEM((ROWS, UNITS), jnp.bfloat16),
            pltpu.VMEM((ROWS, UNITS), jnp.bfloat16),
        ],
        compiler_params=params(BACK_MIB),
        cost_estimate=cost(4 * ROWS * D * 2 * UNITS, 50 * MIB),
        name="back",
    )(tiles, dy, w_out, w_out_other, w_in, w_in_other, *acts, *ders, gate)


def rows_out_body(act_a, act_b, wa, wb, gate, out):
    o = jnp.dot(act_a[...], wa[...], preferred_element_type=jnp.float32)
    o += jnp.dot(act_b[...], wb[...], preferred_element_type=jnp.float32)
    o = (o * gate[...]).astype(out.dtype)
    for f in range(out.shape[0]):
        out[f] = o[:, f * WIDTH : (f + 1) * WIDTH]


def rows_out(acts, w_out, w_out_other, gate):
    per = 4
    a_spec = pl.BlockSpec((ROWS, UNITS), lambda i: (0, 0))
    w_spec = pl.BlockSpec((UNITS, per * WIDTH), lambda i: (0, i))
    return pl.pallas_call(
        rows_out_body,
        grid=(SLICES // per,),
        out_shape=jax.ShapeDtypeStruct((SLICES, ROWS, WIDTH), jnp.bfloat16),
        in_specs=[a_spec, a_spec, w_spec, w_spec, pl.BlockSpec((ROWS, 1), lambda i: (0, 0))],
        out_specs=pl.BlockSpec((per, ROWS, WIDTH), lambda i: (i, 0, 0)),
        compiler_params=params(OUT_MIB),
        cost_estimate=cost(2 * ROWS * D * 2 * UNITS, 21 * MIB),
        name="rows_out",
    )(*acts, w_out, w_out_other, gate)


def merge_body(count, ids, parts, out, total):
    total[...] = jnp.zeros_like(total)

    def step(i, carry):
        total[ids[i]] += parts[i].astype(jnp.float32)
        return carry

    lax.fori_loop(0, count, step, 0)
    out[...] = total[: out.shape[0]].astype(out.dtype)


def merge(parts, ids, blocks):
    count = parts.shape[0]
    return pl.pallas_call(
        functools.partial(merge_body, count),
        out_shape=jax.ShapeDtypeStruct((blocks, BLK, WIDTH), jnp.bfloat16),
        in_specs=[SMEM, VMEM],
        out_specs=VMEM,
        scratch_shapes=[pltpu.VMEM((blocks + 1, BLK, WIDTH), jnp.float32)],
        compiler_params=params(MERGE_MIB),
        cost_estimate=cost(0, (count + blocks) * BLK * WIDTH * 2 * 2),
        name="merge",
    )(ids, parts)


def exchange(value):
    return lax.all_to_all(value, "exp", split_axis=0, concat_axis=0, tiled=True)


def along_z(value, hops, chips):
    pairs = [
        (2 * ((z + hops) % chips) + core, 2 * z + core) for z in range(chips) for core in range(2)
    ]
    return lax.ppermute(value, "tok", pairs)


def other_core(value, chips):
    return lax.ppermute(value, "tok", [(i, i ^ 1) for i in range(2 * chips)])


def on_device(tokens, cotangent, gates, picks, w_in, w_out):
    tile_count = lax.axis_size("tok")
    chips = tile_count // 2
    my_tile = lax.axis_index("tok")
    my_expert = lax.axis_index("exp")
    core = my_tile % 2
    blocks = tokens.shape[0] // BLK
    experts = gates.shape[1]
    w_in, w_out = w_in[0], w_out[0]

    cot_all = lax.all_gather(cotangent.reshape(blocks, BLK, WIDTH), "tok", tiled=True)
    tile_picks = lax.dynamic_index_in_dim(picks, my_tile, 0, False)
    x_slot = pick_blocks(tokens.reshape(blocks, BLK, WIDTH), jnp.minimum(tile_picks, blocks - 1))
    x_all = lax.all_gather(exchange(x_slot), "tok")

    chosen = picks < blocks
    order = jnp.arange(tile_count, dtype=jnp.int32)
    before = (order[None, :] < order[:, None])[:, :, None] & chosen[None]
    rank = jnp.sum(before.astype(jnp.int32), axis=1)
    slot = jnp.arange(CAP, dtype=jnp.int32)
    at_slot = chosen[:, :, None] & (rank[:, :, None] == slot)
    slot_tile = jnp.sum(jnp.where(at_slot, order[:, None, None], 0), axis=0)
    slot_block = jnp.sum(jnp.where(at_slot, picks[:, :, None], 0), axis=0)
    slot_place = (slot_tile // 2 - my_tile // 2) % chips + chips * ((slot_tile + core) % 2)

    def own_of(values):
        return lax.dynamic_slice_in_dim(values, core * OWN, OWN, 1)

    own_rows = own_of(slot_tile * blocks + slot_block)
    own_places = own_of(slot_place * blocks + slot_block)
    own_tiles = lax.dynamic_index_in_dim(own_of(slot_tile), my_expert, 0, False)
    my_places = lax.dynamic_index_in_dim(own_places, my_expert, 0, False)

    gate_mine = lax.dynamic_index_in_dim(gates, my_expert, 1, False).reshape(blocks, BLK)
    gate_near = jnp.concatenate([gate_mine] + [along_z(gate_mine, k, chips) for k in (1, 2, 3)])
    gate_all = jnp.concatenate([gate_near, other_core(gate_near, chips)])
    gate = jnp.take(gate_all, my_places, axis=0, mode="clip").reshape(ROWS, 1)

    dy = exchange(pick_blocks(cot_all, own_rows.reshape(-1)).reshape(experts, ROWS, WIDTH))
    w_in_other = other_core(w_in, chips)
    w_out_other = other_core(w_out, chips)

    act_a, act_b, der_a, der_b = hidden(own_tiles, x_all, w_in, w_in_other)
    dx_all, dgate = back(
        own_tiles, dy, w_out, w_out_other, w_in, w_in_other,
        (act_a, act_b), (der_a, der_b), gate, tile_count,
    )
    out_rows = rows_out((act_a, act_b), w_out, w_out_other, gate)

    dx = lax.psum_scatter(dx_all, "tok", scatter_dimension=0)

    parts = exchange(out_rows).reshape(experts * OWN, BLK, WIDTH)
    mixed_all = merge(parts, own_rows.reshape(-1), tile_count * blocks)
    mixed = lax.psum_scatter(
        mixed_all.reshape(tile_count, blocks * BLK, WIDTH), "tok", scatter_dimension=0
    )
    dx = exchange(dx)
    d_tokens = merge(dx, tile_picks, blocks)

    dgate = dgate.reshape(OWN, BLK)
    dgate += sum(along_z(dgate, k, chips) for k in (1, 2, 3))
    theirs = other_core(dgate, chips)
    low = jnp.where(core == 0, dgate, theirs)
    high = jnp.where(core == 0, theirs, dgate)
    both = jnp.concatenate([low, high])
    both, _ = lax.optimization_barrier((both, dx))
    grads = exchange(jnp.broadcast_to(both[None], (experts, CAP, BLK)))
    taken = lax.dynamic_index_in_dim(chosen, my_tile, 0, False)
    here = (slot_tile == my_tile) & taken[:, None]
    mine = jnp.sum(jnp.where(here[:, :, None], grads, 0.0), axis=1)
    at_block = tile_picks[None, :] == jnp.arange(blocks, dtype=jnp.int32)[:, None]
    d_gates = jnp.where(at_block[:, None, :], mine.T[None], 0.0)
    return (
        mixed,
        d_tokens.reshape(blocks * BLK, WIDTH),
        d_gates.reshape(blocks * BLK, experts),
    )


def solution(mesh):
    return jax.shard_map(
        on_device,
        mesh=mesh,
        in_specs=(
            P("tok", "exp"),
            P("tok", "exp"),
            P("tok", None),
            P(),
            P("exp", None, "tok"),
            P("exp", "tok", None),
        ),
        out_specs=(P("tok", "exp"), P("tok", "exp"), P("tok", None)),
        check_vma=False,
    )
```

time: 401 us -> 251 us (0.63)
  Pallas kernels: 197 us -> 67.6 us
  blocking collectives: 159 us -> 70.9 us
  waiting for transfers between devices: 11.7 us -> 67.2 us
  starting transfers between devices: 8.77 us -> 22.6 us
    pallas_call x2, Pallas kernels: 131 us -> 7.88 us  [pick_blocks(): pl.pallas_call(functools.partial(pick_body, count), out_shape=jax.ShapeDt...]
    psum x1 -> x0, blocking collectives: 71.3 us -> none  [on_device(): grads = lax.psum(spread, ('tok', 'exp'))]
    all_gather x1, waiting for transfers between devices: 0.01 us -> 30.5 us  [on_device(): x_all = lax.all_gather(exchange(x_slot), 'tok')]
    all_gather x1 -> x0, blocking collectives: 14 us -> none  [on_device(): gate_all = lax.all_gather(gate_mine, 'tok', tiled=True)]
    all_gather x1, waiting for transfers between devices: 0.01 us -> 13.7 us  [on_device(): lax.all_gather(cotangent.reshape(blocks, BLK, WIDTH), 'tok', tiled=True)]
    ppermute x2 -> x10, starting transfers between devices: 0.58 us -> 10.7 us  [the longest x6 10.1 us: along_z(): return lax.ppermute(value, 'tok', pairs)]
    ppermute x2 -> x10, waiting for transfers between devices: 0.01 us -> 5.65 us  [the longest x6 3.36 us: along_z(): return lax.ppermute(value, 'tok', pairs)]
    pallas_call x2 -> x1, Pallas kernels: 29.5 us -> 25.2 us  [back(): pl.pallas_call(functools.partial(back_body, first), grid=(first + second,...]
  transfers between devices with their start and end apart: 8 -> 17, of which waited for: 1 -> 11; matrix products, arithmetic and copies ran while one was open for 1% -> 2% of each run, Pallas kernels for 42% -> 17%
where the time goes in v2:
time: 251 us; the launch traced here: 250 us
  blocking collectives  70.9 us (28%)
  Pallas kernels  67.6 us (27%)
  waiting for transfers between devices  67.2 us (27%)
  starting transfers between devices  22.6 us (9%)
  between operations  14 us (6%)
  local copies, waits for them, and re-layouts  6.08 us (2%)
    all_to_all x2, blocking collectives, exchange(): return lax.all_to_all(value, 'exp', split_axis=0, concat_axis=0, tiled=True)  70.9 us
    all_gather x1, waiting for transfers between devices, on_device(): x_all = lax.all_gather(exchange(x_slot), 'tok')  30.5 us
    pallas_call x1, Pallas kernels, back(): pl.pallas_call(functools.partial(back_body, first), grid=(first + second,...  25.2 us
    pallas_call x1, Pallas kernels, hidden(): pl.pallas_call(hidden_body, grid=(UNITS // cols,), out_shape=(act, act, d...  14.9 us
    all_to_all x3, waiting for transfers between devices, exchange(): return lax.all_to_all(value, 'exp', split_axis=0, concat_axis=0, tiled=True)  14 us
    all_gather x1, waiting for transfers between devices, on_device(): lax.all_gather(cotangent.reshape(blocks, BLK, WIDTH), 'tok', tiled=True)  13.7 us
    all_to_all x3, starting transfers between devices, exchange(): return lax.all_to_all(value, 'exp', split_axis=0, concat_axis=0, tiled=True)  11.7 us
    pallas_call x1, Pallas kernels, rows_out(): pl.pallas_call(rows_out_body, grid=(SLICES // per,), out_shape=jax.ShapeD...  11.7 us
  transfers between devices with their start and end apart: 17, of which 11 were waited for; matrix products, arithmetic and copies ran while one was open for 2% of the time, Pallas kernels for 17%

profile of v2, /device:TPU:0, one launch (start us, length us, event | category | flops | bytes accessed | tf_op | source)
XLA Modules:
  0.0 250.1 jit_solution(2930536379940586681)
XLA Ops:
  7.2 0.7 all-gather.4.cloned.1.call-update
  8.0 1.2 broadcast_minimum_fusion
  9.2 3.2 %pick_blocks.2 = bf16[16,128,256]{2,1,0:T(8,128)(2,1)} custom-call(s32[16]{0:T(128)} %get-tuple-element.19.ids, bf16[8,128,256]{2,1,0:T(8,128)(2,1)} %bitcast.40), custom_call_target="tpu_custom_call" | custom-call | bytes 2097152 | tf_op jit(solution)/shard_map/pick_blocks/pallas_call | solution.py:47
  12.4 24.0 %all_to_all.25 = bf16[16,128,256]{2,1,0:T(8,128)(2,1)} all-to-all(bf16[16,128,256]{2,1,0:T(8,128)(2,1)} %pick_blocks.2), channel_id=1, replica_groups=mesh['tok'=8,'exp'=16] {'exp'}, dimensions={0} | all-to-all | bytes 2097152 | tf_op jit(solution)/shard_map/all_to_all | solution.py:226
  37.9 13.7 %all-gather.4.cloned.1.call-done.src = bf16[64,128,256]{2,1,0:T(8,128)(2,1)} async-done(((bf16[8,128,256]{2,1,0:T(8,128)(2,1)}), bf16[64,128,256]{2,1,0:T(8,128)(2,1)}) %all-gather.4.cloned.1.call-update) | async-done | bytes 4194320 | tf_op jit(solution)/shard_map/all_gather | solution.py:250
  51.6 4.7 %pick_blocks.3 = bf16[48,128,256]{2,1,0:T(8,128)(2,1)} custom-call(s32[48]{0:T(128)} %reshape.103.ids, bf16[64,128,256]{2,1,0:T(8,128)(2,1)} %all-gather.4.cloned.1.call-done.src), custom_call_target="tpu_custom_call" | custom-call | bytes 6291456 | tf_op jit(solution)/shard_map/pick_blocks/pallas_call | solution.py:47
  56.3 4.4 %all-to-all-start.2 = ((bf16[16,384,256]{2,1,0:T(8,128)(2,1)}), bf16[16,384,256]{2,1,0:T(8,128)(2,1)S(1)}, u32[]{:S(2)}, u32[]{:S(2)}) async-start(bf16[16,384,256]{2,1,0:T(8,128)(2,1)} %bitcast.33), calls=%async_computation.3 | async-start | bytes 6291456 | tf_op jit(solution)/shard_map/all_to_all | solution.py:226
  60.8 1.2 collective-permute-start.4
  62.0 3.6 %collective-permute-start.3 = (f32[8,128]{1,0:T(8,128)S(1)}, f32[8,128]{1,0:T(8,128)S(1)}, u32[]{:S(2)}, u32[]{:S(2)}) collective-permute-start(f32[8,128]{1,0:T(8,128)S(1)} %bitcast.48), channel_id=1, source_target_pairs={{64,0},{80,16},{96,32},{112,48},{0,64},{16,80},{32,96},{48,112},{6... | collective-permute-start | bytes 12296 | tf_op jit(solution)/shard_map/ppermute | solution.py:233
  65.6 0.7 collective-permute-start.2
  66.5 0.7 dynamic-slice_reduce_fusion.1.tiles
  67.3 1.9 collective-permute-done.2
  69.3 1.2 collective-permute-done.5
  71.0 0.8 copy.26
  71.9 30.5 %all-gather.6.cloned.1.call-done = bf16[128,128,256]{2,1,0:T(8,128)(2,1)} async-done(((bf16[16,128,256]{2,1,0:T(8,128)(2,1)}), bf16[128,128,256]{2,1,0:T(8,128)(2,1)}) %all-gather.6.cloned.1.call-update) | async-done | bytes 8388624 | tf_op jit(solution)/shard_map/all_gather | solution.py:253
  102.4 14.9 %hidden.1 = (bf16[384,1024]{1,0:T(8,128)(2,1)}, bf16[384,1024]{1,0:T(8,128)(2,1)}, f32[384,1024]{1,0:T(8,128)}, f32[384,1024]{1,0:T(8,128)}) custom-call(s32[3]{0:T(128)} %dynamic-slice_reduce_fusion.1.tiles, bf16[8,16,128,256]{3,2,1,0:T(8,128)(2,1)} %bitcast.38, bf16[4096,1024]{1,0:T(8,128)(2,1)} %bitcast.36, bf16[4096,1024]{1,0:T(8,128)(2,1)} %collective-permute-done.wb.ib), custom_call_target="tpu_custom_call" | custom-call | flops 6442450944 | bytes 25165824 | tf_op jit(solution)/shard_map/hidden/pallas_call | solution.py:88
  117.3 1.6 copy-done.3
  118.9 25.2 %back.1 = (bf16[8,16,128,256]{3,2,1,0:T(8,128)(2,1)}, f32[384,1]{1,0:T(8,128)}) custom-call(s32[3]{0:T(128)} %dynamic-slice_reduce_fusion.1.tiles, bf16[16,384,256]{2,1,0:T(8,128)(2,1)} %copy-done.3, bf16[1024,4096]{1,0:T(8,128)(2,1)} %bitcast.59, bf16[1024,4096]{1,0:T(8,128)(2,1)} %collective-permute-done.1.wb.ob, bf16[4096,1024]{1,0:T(8,128)(2,1)} %bitcast.37, ...), custom_call_target="tpu_custom_call" | custom-call | flops 12884901888 | bytes 52428800 | tf_op jit(solution)/shard_map/back/pallas_call | solution.py:151
  144.2 11.7 %rows_out.1 = bf16[16,384,256]{2,1,0:T(8,128)(2,1)} custom-call(bf16[384,1024]{1,0:T(8,128)(2,1)} %get-tuple-element.10.act_a, bf16[384,1024]{1,0:T(8,128)(2,1)} %get-tuple-element.11.act_b, bf16[1024,4096]{1,0:T(8,128)(2,1)} %bitcast.60, bf16[1024,4096]{1,0:T(8,128)(2,1)} %collective-permute-done.1.wb.ob, f32[384,1]{1,0:T(8,128)} %bitcast.45), custom_call_target="tpu_custom_call" | custom-call | flops 6442450944 | bytes 22020096 | tf_op jit(solution)/shard_map/rows_out/pallas_call | solution.py:188
  155.9 46.9 %all_to_all.26 = bf16[16,384,256]{2,1,0:T(8,128)(2,1)} all-to-all(bf16[16,384,256]{2,1,0:T(8,128)(2,1)} %rows_out.1), channel_id=1, replica_groups=mesh['tok'=8,'exp'=16] {'exp'}, dimensions={0} | all-to-all | bytes 6291456 | tf_op jit(solution)/shard_map/all_to_all | solution.py:226
  202.8 5.5 %merge.2 = bf16[64,128,256]{2,1,0:T(8,128)(2,1)} custom-call(s32[48]{0:T(128)} %reshape.103.ids, bf16[48,128,256]{2,1,0:T(8,128)(2,1)} %bitcast.34), custom_call_target="tpu_custom_call" | custom-call | bytes 14680064 | tf_op jit(solution)/shard_map/merge/pallas_call | solution.py:213
  208.3 3.8 %all-to-all-start.3 = ((bf16[16,128,256]{2,1,0:T(8,128)(2,1)}), bf16[16,128,256]{2,1,0:T(8,128)(2,1)S(1)}, u32[]{:S(2)}, u32[]{:S(2)}) async-start(bf16[16,128,256]{2,1,0:T(8,128)(2,1)} %bitcast.39), calls=%async_computation.5 | async-start | bytes 2097152 | tf_op jit(solution)/shard_map/all_to_all | solution.py:226
  212.3 0.7 collective-permute-start.8
  213.0 1.6 collective-permute-start.7
  214.6 2.2 collective-permute-start.6
  217.2 1.0 collective-permute-done.7
  218.3 1.1 collective-permute-done.9
  219.5 9.0 %all-to-all-done.3.parts = bf16[16,128,256]{2,1,0:T(8,128)(2,1)S(1)} async-done(((bf16[16,128,256]{2,1,0:T(8,128)(2,1)}), bf16[16,128,256]{2,1,0:T(8,128)(2,1)S(1)}, u32[]{:S(2)}, u32[]{:S(2)}) %all-to-all-start.3) | async-done | bytes 1048608 | tf_op jit(solution)/shard_map/all_to_all | solution.py:226
  229.1 3.5 %all-to-all-start.4 = ((f32[16,6,128]{2,1,0:T(8,128)}), f32[16,6,128]{2,1,0:T(8,128)S(1)}, u32[]{:S(2)}, u32[]{:S(2)}) async-start(f32[16,6,128]{2,1,0:T(8,128)} %broadcast_in_dim.85), calls=%async_computation.6 | async-start | bytes 131072 | tf_op jit(solution)/shard_map/all_to_all | solution.py:226
  232.8 2.4 merge.3
  235.2 5.0 %all-to-all-done.4 = f32[16,6,128]{2,1,0:T(8,128)S(1)} async-done(((f32[16,6,128]{2,1,0:T(8,128)}), f32[16,6,128]{2,1,0:T(8,128)S(1)}, u32[]{:S(2)}, u32[]{:S(2)}) %all-to-all-start.4) | async-done | bytes 49184 | tf_op jit(solution)/shard_map/all_to_all | solution.py:226
  241.1 2.5 %reduce-scatter.3.cloned.1.call-done = bf16[1,1024,256]{2,1,0:T(8,128)(2,1)} async-done(((bf16[8,1024,256]{2,1,0:T(8,128)(2,1)}), bf16[1,1024,256]{2,1,0:T(8,128)(2,1)}) %reduce-scatter.3.cloned.1.call-update) | async-done | bytes 524304 | tf_op jit(solution)/shard_map/reduce_scatter | solution.py:293
  (63 shorter events, 4.8 us)
Async XLA Ops:
  7.2 53.6 %copy-start = (f32[1024,16]{0,1:T(8,128)S(1)}, f32[1024,16]{0,1:T(8,128)}, u32[]{:S(2)}) copy-start(f32[1024,16]{0,1:T(8,128)} %param.8) | copy-start | bytes 196612
  7.2 29.8 %copy-start.5 = (s32[8,16]{1,0:T(8,128)S(1)}, s32[8,16]{1,0:T(8,128)}, u32[]{:S(2)}) copy-start(s32[8,16]{1,0:T(8,128)} %param.9) | copy-start | bytes 1540
  7.2 44.4 %all-gather.4.cloned.1.call-start = ((), (), s32[]{:S(2)}) async-start(), calls=%async_computation.8 | async-start | bytes 4718592 | tf_op jit(solution)/shard_map/all_gather | solution.py:250
  7.9 94.4 %all-gather.6.cloned.1.call-start = ((), (), s32[]{:S(2)}) async-start(), calls=%async_computation.10 | async-start | bytes 9437184 | tf_op jit(solution)/shard_map/all_gather | solution.py:253
  9.2 223.4 %copy-start.6 = (s32[16]{0:T(128)}, s32[16]{0:T(128)S(1)}, u32[]{:S(2)}) copy-start(s32[16]{0:T(128)S(1)} %get-tuple-element.20.ids) | copy-start | bytes 196
  36.4 35.4 %collective-permute-start = (bf16[4096,1024]{1,0:T(8,128)(2,1)}, bf16[4096,1024]{1,0:T(8,128)(2,1)}, u32[]{:S(2)}, u32[]{:S(2)}) collective-permute-start(bf16[4096,1024]{1,0:T(8,128)(2,1)} %bitcast.35), channel_id=1, source_target_pairs={{0,16},{16,0},{32,48},{48,32},{64,80},{80,64},{96,112},{112,96},{1... | collective-permute-start | bytes 25165832 | tf_op jit(solution)/shard_map/ppermute | solution.py:237
  36.5 80.7 %collective-permute-start.1 = (bf16[1024,4096]{1,0:T(8,128)(2,1)}, bf16[1024,4096]{1,0:T(8,128)(2,1)}, u32[]{:S(2)}, u32[]{:S(2)}) collective-permute-start(bf16[1024,4096]{1,0:T(8,128)(2,1)} %bitcast.58), channel_id=1, source_target_pairs={{0,16},{16,0},{32,48},{48,32},{64,80},{80,64},{96,112},{112,96},{1... | collective-permute-start | bytes 25165832 | tf_op jit(solution)/shard_map/ppermute | solution.py:237
  56.3 61.0 %all-to-all-start.2 = ((bf16[16,384,256]{2,1,0:T(8,128)(2,1)}), bf16[16,384,256]{2,1,0:T(8,128)(2,1)S(1)}, u32[]{:S(2)}, u32[]{:S(2)}) async-start(bf16[16,384,256]{2,1,0:T(8,128)(2,1)} %bitcast.33), calls=%async_computation.3 | async-start | bytes 6291456 | tf_op jit(solution)/shard_map/all_to_all | solution.py:226
  60.7 147.6 %reduce-scatter.5.cloned.1.call-start = ((), (), s32[]{:S(2)}) async-start(), calls=%async_computation.9 | async-start | bytes 9437184 | tf_op jit(solution)/shard_map/reduce_scatter | solution.py:289
  60.8 6.4 %collective-permute-start.4 = (f32[8,128]{1,0:T(8,128)S(1)}, f32[8,128]{1,0:T(8,128)S(1)}, u32[]{:S(2)}, u32[]{:S(2)}) collective-permute-start(f32[8,128]{1,0:T(8,128)S(1)} %bitcast.47), channel_id=1, source_target_pairs={{96,0},{112,16},{0,32},{16,48},{32,64},{48,80},{64,96},{80,112},{9... | collective-permute-start | bytes 12296 | tf_op jit(solution)/shard_map/ppermute | solution.py:233
  62.0 5.3 %collective-permute-start.3 = (f32[8,128]{1,0:T(8,128)S(1)}, f32[8,128]{1,0:T(8,128)S(1)}, u32[]{:S(2)}, u32[]{:S(2)}) collective-permute-start(f32[8,128]{1,0:T(8,128)S(1)} %bitcast.48), channel_id=1, source_target_pairs={{64,0},{80,16},{96,32},{112,48},{0,64},{16,80},{32,96},{48,112},{6... | collective-permute-start | bytes 12296 | tf_op jit(solution)/shard_map/ppermute | solution.py:233
  65.6 3.7 %collective-permute-start.2 = (f32[8,128]{1,0:T(8,128)S(1)}, f32[8,128]{1,0:T(8,128)S(1)}, u32[]{:S(2)}, u32[]{:S(2)}) collective-permute-start(f32[8,128]{1,0:T(8,128)S(1)} %bitcast.49), channel_id=1, source_target_pairs={{32,0},{48,16},{64,32},{80,48},{96,64},{112,80},{0,96},{16,112},{3... | collective-permute-start | bytes 12296 | tf_op jit(solution)/shard_map/ppermute | solution.py:233
  69.3 1.2 collective-permute-start.5
  117.3 1.6 copy-start.3
  144.2 99.4 %reduce-scatter.3.cloned.1.call-start = ((), (), s32[]{:S(2)}) async-start(), calls=%async_computation.7 | async-start | bytes 4718592 | tf_op jit(solution)/shard_map/reduce_scatter | solution.py:293
  208.3 3.9 %copy-start.4 = (f32[384,1]{1,0:T(8,128)S(1)}, f32[384,1]{1,0:T(8,128)}, u32[]{:S(2)}) copy-start(f32[384,1]{1,0:T(8,128)} %get-tuple-element.15) | copy-start | bytes 4612
  208.3 35.3 %copy-start.1 = (f32[1024,16]{0,1:T(8,128)S(1)}, f32[1024,16]{0,1:T(8,128)}, u32[]{:S(2)}) copy-start(f32[1024,16]{0,1:T(8,128)} %param.8) | copy-start | bytes 196612
  208.3 20.1 %all-to-all-start.3 = ((bf16[16,128,256]{2,1,0:T(8,128)(2,1)}), bf16[16,128,256]{2,1,0:T(8,128)(2,1)S(1)}, u32[]{:S(2)}, u32[]{:S(2)}) async-start(bf16[16,128,256]{2,1,0:T(8,128)(2,1)} %bitcast.39), calls=%async_computation.5 | async-start | bytes 2097152 | tf_op jit(solution)/shard_map/all_to_all | solution.py:226
  212.3 4.9 %collective-permute-start.8 = (f32[3,128]{1,0:T(4,128)S(1)}, f32[3,128]{1,0:T(4,128)S(1)}, u32[]{:S(2)}, u32[]{:S(2)}) collective-permute-start(f32[3,128]{1,0:T(4,128)S(1)} %bitcast.53), channel_id=1, source_target_pairs={{96,0},{112,16},{0,32},{16,48},{32,64},{48,80},{64,96},{80,112},{9... | collective-permute-start | bytes 4616 | tf_op jit(solution)/shard_map/ppermute | solution.py:233
  213.0 5.2 %collective-permute-start.7 = (f32[3,128]{1,0:T(4,128)S(1)}, f32[3,128]{1,0:T(4,128)S(1)}, u32[]{:S(2)}, u32[]{:S(2)}) collective-permute-start(f32[3,128]{1,0:T(4,128)S(1)} %bitcast.54), channel_id=1, source_target_pairs={{64,0},{80,16},{96,32},{112,48},{0,64},{16,80},{32,96},{48,112},{6... | collective-permute-start | bytes 4616 | tf_op jit(solution)/shard_map/ppermute | solution.py:233
  214.6 3.6 %collective-permute-start.6 = (f32[3,128]{1,0:T(4,128)S(1)}, f32[3,128]{1,0:T(4,128)S(1)}, u32[]{:S(2)}, u32[]{:S(2)}) collective-permute-start(f32[3,128]{1,0:T(4,128)S(1)} %bitcast.55), channel_id=1, source_target_pairs={{32,0},{48,16},{64,32},{80,48},{96,64},{112,80},{0,96},{16,112},{3... | collective-permute-start | bytes 4616 | tf_op jit(solution)/shard_map/ppermute | solution.py:233
  218.2 1.2 collective-permute-start.9
  228.4 4.4 %copy-start.2 = (bf16[16,128,256]{2,1,0:T(8,128)(2,1)}, bf16[16,128,256]{2,1,0:T(8,128)(2,1)S(1)}, u32[]{:S(2)}) copy-start(bf16[16,128,256]{2,1,0:T(8,128)(2,1)S(1)} %all-to-all-done.3.parts) | copy-start | bytes 3145732
  229.1 11.1 %all-to-all-start.4 = ((f32[16,6,128]{2,1,0:T(8,128)}), f32[16,6,128]{2,1,0:T(8,128)S(1)}, u32[]{:S(2)}, u32[]{:S(2)}) async-start(f32[16,6,128]{2,1,0:T(8,128)} %broadcast_in_dim.85), calls=%async_computation.6 | async-start | bytes 131072 | tf_op jit(solution)/shard_map/all_to_all | solution.py:226
Sparse Core Ops, SparseCore 0:
  9.7 41.8 all-gather.3
  53.3 48.9 all-gather.5
  144.3 52.6 reduce-scatter.4
  208.4 35.1 reduce-scatter.2

commit v3 on v2

v3 whole, which is shorter than its diff:
```python
import functools

import jax
import jax.numpy as jnp
from jax import lax
from jax.experimental import pallas as pl
from jax.experimental.pallas import tpu as pltpu
from jax.sharding import PartitionSpec as P

D = 4096
BLK = 128
WIDTH = 256
SLICES = D // WIDTH
CAP = 6
OWN = CAP // 2
ROWS = OWN * BLK
UNITS = 1024
GELU_C = 0.7978845608028654
GELU_K = 0.044715
MIB = 1024 * 1024
HID_COST = 2
PICK_MIB, HID_MIB, BACK_MIB, OUT_MIB, MERGE_MIB = 60, 60, 60, 60, 60
ANY = pl.BlockSpec(memory_space=pl.ANY)
SMEM = pl.BlockSpec(memory_space=pltpu.SMEM)
VMEM = pl.BlockSpec(memory_space=pltpu.VMEM)


def params(mib):
    return pltpu.CompilerParams(vmem_limit_bytes=mib * MIB)


def cost(flops, nbytes):
    return pl.CostEstimate(flops=flops, bytes_accessed=nbytes, transcendentals=0)


def pick_body(count, ids, src, out, sems):
    copies = [
        pltpu.make_async_copy(src.at[ids[i]], out.at[i], sems.at[i]) for i in range(count)
    ]
    for copy in copies:
        copy.start()
    for copy in copies:
        copy.wait()


def pick_blocks(src, ids):
    count = ids.shape[0]
    return pl.pallas_call(
        functools.partial(pick_body, count),
        out_shape=jax.ShapeDtypeStruct((count, BLK, WIDTH), src.dtype),
        in_specs=[SMEM, ANY],
        out_specs=VMEM,
        scratch_shapes=[pltpu.SemaphoreType.DMA((count,))],
        compiler_params=params(PICK_MIB),
        cost_estimate=cost(0, 2 * count * BLK * WIDTH * 2),
        name="pick_blocks",
    )(ids, src)


def start(copies):
    for copy in copies:
        copy.start()


def wait(copies):
    for copy in copies:
        copy.wait()


GROUP = 512
HALF = GROUP // 2
CHIP_UNITS = 2 * UNITS
STEPS = CHIP_UNITS // GROUP
PART = SLICES // 2


def hidden_body(sources, picked, *refs):
    srcs = refs[:sources]
    wa, wb, act, der, x_raw, x_v, w_v, x_sems, w_sems = refs[sources:]
    step = pl.program_id(0)

    def weights(i):
        cols = pl.ds(pl.multiple_of(i * HALF, HALF), HALF)
        slot = i % 2
        return [
            pltpu.make_async_copy(
                w.at[:, cols], w_v.at[slot, :, pl.ds(k * HALF, HALF)], w_sems.at[slot, k]
            )
            for k, w in enumerate((wa, wb))
        ]

    @pl.when(step == 0)
    def _():
        for s in range(OWN):
            for side in range(2):
                own, above, below, far_a, far_b = srcs[5 * side : 5 * side + 5]
                for hops, source in ((0, own), (1, above), (3, below)):

                    @pl.when(picked[s] == 4 * side + hops)
                    def _(s=s, source=source):
                        pltpu.make_async_copy(source, x_raw.at[s], x_sems.at[s]).start()

                @pl.when(picked[s] == 4 * side + 2)
                def _(s=s, far_a=far_a, far_b=far_b):
                    for source, at in ((far_a, 0), (far_b, PART)):
                        to = x_raw.at[s, pl.ds(at, PART)]
                        pltpu.make_async_copy(source, to, x_sems.at[s]).start()

        start(weights(0))
        for s in range(OWN):
            pltpu.make_async_copy(srcs[0], x_raw.at[s], x_sems.at[s]).wait()
            for f in range(SLICES):
                x_v[s * BLK : (s + 1) * BLK, f * WIDTH : (f + 1) * WIDTH] = x_raw[s, f]

    @pl.when(step + 1 < STEPS)
    def _():
        start(weights(step + 1))

    wait(weights(step))
    h = jnp.dot(x_v[...], w_v[step % 2], preferred_element_type=jnp.float32)
    sq = h * h
    t = jnp.tanh(h * (GELU_C + (GELU_C * GELU_K) * sq))
    half = 0.5 + 0.5 * t
    act[...] = (h * half).astype(act.dtype)
    slope = 0.5 * GELU_C + (1.5 * GELU_C * GELU_K) * sq
    der[...] = half + (h * slope) * (1.0 - t * t)


def hidden(picked, srcs, w_in, w_in_other):
    o_spec = pl.BlockSpec((ROWS, GROUP), lambda i: (0, i))
    return pl.pallas_call(
        functools.partial(hidden_body, len(srcs)),
        grid=(STEPS,),
        out_shape=(
            jax.ShapeDtypeStruct((ROWS, CHIP_UNITS), jnp.bfloat16),
            jax.ShapeDtypeStruct((ROWS, CHIP_UNITS), jnp.float32),
        ),
        in_specs=[SMEM] + [ANY] * (len(srcs) + 2),
        out_specs=(o_spec, o_spec),
        scratch_shapes=[
            pltpu.VMEM((OWN, SLICES, BLK, WIDTH), jnp.bfloat16),
            pltpu.VMEM((ROWS, D), jnp.bfloat16),
            pltpu.VMEM((2, D, GROUP), jnp.bfloat16),
            pltpu.SemaphoreType.DMA((OWN,)),
            pltpu.SemaphoreType.DMA((2, 2)),
        ],
        compiler_params=params(HID_MIB),
        cost_estimate=cost(HID_COST * 2 * ROWS * D * 2 * UNITS, 24 * MIB),
        name="hidden",
    )(picked, *srcs, w_in, w_in_other)


def back_body(
    feats, tiles, dy, oa, ob, ia, ib, act, der, gate, out, dgate,
    dy_v, g_v, o_v, i_v, dh, dy_sem, o_sems, i_sems,
):
    step = pl.program_id(0)
    last = pl.num_programs(0) - 1
    dims = (((1,), (1,)), ((), ()))

    def out_weights(i):
        rows = pl.ds(pl.multiple_of(i * HALF, HALF), HALF)
        slot = i % 2
        return [
            pltpu.make_async_copy(
                w.at[rows, :], o_v.at[slot, pl.ds(k * HALF, HALF), :], o_sems.at[slot, k]
            )
            for k, w in enumerate((oa, ob))
        ]

    def in_weights(i):
        rows = pl.ds(pl.multiple_of(i * feats, feats), feats)
        slot = i % 2
        return [
            pltpu.make_async_copy(
                w.at[rows, pl.ds(j * HALF, HALF)],
                i_v.at[slot, :, pl.ds(j * GROUP + k * HALF, HALF)],
                i_sems.at[slot, k, j],
            )
            for k, w in enumerate((ia, ib))
            for j in range(STEPS)
        ]

    @pl.when(step == 0)
    def _():
        whole = pltpu.make_async_copy(dy, dy_v, dy_sem)
        whole.start()
        start(out_weights(0))
        whole.wait()
        scale = gate[...]
        for f in range(SLICES):
            g = scale * dy_v[f].astype(jnp.float32)
            g_v[:, f * WIDTH : (f + 1) * WIDTH] = g.astype(g_v.dtype)
        dgate[...] = jnp.zeros_like(dgate)

    @pl.when(step < STEPS)
    def _():
        @pl.when(step + 1 < STEPS)
        def _():
            start(out_weights(step + 1))

        @pl.when(step + 1 == STEPS)
        def _():
            start(in_weights(0))

        wait(out_weights(step))
        u = lax.dot_general(g_v[...], o_v[step % 2], dims, preferred_element_type=jnp.float32)
        here = pl.ds(pl.multiple_of(step * GROUP, GROUP), GROUP)
        dh[:, here] = (u * der[...]).astype(dh.dtype)
        total = dgate[...] + jnp.sum(act[...].astype(jnp.float32) * u, axis=1, keepdims=True)
        dgate[...] = jnp.where(step == STEPS - 1, total / gate[...], total)

    @pl.when(step >= STEPS)
    def _():
        i = step - STEPS

        @pl.when(step < last)
        def _():
            start(in_weights(i + 1))

        wait(in_weights(i))
        r = lax.dot_general(dh[...], i_v[i % 2], dims, preferred_element_type=jnp.float32)
        r = r.astype(out.dtype)
        out[...] = jnp.zeros_like(out)
        for s in range(OWN):
            for f in range(out.shape[1]):
                out[tiles[s], f] = r[s * BLK : (s + 1) * BLK, f * WIDTH : (f + 1) * WIDTH]


def back(tiles, dy, w_out, w_out_other, w_in, w_in_other, act, der, gate, tile_count):
    per = 4
    feats = per * WIDTH
    h_spec = pl.BlockSpec((ROWS, GROUP), lambda i: (0, jnp.minimum(i, STEPS - 1)))
    g_spec = pl.BlockSpec((ROWS, 1), lambda i: (0, 0))
    return pl.pallas_call(
        functools.partial(back_body, feats),
        grid=(STEPS + SLICES // per,),
        out_shape=(
            jax.ShapeDtypeStruct((tile_count, SLICES, BLK, WIDTH), jnp.bfloat16),
            jax.ShapeDtypeStruct((ROWS, 1), jnp.float32),
        ),
        in_specs=[SMEM, ANY, ANY, ANY, ANY, ANY, h_spec, h_spec, g_spec],
        out_specs=(
            pl.BlockSpec(
                (tile_count, per, BLK, WIDTH), lambda i: (0, jnp.maximum(i - STEPS, 0), 0, 0)
            ),
            g_spec,
        ),
        scratch_shapes=[
            pltpu.VMEM((SLICES, ROWS, WIDTH), jnp.bfloat16),
            pltpu.VMEM((ROWS, D), jnp.bfloat16),
            pltpu.VMEM((2, GROUP, D), jnp.bfloat16),
            pltpu.VMEM((2, feats, CHIP_UNITS), jnp.bfloat16),
            pltpu.VMEM((ROWS, CHIP_UNITS), jnp.bfloat16),
            pltpu.SemaphoreType.DMA,
            pltpu.SemaphoreType.DMA((2, 2)),
            pltpu.SemaphoreType.DMA((2, 2, STEPS)),
        ],
        compiler_params=params(BACK_MIB),
        cost_estimate=cost(4 * ROWS * D * 2 * UNITS, 50 * MIB),
        name="back",
    )(tiles, dy, w_out, w_out_other, w_in, w_in_other, act, der, gate)


def rows_out_body(feats, act, wa, wb, gate, out, w_v, sems):
    step = pl.program_id(0)

    def weights(i):
        cols = pl.ds(pl.multiple_of(i * feats, feats), feats)
        slot = i % 2
        return [
            pltpu.make_async_copy(
                w.at[pl.ds(j * HALF, HALF), cols],
                w_v.at[slot, pl.ds(j * GROUP + k * HALF, HALF), :],
                sems.at[slot, k, j],
            )
            for k, w in enumerate((wa, wb))
            for j in range(STEPS)
        ]

    @pl.when(step == 0)
    def _():
        start(weights(0))

    @pl.when(step + 1 < pl.num_programs(0))
    def _():
        start(weights(step + 1))

    wait(weights(step))
    o = jnp.dot(act[...], w_v[step % 2], preferred_element_type=jnp.float32)
    o = (o * gate[...]).astype(out.dtype)
    for f in range(out.shape[0]):
        out[f] = o[:, f * WIDTH : (f + 1) * WIDTH]


def rows_out(act, w_out, w_out_other, gate):
    per = 4
    feats = per * WIDTH
    return pl.pallas_call(
        functools.partial(rows_out_body, feats),
        grid=(SLICES // per,),
        out_shape=jax.ShapeDtypeStruct((SLICES, ROWS, WIDTH), jnp.bfloat16),
        in_specs=[
            pl.BlockSpec((ROWS, CHIP_UNITS), lambda i: (0, 0)),
            ANY,
            ANY,
            pl.BlockSpec((ROWS, 1), lambda i: (0, 0)),
        ],
        out_specs=pl.BlockSpec((per, ROWS, WIDTH), lambda i: (i, 0, 0)),
        scratch_shapes=[
            pltpu.VMEM((2, CHIP_UNITS, feats), jnp.bfloat16),
            pltpu.SemaphoreType.DMA((2, 2, STEPS)),
        ],
        compiler_params=params(OUT_MIB),
        cost_estimate=cost(2 * ROWS * D * 2 * UNITS, 21 * MIB),
        name="rows_out",
    )(act, w_out, w_out_other, gate)


def merge_body(count, ids, parts, out, total):
    total[...] = jnp.zeros_like(total)

    def step(i, carry):
        total[ids[i]] += parts[i].astype(jnp.float32)
        return carry

    lax.fori_loop(0, count, step, 0)
    out[...] = total[: out.shape[0]].astype(out.dtype)


def merge(parts, ids, blocks):
    count = parts.shape[0]
    return pl.pallas_call(
        functools.partial(merge_body, count),
        out_shape=jax.ShapeDtypeStruct((blocks, BLK, WIDTH), jnp.bfloat16),
        in_specs=[SMEM, VMEM],
        out_specs=VMEM,
        scratch_shapes=[pltpu.VMEM((blocks + 1, BLK, WIDTH), jnp.float32)],
        compiler_params=params(MERGE_MIB),
        cost_estimate=cost(0, (count + blocks) * BLK * WIDTH * 2 * 2),
        name="merge",
    )(ids, parts)


def exchange(value):
    return lax.all_to_all(value, "exp", split_axis=0, concat_axis=0, tiled=True)


def along_z(value, hops, chips):
    pairs = [
        (2 * ((z + hops) % chips) + core, 2 * z + core) for z in range(chips) for core in range(2)
    ]
    return lax.ppermute(value, "tok", pairs)


def other_core(value, chips):
    return lax.ppermute(value, "tok", [(i, i ^ 1) for i in range(2 * chips)])


def on_device(tokens, cotangent, gates, picks, w_in, w_out):
    tile_count = lax.axis_size("tok")
    chips = tile_count // 2
    my_tile = lax.axis_index("tok")
    my_expert = lax.axis_index("exp")
    core = my_tile % 2
    blocks = tokens.shape[0] // BLK
    experts = gates.shape[1]
    w_in, w_out = w_in[0], w_out[0]

    cot_all = lax.all_gather(cotangent.reshape(blocks, BLK, WIDTH), "tok", tiled=True)
    tile_picks = lax.dynamic_index_in_dim(picks, my_tile, 0, False)
    x_slot = pick_blocks(tokens.reshape(blocks, BLK, WIDTH), jnp.minimum(tile_picks, blocks - 1))
    x_mine = exchange(x_slot)

    chosen = picks < blocks
    order = jnp.arange(tile_count, dtype=jnp.int32)
    before = (order[None, :] < order[:, None])[:, :, None] & chosen[None]
    rank = jnp.sum(before.astype(jnp.int32), axis=1)
    slot = jnp.arange(CAP, dtype=jnp.int32)
    at_slot = chosen[:, :, None] & (rank[:, :, None] == slot)
    slot_tile = jnp.sum(jnp.where(at_slot, order[:, None, None], 0), axis=0)
    slot_block = jnp.sum(jnp.where(at_slot, picks[:, :, None], 0), axis=0)
    slot_place = (slot_tile // 2 - my_tile // 2) % chips + chips * ((slot_tile + core) % 2)

    def own_of(values):
        return lax.dynamic_slice_in_dim(values, core * OWN, OWN, 1)

    own_rows = own_of(slot_tile * blocks + slot_block)
    own_places = own_of(slot_place * blocks + slot_block)
    own_tiles = lax.dynamic_index_in_dim(own_of(slot_tile), my_expert, 0, False)
    my_places = lax.dynamic_index_in_dim(own_places, my_expert, 0, False)
    my_rows = lax.dynamic_index_in_dim(own_rows, my_expert, 0, False)

    gate_mine = lax.dynamic_index_in_dim(gates, my_expert, 1, False).reshape(blocks, BLK)
    gate_all = lax.all_gather(gate_mine, "tok", tiled=True)
    gate = jnp.take(gate_all, my_rows, axis=0, mode="clip").reshape(ROWS, 1)
    places = my_places // blocks
    x_mine, gate, places, own_tiles = lax.optimization_barrier((x_mine, gate, places, own_tiles))
    above, below = along_z(x_mine, 1, chips), along_z(x_mine, 3, chips)
    far = [along_z(above[:PART], 1, chips), along_z(below[PART:], 3, chips)]
    x_near = [x_mine, above, below, *far]
    send_dy = pick_blocks(cot_all, own_rows.reshape(-1))
    dy = exchange(send_dy.reshape(experts, ROWS, WIDTH))
    x_all = x_near + [other_core(piece, chips) for piece in x_near]
    w_in_other = other_core(w_in, chips)
    w_out_other = other_core(w_out, chips)

    act, der = hidden(places, x_all, w_in, w_in_other)
    dx_all, dgate = back(
        own_tiles, dy, w_out, w_out_other, w_in, w_in_other, act, der, gate, tile_count
    )
    out_rows = rows_out(act, w_out, w_out_other, gate)

    dx = lax.psum_scatter(dx_all, "tok", scatter_dimension=0)

    parts = exchange(out_rows).reshape(experts * OWN, BLK, WIDTH)
    mixed_all = merge(parts, own_rows.reshape(-1), tile_count * blocks)
    mixed = lax.psum_scatter(
        mixed_all.reshape(tile_count, blocks * BLK, WIDTH), "tok", scatter_dimension=0
    )
    dx = exchange(dx)
    d_tokens = merge(dx, tile_picks, blocks)

    dgate = dgate.reshape(OWN, BLK)
    dgate += sum(along_z(dgate, k, chips) for k in (1, 2, 3))
    theirs = other_core(dgate, chips)
    low = jnp.where(core == 0, dgate, theirs)
    high = jnp.where(core == 0, theirs, dgate)
    both = jnp.concatenate([low, high])
    both, _ = lax.optimization_barrier((both, dx))
    grads = exchange(jnp.broadcast_to(both[None], (experts, CAP, BLK)))
    taken = lax.dynamic_index_in_dim(chosen, my_tile, 0, False)
    here = (slot_tile == my_tile) & taken[:, None]
    mine = jnp.sum(jnp.where(here[:, :, None], grads, 0.0), axis=1)
    at_block = tile_picks[None, :] == jnp.arange(blocks, dtype=jnp.int32)[:, None]
    d_gates = jnp.where(at_block[:, None, :], mine.T[None], 0.0)
    return (
        mixed,
        d_tokens.reshape(blocks * BLK, WIDTH),
        d_gates.reshape(blocks * BLK, experts),
    )


def solution(mesh):
    return jax.shard_map(
        on_device,
        mesh=mesh,
        in_specs=(
            P("tok", "exp"),
            P("tok", "exp"),
            P("tok", None),
            P(),
            P("exp", None, "tok"),
            P("exp", "tok", None),
        ),
        out_specs=(P("tok", "exp"), P("tok", "exp"), P("tok", None)),
        check_vma=False,
    )
```

time: 251 us -> 240 us (0.956)
  waiting for transfers between devices: 67.2 us -> 44.8 us
  starting transfers between devices: 22.6 us -> 33.8 us
  local copies, waits for them, and re-layouts: 6.08 us -> 9.69 us
  blocking collectives: 70.9 us -> 67.4 us
    all_gather x1 -> x0, waiting for transfers between devices: 30.5 us -> none  [on_device(): x_all = lax.all_gather(exchange(x_slot), 'tok')]
    all_to_all x2 -> x1, blocking collectives: 70.9 us -> 47 us  [exchange(): return lax.all_to_all(value, 'exp', split_axis=0, concat_axis=0, tiled=True)]
    ppermute x6 -> x7, waiting for transfers between devices: 3.36 us -> 25.2 us  [along_z(): return lax.ppermute(value, 'tok', pairs)]
    all_gather x0 -> x1, blocking collectives: none -> 20.4 us  [on_device(): gate_all = lax.all_gather(gate_mine, 'tok', tiled=True)]
    all_gather x1, waiting for transfers between devices: 13.7 us -> 0.01 us  [on_device(): lax.all_gather(cotangent.reshape(blocks, BLK, WIDTH), 'tok', tiled=True)]
    all_to_all x3 -> x4, starting transfers between devices: 11.7 us -> 21.5 us  [exchange(): return lax.all_to_all(value, 'exp', split_axis=0, concat_axis=0, tiled=True)]
    all_to_all x3 -> x4, waiting for transfers between devices: 14 us -> 10.6 us  [exchange(): return lax.all_to_all(value, 'exp', split_axis=0, concat_axis=0, tiled=True)]
    ppermute x6 -> x7, starting transfers between devices: 10.1 us -> 11.2 us  [along_z(): return lax.ppermute(value, 'tok', pairs)]
  transfers between devices with their start and end apart: 17 -> 22, of which waited for: 11 -> 12; matrix products, arithmetic and copies ran while one was open for 2% -> 4% of each run, Pallas kernels for 17% -> 18%
where the time goes in v3:
time: 240 us; the launch traced here: 239 us
  Pallas kernels  67.4 us (28%)
  blocking collectives  67.4 us (28%)
  waiting for transfers between devices  44.8 us (19%)
  starting transfers between devices  33.8 us (14%)
  between operations  14 us (6%)
  local copies, waits for them, and re-layouts  9.69 us (4%)
    all_to_all x1, blocking collectives, exchange(): return lax.all_to_all(value, 'exp', split_axis=0, concat_axis=0, tiled=True)  47 us
    ppermute x7, waiting for transfers between devices, along_z(): return lax.ppermute(value, 'tok', pairs)  25.2 us
    pallas_call x1, Pallas kernels, back(): pl.pallas_call(functools.partial(back_body, feats), grid=(STEPS + SLICES...  24.7 us
    all_to_all x4, starting transfers between devices, exchange(): return lax.all_to_all(value, 'exp', split_axis=0, concat_axis=0, tiled=True)  21.5 us
    all_gather x1, blocking collectives, on_device(): gate_all = lax.all_gather(gate_mine, 'tok', tiled=True)  20.4 us
    pallas_call x1, Pallas kernels, hidden(): pl.pallas_call(functools.partial(hidden_body, len(srcs)), grid=(STEPS,),...  14.2 us
    pallas_call x1, Pallas kernels, rows_out(): pl.pallas_call(functools.partial(rows_out_body, feats), grid=(SLICES // p...  12.7 us
    ppermute x7, starting transfers between devices, along_z(): return lax.ppermute(value, 'tok', pairs)  11.2 us
  transfers between devices with their start and end apart: 22, of which 12 were waited for; matrix products, arithmetic and copies ran while one was open for 4% of the time, Pallas kernels for 18%

profile of v3, /device:TPU:0, one launch (start us, length us, event | category | flops | bytes accessed | tf_op | source)
XLA Modules:
  0.0 239.5 jit_solution(14623745642094095696)
XLA Ops:
  8.5 1.2 broadcast_minimum_fusion
  9.7 3.1 %pick_blocks.2 = bf16[16,128,256]{2,1,0:T(8,128)(2,1)} custom-call(s32[16]{0:T(128)} %get-tuple-element.23.ids, bf16[8,128,256]{2,1,0:T(8,128)(2,1)} %bitcast.35), custom_call_target="tpu_custom_call" | custom-call | bytes 2097152 | tf_op jit(solution)/shard_map/pick_blocks/pallas_call | solution.py:48
  12.9 7.2 %all-to-all-start = ((bf16[16,128,256]{2,1,0:T(8,128)(2,1)}), bf16[16,128,256]{2,1,0:T(8,128)(2,1)}, u32[]{:S(2)}, u32[]{:S(2)}) async-start(bf16[16,128,256]{2,1,0:T(8,128)(2,1)} %pick_blocks.2), calls=%async_computation | async-start | bytes 2097152 | tf_op jit(solution)/shard_map/all_to_all | solution.py:346
  21.4 20.4 %all_gather.6 = f32[64,128]{1,0:T(8,128)S(1)} all-gather(f32[8,128]{1,0:T(8,128)S(1)} %bitcast.41), channel_id=1, replica_groups=mesh['tok'=8,'exp'=16] {'tok'}, dimensions={0}, use_global_device_ids=true | all-gather | bytes 36864 | tf_op jit(solution)/shard_map/all_gather | solution.py:395
  42.9 1.6 collective-permute-start.1
  44.5 1.6 collective-permute-start
  46.8 4.8 %pick_blocks.3 = bf16[48,128,256]{2,1,0:T(8,128)(2,1)} custom-call(s32[48]{0:T(128)} %reshape.103.ids, bf16[64,128,256]{2,1,0:T(8,128)(2,1)} %all-gather.2.cloned.1.call-done.src), custom_call_target="tpu_custom_call" | custom-call | bytes 6291456 | tf_op jit(solution)/shard_map/pick_blocks/pallas_call | solution.py:48
  51.7 7.1 %all-to-all-start.2 = ((bf16[16,384,256]{2,1,0:T(8,128)(2,1)}), bf16[16,384,256]{2,1,0:T(8,128)(2,1)S(1)}, u32[]{:S(2)}, u32[]{:S(2)}) async-start(bf16[16,384,256]{2,1,0:T(8,128)(2,1)} %bitcast.32), calls=%async_computation.3 | async-start | bytes 6291456 | tf_op jit(solution)/shard_map/all_to_all | solution.py:346
  58.8 11.0 %collective-permute-done.1.refs_2_ = bf16[16,128,256]{2,1,0:T(8,128)(2,1)} collective-permute-done((bf16[16,128,256]{2,1,0:T(8,128)(2,1)}, bf16[16,128,256]{2,1,0:T(8,128)(2,1)}, u32[]{:S(2)}, u32[]{:S(2)}) %collective-permute-start.1) | collective-permute-done | bytes 1048608 | tf_op jit(solution)/shard_map/ppermute | solution.py:353
  69.8 1.1 slice.11
  71.4 1.1 slice.10
  72.4 2.9 %collective-permute-start.2 = (bf16[8,128,256]{2,1,0:T(8,128)(2,1)S(1)}, bf16[8,128,256]{2,1,0:T(8,128)(2,1)}, u32[]{:S(2)}, u32[]{:S(2)}) collective-permute-start(bf16[8,128,256]{2,1,0:T(8,128)(2,1)S(1)} %slice.10), channel_id=1, source_target_pairs={{32,0},{48,16},{64,32},{80,48},{96,64},{112,80},{0,96},{16,112},{3... | collective-permute-start | bytes 1572872 | tf_op jit(solution)/shard_map/ppermute | solution.py:353
  75.3 10.1 %collective-permute-done.3.refs_4_ = bf16[8,128,256]{2,1,0:T(8,128)(2,1)S(1)} collective-permute-done((bf16[8,128,256]{2,1,0:T(8,128)(2,1)S(1)}, bf16[8,128,256]{2,1,0:T(8,128)(2,1)S(1)}, u32[]{:S(2)}, u32[]{:S(2)}) %collective-permute-start.3) | collective-permute-done | bytes 524320 | tf_op jit(solution)/shard_map/ppermute | solution.py:353
  86.3 1.1 collective-permute-done.8.refs_9_
  88.3 0.8 copy.20.gate
  89.2 1.3 collective-permute-done.7.refs_8_
  90.5 14.2 %hidden.1 = (bf16[384,2048]{1,0:T(8,128)(2,1)}, f32[384,2048]{1,0:T(8,128)}) custom-call(s32[3]{0:T(128)} %and_select_fusion.picked, bf16[16,128,256]{2,1,0:T(8,128)(2,1)} %all-to-all-done.refs_0_, bf16[16,128,256]{2,1,0:T(8,128)(2,1)} %collective-permute-done.refs_1_, bf16[16,128,256]{2,1,0:T(8,128)(2,1)} %collective-permute-done.1.refs_2_, ...), custom_call_target="tpu_custom_call" | custom-call | flops 12884901888 | bytes 25165824 | tf_op jit(solution)/shard_map/hidden/pallas_call | solution.py:131
  104.7 1.7 copy-done.3
  106.4 24.7 %back.1 = (bf16[8,16,128,256]{3,2,1,0:T(8,128)(2,1)}, f32[384,1]{1,0:T(8,128)}) custom-call(s32[3]{0:T(128)} %dynamic-slice_reduce_fusion.tiles, bf16[16,384,256]{2,1,0:T(8,128)(2,1)} %copy-done.3, bf16[1024,4096]{1,0:T(8,128)(2,1)} %bitcast.51, bf16[1024,4096]{1,0:T(8,128)(2,1)} %collective-permute-done.10.wb.ob, bf16[4096,1024]{1,0:T(8,128)(2,1)} %bitcast.49, ...), custom_call_target="tpu_custom_call" | custom-call | flops 12884901888 | bytes 52428800 | tf_op jit(solution)/shard_map/back/pallas_call | solution.py:235
  131.4 12.7 %rows_out.1 = bf16[16,384,256]{2,1,0:T(8,128)(2,1)} custom-call(bf16[384,2048]{1,0:T(8,128)(2,1)} %get-tuple-element.14.act, bf16[1024,4096]{1,0:T(8,128)(2,1)} %bitcast.52, bf16[1024,4096]{1,0:T(8,128)(2,1)} %collective-permute-done.10.wb.ob, f32[384,1]{1,0:T(8,128)} %copy.20.gate), custom_call_target="tpu_custom_call" | custom-call | flops 6442450944 | bytes 22020096 | tf_op jit(solution)/shard_map/rows_out/pallas_call | solution.py:299
  144.0 47.0 %all_to_all.25 = bf16[16,384,256]{2,1,0:T(8,128)(2,1)} all-to-all(bf16[16,384,256]{2,1,0:T(8,128)(2,1)} %rows_out.1), channel_id=1, replica_groups=mesh['tok'=8,'exp'=16] {'exp'}, dimensions={0} | all-to-all | bytes 6291456 | tf_op jit(solution)/shard_map/all_to_all | solution.py:346
  191.1 5.5 %merge.2 = bf16[64,128,256]{2,1,0:T(8,128)(2,1)} custom-call(s32[48]{0:T(128)} %reshape.103.ids, bf16[48,128,256]{2,1,0:T(8,128)(2,1)} %bitcast.33), custom_call_target="tpu_custom_call" | custom-call | bytes 14680064 | tf_op jit(solution)/shard_map/merge/pallas_call | solution.py:333
  196.6 3.8 %all-to-all-start.3 = ((bf16[16,128,256]{2,1,0:T(8,128)(2,1)}), bf16[16,128,256]{2,1,0:T(8,128)(2,1)S(1)}, u32[]{:S(2)}, u32[]{:S(2)}) async-start(bf16[16,128,256]{2,1,0:T(8,128)(2,1)} %bitcast.34), calls=%async_computation.5 | async-start | bytes 2097152 | tf_op jit(solution)/shard_map/all_to_all | solution.py:346
  200.9 4.2 %collective-permute-start.12 = (f32[3,128]{1,0:T(4,128)S(1)}, f32[3,128]{1,0:T(4,128)S(1)}, u32[]{:S(2)}, u32[]{:S(2)}) collective-permute-start(f32[3,128]{1,0:T(4,128)S(1)} %bitcast.43), channel_id=1, source_target_pairs={{64,0},{80,16},{96,32},{112,48},{0,64},{16,80},{32,96},{48,112},{6... | collective-permute-start | bytes 4616 | tf_op jit(solution)/shard_map/ppermute | solution.py:353
  205.5 1.3 collective-permute-done.12
  206.8 2.1 collective-permute-done.11
  208.9 1.1 collective-permute-done.14
  210.0 5.5 %all-to-all-done.3.parts = bf16[16,128,256]{2,1,0:T(8,128)(2,1)S(1)} async-done(((bf16[16,128,256]{2,1,0:T(8,128)(2,1)}), bf16[16,128,256]{2,1,0:T(8,128)(2,1)S(1)}, u32[]{:S(2)}, u32[]{:S(2)}) %all-to-all-start.3) | async-done | bytes 1048608 | tf_op jit(solution)/shard_map/all_to_all | solution.py:346
  216.2 3.5 %all-to-all-start.4 = ((f32[16,6,128]{2,1,0:T(8,128)}), f32[16,6,128]{2,1,0:T(8,128)S(1)}, u32[]{:S(2)}, u32[]{:S(2)}) async-start(f32[16,6,128]{2,1,0:T(8,128)} %broadcast_in_dim.85), calls=%async_computation.6 | async-start | bytes 131072 | tf_op jit(solution)/shard_map/all_to_all | solution.py:346
  219.9 2.4 %merge.3 = bf16[8,128,256]{2,1,0:T(8,128)(2,1)} custom-call(s32[16]{0:T(128)} %copy-done.6, bf16[16,128,256]{2,1,0:T(8,128)(2,1)} %copy-done.2), custom_call_target="tpu_custom_call" | custom-call | bytes 3145728 | tf_op jit(solution)/shard_map/merge/pallas_call | solution.py:333
  222.3 5.0 %all-to-all-done.4 = f32[16,6,128]{2,1,0:T(8,128)S(1)} async-done(((f32[16,6,128]{2,1,0:T(8,128)}), f32[16,6,128]{2,1,0:T(8,128)S(1)}, u32[]{:S(2)}, u32[]{:S(2)}) %all-to-all-start.4) | async-done | bytes 49184 | tf_op jit(solution)/shard_map/all_to_all | solution.py:346
  228.2 4.7 %reduce-scatter.3.cloned.1.call-done = bf16[1,1024,256]{2,1,0:T(8,128)(2,1)} async-done(((bf16[8,1024,256]{2,1,0:T(8,128)(2,1)}), bf16[1,1024,256]{2,1,0:T(8,128)(2,1)}) %reduce-scatter.3.cloned.1.call-update) | async-done | bytes 524304 | tf_op jit(solution)/shard_map/reduce_scatter | solution.py:418
  (74 shorter events, 9.4 us)
Async XLA Ops:
  7.2 14.2 %copy-start = (f32[1024,16]{0,1:T(8,128)S(1)}, f32[1024,16]{0,1:T(8,128)}, u32[]{:S(2)}) copy-start(f32[1024,16]{0,1:T(8,128)} %param.8) | copy-start | bytes 196612
  7.2 12.9 %copy-start.5 = (s32[8,16]{1,0:T(8,128)S(1)}, s32[8,16]{1,0:T(8,128)}, u32[]{:S(2)}) copy-start(s32[8,16]{1,0:T(8,128)} %param.9) | copy-start | bytes 1540
  7.2 39.7 %all-gather.2.cloned.1.call-start = ((), (), s32[]{:S(2)}) async-start(), calls=%async_computation.8 | async-start | bytes 4718592 | tf_op jit(solution)/shard_map/all_gather | solution.py:370
  7.9 82.5 %collective-permute-start.9 = (bf16[4096,1024]{1,0:T(8,128)(2,1)}, bf16[4096,1024]{1,0:T(8,128)(2,1)}, u32[]{:S(2)}, u32[]{:S(2)}) collective-permute-start(bf16[4096,1024]{1,0:T(8,128)(2,1)} %bitcast.47), channel_id=1, source_target_pairs={{0,16},{16,0},{32,48},{48,32},{64,80},{80,64},{96,112},{112,96},{1... | collective-permute-start | bytes 25165832 | tf_op jit(solution)/shard_map/ppermute | solution.py:357
  8.0 96.6 %collective-permute-start.10 = (bf16[1024,4096]{1,0:T(8,128)(2,1)}, bf16[1024,4096]{1,0:T(8,128)(2,1)}, u32[]{:S(2)}, u32[]{:S(2)}) collective-permute-start(bf16[1024,4096]{1,0:T(8,128)(2,1)} %bitcast.50), channel_id=1, source_target_pairs={{0,16},{16,0},{32,48},{48,32},{64,80},{80,64},{96,112},{112,96},{1... | collective-permute-start | bytes 25165832 | tf_op jit(solution)/shard_map/ppermute | solution.py:357
  9.7 210.0 %copy-start.6 = (s32[16]{0:T(128)}, s32[16]{0:T(128)S(1)}, u32[]{:S(2)}) copy-start(s32[16]{0:T(128)S(1)} %get-tuple-element.24.ids) | copy-start | bytes 196
  12.9 30.1 %all-to-all-start = ((bf16[16,128,256]{2,1,0:T(8,128)(2,1)}), bf16[16,128,256]{2,1,0:T(8,128)(2,1)}, u32[]{:S(2)}, u32[]{:S(2)}) async-start(bf16[16,128,256]{2,1,0:T(8,128)(2,1)} %pick_blocks.2), calls=%async_computation | async-start | bytes 2097152 | tf_op jit(solution)/shard_map/all_to_all | solution.py:346
  42.9 26.9 %collective-permute-start.1 = (bf16[16,128,256]{2,1,0:T(8,128)(2,1)}, bf16[16,128,256]{2,1,0:T(8,128)(2,1)}, u32[]{:S(2)}, u32[]{:S(2)}) collective-permute-start(bf16[16,128,256]{2,1,0:T(8,128)(2,1)} %all-to-all-done.refs_0_), channel_id=1, source_target_pairs={{96,0},{112,16},{0,32},{16,48},{32,64},{48,80},{64,96},{80,112},{9... | collective-permute-start | bytes 3145736 | tf_op jit(solution)/shard_map/ppermute | solution.py:353
  44.5 26.8 %collective-permute-start = (bf16[16,128,256]{2,1,0:T(8,128)(2,1)}, bf16[16,128,256]{2,1,0:T(8,128)(2,1)}, u32[]{:S(2)}, u32[]{:S(2)}) collective-permute-start(bf16[16,128,256]{2,1,0:T(8,128)(2,1)} %all-to-all-done.refs_0_), channel_id=1, source_target_pairs={{32,0},{48,16},{64,32},{80,48},{96,64},{112,80},{0,96},{16,112},{3... | collective-permute-start | bytes 3145736 | tf_op jit(solution)/shard_map/ppermute | solution.py:353
  46.1 29.2 %collective-permute-start.4 = (bf16[16,128,256]{2,1,0:T(8,128)(2,1)}, bf16[16,128,256]{2,1,0:T(8,128)(2,1)}, u32[]{:S(2)}, u32[]{:S(2)}) collective-permute-start(bf16[16,128,256]{2,1,0:T(8,128)(2,1)} %all-to-all-done.refs_0_), channel_id=1, source_target_pairs={{0,16},{16,0},{32,48},{48,32},{64,80},{80,64},{96,112},{112,96},{1... | collective-permute-start | bytes 3145736 | tf_op jit(solution)/shard_map/ppermute | solution.py:357
  51.7 53.0 %all-to-all-start.2 = ((bf16[16,384,256]{2,1,0:T(8,128)(2,1)}), bf16[16,384,256]{2,1,0:T(8,128)(2,1)S(1)}, u32[]{:S(2)}, u32[]{:S(2)}) async-start(bf16[16,384,256]{2,1,0:T(8,128)(2,1)} %bitcast.32), calls=%async_computation.3 | async-start | bytes 6291456 | tf_op jit(solution)/shard_map/all_to_all | solution.py:346
  58.7 137.9 %reduce-scatter.5.cloned.1.call-start = ((), (), s32[]{:S(2)}) async-start(), calls=%async_computation.9 | async-start | bytes 9437184 | tf_op jit(solution)/shard_map/reduce_scatter | solution.py:414
  70.9 14.6 %collective-permute-start.3 = (bf16[8,128,256]{2,1,0:T(8,128)(2,1)S(1)}, bf16[8,128,256]{2,1,0:T(8,128)(2,1)S(1)}, u32[]{:S(2)}, u32[]{:S(2)}) collective-permute-start(bf16[8,128,256]{2,1,0:T(8,128)(2,1)S(1)} %slice.11), channel_id=1, source_target_pairs={{96,0},{112,16},{0,32},{16,48},{32,64},{48,80},{64,96},{80,112},{9... | collective-permute-start | bytes 1572872 | tf_op jit(solution)/shard_map/ppermute | solution.py:353
  72.4 13.5 %collective-permute-start.2 = (bf16[8,128,256]{2,1,0:T(8,128)(2,1)S(1)}, bf16[8,128,256]{2,1,0:T(8,128)(2,1)}, u32[]{:S(2)}, u32[]{:S(2)}) collective-permute-start(bf16[8,128,256]{2,1,0:T(8,128)(2,1)S(1)} %slice.10), channel_id=1, source_target_pairs={{32,0},{48,16},{64,32},{80,48},{96,64},{112,80},{0,96},{16,112},{3... | collective-permute-start | bytes 1572872 | tf_op jit(solution)/shard_map/ppermute | solution.py:353
  75.3 13.8 %collective-permute-start.6 = (bf16[16,128,256]{2,1,0:T(8,128)(2,1)}, bf16[16,128,256]{2,1,0:T(8,128)(2,1)}, u32[]{:S(2)}, u32[]{:S(2)}) collective-permute-start(bf16[16,128,256]{2,1,0:T(8,128)(2,1)} %collective-permute-done.1.refs_2_), channel_id=1, source_target_pairs={{0,16},{16,0},{32,48},{48,32},{64,80},{80,64},{96,112},{112,96},{1... | collective-permute-start | bytes 3145736 | tf_op jit(solution)/shard_map/ppermute | solution.py:357
  85.5 0.8 copy-start.7
  85.5 1.9 collective-permute-start.8
  86.3 4.2 %collective-permute-start.5 = (bf16[16,128,256]{2,1,0:T(8,128)(2,1)}, bf16[16,128,256]{2,1,0:T(8,128)(2,1)}, u32[]{:S(2)}, u32[]{:S(2)}) collective-permute-start(bf16[16,128,256]{2,1,0:T(8,128)(2,1)} %collective-permute-done.refs_1_), channel_id=1, source_target_pairs={{0,16},{16,0},{32,48},{48,32},{64,80},{80,64},{96,112},{112,96},{1... | collective-permute-start | bytes 3145736 | tf_op jit(solution)/shard_map/ppermute | solution.py:357
  87.4 0.8 copy-start.8
  88.2 2.3 collective-permute-start.7
  104.6 1.7 copy-start.3
  131.1 101.8 %reduce-scatter.3.cloned.1.call-start = ((), (), s32[]{:S(2)}) async-start(), calls=%async_computation.7 | async-start | bytes 4718592 | tf_op jit(solution)/shard_map/reduce_scatter | solution.py:418
  196.6 3.9 %copy-start.4 = (f32[384,1]{1,0:T(8,128)S(1)}, f32[384,1]{1,0:T(8,128)}, u32[]{:S(2)}) copy-start(f32[384,1]{1,0:T(8,128)} %get-tuple-element.19) | copy-start | bytes 4612
  196.6 36.4 %copy-start.1 = (f32[1024,16]{0,1:T(8,128)S(1)}, f32[1024,16]{0,1:T(8,128)}, u32[]{:S(2)}) copy-start(f32[1024,16]{0,1:T(8,128)} %param.8) | copy-start | bytes 196612
  196.6 18.9 %all-to-all-start.3 = ((bf16[16,128,256]{2,1,0:T(8,128)(2,1)}), bf16[16,128,256]{2,1,0:T(8,128)(2,1)S(1)}, u32[]{:S(2)}, u32[]{:S(2)}) async-start(bf16[16,128,256]{2,1,0:T(8,128)(2,1)} %bitcast.34), calls=%async_computation.5 | async-start | bytes 2097152 | tf_op jit(solution)/shard_map/all_to_all | solution.py:346
  200.6 4.9 %collective-permute-start.13 = (f32[3,128]{1,0:T(4,128)S(1)}, f32[3,128]{1,0:T(4,128)S(1)}, u32[]{:S(2)}, u32[]{:S(2)}) collective-permute-start(f32[3,128]{1,0:T(4,128)S(1)} %bitcast.42), channel_id=1, source_target_pairs={{96,0},{112,16},{0,32},{16,48},{32,64},{48,80},{64,96},{80,112},{9... | collective-permute-start | bytes 4616 | tf_op jit(solution)/shard_map/ppermute | solution.py:353
  200.9 5.9 %collective-permute-start.12 = (f32[3,128]{1,0:T(4,128)S(1)}, f32[3,128]{1,0:T(4,128)S(1)}, u32[]{:S(2)}, u32[]{:S(2)}) collective-permute-start(f32[3,128]{1,0:T(4,128)S(1)} %bitcast.43), channel_id=1, source_target_pairs={{64,0},{80,16},{96,32},{112,48},{0,64},{16,80},{32,96},{48,112},{6... | collective-permute-start | bytes 4616 | tf_op jit(solution)/shard_map/ppermute | solution.py:353
  205.1 3.7 %collective-permute-start.11 = (f32[3,128]{1,0:T(4,128)S(1)}, f32[3,128]{1,0:T(4,128)S(1)}, u32[]{:S(2)}, u32[]{:S(2)}) collective-permute-start(f32[3,128]{1,0:T(4,128)S(1)} %bitcast.44), channel_id=1, source_target_pairs={{32,0},{48,16},{64,32},{80,48},{96,64},{112,80},{0,96},{16,112},{3... | collective-permute-start | bytes 4616 | tf_op jit(solution)/shard_map/ppermute | solution.py:353
  208.8 1.2 collective-permute-start.14
  215.5 4.4 %copy-start.2 = (bf16[16,128,256]{2,1,0:T(8,128)(2,1)}, bf16[16,128,256]{2,1,0:T(8,128)(2,1)S(1)}, u32[]{:S(2)}) copy-start(bf16[16,128,256]{2,1,0:T(8,128)(2,1)S(1)} %all-to-all-done.3.parts) | copy-start | bytes 3145732
  216.2 11.2 %all-to-all-start.4 = ((f32[16,6,128]{2,1,0:T(8,128)}), f32[16,6,128]{2,1,0:T(8,128)S(1)}, u32[]{:S(2)}, u32[]{:S(2)}) async-start(f32[16,6,128]{2,1,0:T(8,128)} %broadcast_in_dim.85), calls=%async_computation.6 | async-start | bytes 131072 | tf_op jit(solution)/shard_map/all_to_all | solution.py:346
Sparse Core Ops, SparseCore 0:
  9.7 34.9 all-gather.1
  131.2 54.0 reduce-scatter.4
  196.7 36.1 reduce-scatter.2

commit v4 on v3

--- a/solution.py
+++ b/solution.py
@@ -19,7 +19,8 @@
 GELU_K = 0.044715
 MIB = 1024 * 1024
 HID_COST = 2
-PICK_MIB, HID_MIB, BACK_MIB, OUT_MIB, MERGE_MIB = 60, 60, 60, 60, 60
+BACK_COST = 16
+PICK_MIB, HID_MIB, BACK_MIB, MERGE_MIB = 60, 60, 62, 60
 ANY = pl.BlockSpec(memory_space=pl.ANY)
 SMEM = pl.BlockSpec(memory_space=pltpu.SMEM)
 VMEM = pl.BlockSpec(memory_space=pltpu.VMEM)
@@ -74,19 +75,52 @@
 PART = SLICES // 2
 
 
-def hidden_body(sources, picked, *refs):
+def forward_body(sources, feats, picked, tiles, empty, *refs):
     srcs = refs[:sources]
-    wa, wb, act, der, x_raw, x_v, w_v, x_sems, w_sems = refs[sources:]
+    (
+        ia, ib, oa, ob, gate, act, der, out,
+        x_raw, x_v, i_v, o_v, act_v, zero_v, r_v, x_sems, i_sems, o_sems, zero_sems, r_sems,
+    ) = refs[sources:]
     step = pl.program_id(0)
-
-    def weights(i):
+    last = pl.num_programs(0) - 1
+    per = feats // WIDTH
+
+    def in_weights(i):
         cols = pl.ds(pl.multiple_of(i * HALF, HALF), HALF)
         slot = i % 2
         return [
             pltpu.make_async_copy(
-                w.at[:, cols], w_v.at[slot, :, pl.ds(k * HALF, HALF)], w_sems.at[slot, k]
+                w.at[:, cols], i_v.at[slot, :, pl.ds(k * HALF, HALF)], i_sems.at[slot, k]
             )
-            for k, w in enumerate((wa, wb))
+            for k, w in enumerate((ia, ib))
+        ]
+
+    def out_weights(i):
+        cols = pl.ds(pl.multiple_of(i * feats, feats), feats)
+        slot = i % 2
+        return [
+            pltpu.make_async_copy(
+                w.at[pl.ds(j * HALF, HALF), cols],
+                o_v.at[slot, pl.ds(j * GROUP + k * HALF, HALF), :],
+                o_sems.at[slot, k, j],
+            )
+            for k, w in enumerate((oa, ob))
+            for j in range(STEPS)
+        ]
+
+    def zeros():
+        return [
+            pltpu.make_async_copy(zero_v, out.at[empty[k]], zero_sems.at[k])
+            for k in range(zero_sems.shape[0])
+        ]
+
+    def results(i):
+        here = pl.ds(i * per, per)
+        return [
+            pltpu.make_async_copy(
+                r_v.at[i % 2, s], out.at[tiles[s], here], r_sems.at[i % 2, s]
+            )
+            for s in range(OWN)
         ]
 
     @pl.when(step == 0)
@@ -106,52 +140,106 @@
                         to = x_raw.at[s, pl.ds(at, PART)]
                         pltpu.make_async_copy(source, to, x_sems.at[s]).start()
 
-        start(weights(0))
+        start(in_weights(0))
+        zero_v[...] = jnp.zeros_like(zero_v)
         for s in range(OWN):
             pltpu.make_async_copy(srcs[0], x_raw.at[s], x_sems.at[s]).wait()
             for f in range(SLICES):
                 x_v[s * BLK : (s + 1) * BLK, f * WIDTH : (f + 1) * WIDTH] = x_raw[s, f]
 
-    @pl.when(step + 1 < STEPS)
-    def _():
-        start(weights(step + 1))
-
-    wait(weights(step))
-    h = jnp.dot(x_v[...], w_v[step % 2], preferred_element_type=jnp.float32)
-    sq = h * h
-    t = jnp.tanh(h * (GELU_C + (GELU_C * GELU_K) * sq))
-    half = 0.5 + 0.5 * t
-    act[...] = (h * half).astype(act.dtype)
-    slope = 0.5 * GELU_C + (1.5 * GELU_C * GELU_K) * sq
-    der[...] = half + (h * slope) * (1.0 - t * t)
-
-
-def hidden(picked, srcs, w_in, w_in_other):
-    o_spec = pl.BlockSpec((ROWS, GROUP), lambda i: (0, i))
+    for k, zero in enumerate(zeros()):
+
+        @pl.when(step == k + 1)
+        def _(zero=zero):
+            zero.start()
+
+    @pl.when(step < STEPS)
+    def _():
+        @pl.when(step + 1 < STEPS)
+        def _():
+            start(in_weights(step + 1))
+
+        @pl.when(step + 1 == STEPS)
+        def _():
+            start(out_weights(0))
+
+        wait(in_weights(step))
+        h = jnp.dot(x_v[...], i_v[step % 2], preferred_element_type=jnp.float32)
+        sq = h * h
+        t = jnp.tanh(h * (GELU_C + (GELU_C * GELU_K) * sq))
+        half = 0.5 + 0.5 * t
+        a = (h * half).astype(act.dtype)
+        act[...] = a
+        act_v[:, pl.ds(pl.multiple_of(step * GROUP, GROUP), GROUP)] = a
+        slope = 0.5 * GELU_C + (1.5 * GELU_C * GELU_K) * sq
+        der[...] = half + (h * slope) * (1.0 - t * t)
+
+    @pl.when(step >= STEPS)
+    def _():
+        i = step - STEPS
+
+        @pl.when(step < last)
+        def _():
+            start(out_weights(i + 1))
+
+        wait(out_weights(i))
+
+        @pl.when(i >= 2)
+        def _():
+            wait(results(i - 2))
+
+        o = jnp.dot(act_v[...], o_v[i % 2], preferred_element_type=jnp.float32)
+        o = (o * gate[...]).astype(out.dtype)
+        for s in range(OWN):
+            for f in range(per):
+                r_v[i % 2, s, f] = o[s * BLK : (s + 1) * BLK, f * WIDTH : (f + 1) * WIDTH]
+        start(results(i))
+
+        @pl.when(step == last)
+        def _():
+            wait(results(i - 1))
+            wait(results(i))
+            wait(zeros())
+
+
+def forward(picked, tiles, empty, srcs, w_in, w_in_other, w_out, w_out_other, gate, tile_count):
+    per = 4
+    feats = per * WIDTH
+    o_spec = pl.BlockSpec((ROWS, GROUP), lambda i: (0, jnp.minimum(i, STEPS - 1)))
     return pl.pallas_call(
-        functools.partial(hidden_body, len(srcs)),
-        grid=(STEPS,),
+        functools.partial(forward_body, len(srcs), feats),
+        grid=(STEPS + SLICES // per,),
         out_shape=(
             jax.ShapeDtypeStruct((ROWS, CHIP_UNITS), jnp.bfloat16),
             jax.ShapeDtypeStruct((ROWS, CHIP_UNITS), jnp.float32),
+            jax.ShapeDtypeStruct((tile_count, SLICES, BLK, WIDTH), jnp.bfloat16),
         ),
-        in_specs=[SMEM] + [ANY] * (len(srcs) + 2),
-        out_specs=(o_spec, o_spec),
+        in_specs=[SMEM] * 3
+        + [ANY] * (len(srcs) + 4)
+        + [pl.BlockSpec((ROWS, 1), lambda i: (0, 0))],
+        out_specs=(o_spec, o_spec, ANY),
         scratch_shapes=[
             pltpu.VMEM((OWN, SLICES, BLK, WIDTH), jnp.bfloat16),
             pltpu.VMEM((ROWS, D), jnp.bfloat16),
             pltpu.VMEM((2, D, GROUP), jnp.bfloat16),
+            pltpu.VMEM((2, CHIP_UNITS, feats), jnp.bfloat16),
+            pltpu.VMEM((ROWS, CHIP_UNITS), jnp.bfloat16),
+            pltpu.VMEM((SLICES, BLK, WIDTH), jnp.bfloat16),
+            pltpu.VMEM((2, OWN, per, BLK, WIDTH), jnp.bfloat16),
             pltpu.SemaphoreType.DMA((OWN,)),
             pltpu.SemaphoreType.DMA((2, 2)),
+            pltpu.SemaphoreType.DMA((2, 2, STEPS)),
+            pltpu.SemaphoreType.DMA((tile_count - OWN,)),
+            pltpu.SemaphoreType.DMA((2, OWN)),
         ],
         compiler_params=params(HID_MIB),
         cost_estimate=cost(HID_COST * 2 * ROWS * D * 2 * UNITS, 24 * MIB),
-        name="hidden",
-    )(picked, *srcs, w_in, w_in_other)
+        name="forward",
+    )(picked, tiles, empty, *srcs, w_in, w_in_other, w_out, w_out_other, gate)
 
 
 def back_body(
-    feats, tiles, dy, oa, ob, ia, ib, act, der, gate, out, dgate,
+    feats, dy, oa, ob, ia, ib, act, der, gate, out, dgate,
     dy_v, g_v, o_v, i_v, dh, dy_sem, o_sems, i_sems,
 ):
     step = pl.program_id(0)
@@ -221,13 +309,11 @@
         wait(in_weights(i))
         r = lax.dot_general(dh[...], i_v[i % 2], dims, preferred_element_type=jnp.float32)
         r = r.astype(out.dtype)
-        out[...] = jnp.zeros_like(out)
-        for s in range(OWN):
-            for f in range(out.shape[1]):
-                out[tiles[s], f] = r[s * BLK : (s + 1) * BLK, f * WIDTH : (f + 1) * WIDTH]
-
-
-def back(tiles, dy, w_out, w_out_other, w_in, w_in_other, act, der, gate, tile_count):
+        for f in range(out.shape[0]):
+            out[f] = r[:, f * WIDTH : (f + 1) * WIDTH]
+
+
+def back(dy, w_out, w_out_other, w_in, w_in_other, act, der, gate):
     per = 4
     feats = per * WIDTH
     h_spec = pl.BlockSpec((ROWS, GROUP), lambda i: (0, jnp.minimum(i, STEPS - 1)))
@@ -236,14 +322,12 @@
         functools.partial(back_body, feats),
         grid=(STEPS + SLICES // per,),
         out_shape=(
-            jax.ShapeDtypeStruct((tile_count, SLICES, BLK, WIDTH), jnp.bfloat16),
+            jax.ShapeDtypeStruct((SLICES, ROWS, WIDTH), jnp.bfloat16),
             jax.ShapeDtypeStruct((ROWS, 1), jnp.float32),
         ),
-        in_specs=[SMEM, ANY, ANY, ANY, ANY, ANY, h_spec, h_spec, g_spec],
+        in_specs=[ANY, ANY, ANY, ANY, ANY, h_spec, h_spec, g_spec],
         out_specs=(
-            pl.BlockSpec(
-                (tile_count, per, BLK, WIDTH), lambda i: (0, jnp.maximum(i - STEPS, 0), 0, 0)
-            ),
+            pl.BlockSpec((per, ROWS, WIDTH), lambda i: (jnp.maximum(i - STEPS, 0), 0, 0)),
             g_spec,
         ),
         scratch_shapes=[
@@ -257,64 +341,9 @@
             pltpu.SemaphoreType.DMA((2, 2, STEPS)),
         ],
         compiler_params=params(BACK_MIB),
-        cost_estimate=cost(4 * ROWS * D * 2 * UNITS, 50 * MIB),
+        cost_estimate=cost(BACK_COST * 4 * ROWS * D * 2 * UNITS, 50 * MIB),
         name="back",
-    )(tiles, dy, w_out, w_out_other, w_in, w_in_other, act, der, gate)
-
-
-def rows_out_body(feats, act, wa, wb, gate, out, w_v, sems):
-    step = pl.program_id(0)
-
-    def weights(i):
-        cols = pl.ds(pl.multiple_of(i * feats, feats), feats)
-        slot = i % 2
-        return [
-            pltpu.make_async_copy(
-                w.at[pl.ds(j * HALF, HALF), cols],
-                w_v.at[slot, pl.ds(j * GROUP + k * HALF, HALF), :],
-                sems.at[slot, k, j],
-            )
-            for k, w in enumerate((wa, wb))
-            for j in range(STEPS)
-        ]
-
-    @pl.when(step == 0)
-    def _():
-        start(weights(0))
-
-    @pl.when(step + 1 < pl.num_programs(0))
-    def _():
-        start(weights(step + 1))
-
-    wait(weights(step))
-    o = jnp.dot(act[...], w_v[step % 2], preferred_element_type=jnp.float32)
-    o = (o * gate[...]).astype(out.dtype)
-    for f in range(out.shape[0]):
-        out[f] = o[:, f * WIDTH : (f + 1) * WIDTH]
-
-
-def rows_out(act, w_out, w_out_other, gate):
-    per = 4
-    feats = per * WIDTH
-    return pl.pallas_call(
-        functools.partial(rows_out_body, feats),
-        grid=(SLICES // per,),
-        out_shape=jax.ShapeDtypeStruct((SLICES, ROWS, WIDTH), jnp.bfloat16),
-        in_specs=[
-            pl.BlockSpec((ROWS, CHIP_UNITS), lambda i: (0, 0)),
-            ANY,
-            ANY,
-            pl.BlockSpec((ROWS, 1), lambda i: (0, 0)),
-        ],
-        out_specs=pl.BlockSpec((per, ROWS, WIDTH), lambda i: (i, 0, 0)),
-        scratch_shapes=[
-            pltpu.VMEM((2, CHIP_UNITS, feats), jnp.bfloat16),
-            pltpu.SemaphoreType.DMA((2, 2, STEPS)),
-        ],
-        compiler_params=params(OUT_MIB),
-        cost_estimate=cost(2 * ROWS * D * 2 * UNITS, 21 * MIB),
-        name="rows_out",
-    )(act, w_out, w_out_other, gate)
+    )(dy, w_out, w_out_other, w_in, w_in_other, act, der, gate)
 
 
 def merge_body(count, ids, parts, out, total):
@@ -388,14 +417,20 @@
     own_rows = own_of(slot_tile * blocks + slot_block)
     own_places = own_of(slot_place * blocks + slot_block)
     own_tiles = lax.dynamic_index_in_dim(own_of(slot_tile), my_expert, 0, False)
+    others = jnp.all(own_tiles[:, None] != order, axis=0)
+    at = jnp.sum(((order[:, None] > order) & others).astype(jnp.int32), axis=1)
+    free = jnp.arange(tile_count - OWN, dtype=jnp.int32)[:, None]
+    empty = jnp.sum(jnp.where(others & (at == free), order, 0), axis=1)
     my_places = lax.dynamic_index_in_dim(own_places, my_expert, 0, False)
-    my_rows = lax.dynamic_index_in_dim(own_rows, my_expert, 0, False)
 
     gate_mine = lax.dynamic_index_in_dim(gates, my_expert, 1, False).reshape(blocks, BLK)
-    gate_all = lax.all_gather(gate_mine, "tok", tiled=True)
-    gate = jnp.take(gate_all, my_rows, axis=0, mode="clip").reshape(ROWS, 1)
+    gate_near = jnp.concatenate([gate_mine] + [along_z(gate_mine, k, chips) for k in (1, 2, 3)])
+    gate_all = jnp.concatenate([gate_near, other_core(gate_near, chips)])
+    gate = jnp.take(gate_all, my_places, axis=0, mode="clip").reshape(ROWS, 1)
     places = my_places // blocks
-    x_mine, gate, places, own_tiles = lax.optimization_barrier((x_mine, gate, places, own_tiles))
+    x_mine, gate, places, own_tiles, empty = lax.optimization_barrier(
+        (x_mine, gate, places, own_tiles, empty)
+    )
     above, below = along_z(x_mine, 1, chips), along_z(x_mine, 3, chips)
     far = [along_z(above[:PART], 1, chips), along_z(below[PART:], 3, chips)]
     x_near = [x_mine, above, below, *far]
@@ -405,21 +440,19 @@
     w_in_other = other_core(w_in, chips)
     w_out_other = other_core(w_out, chips)
 
-    act, der = hidden(places, x_all, w_in, w_in_other)
-    dx_all, dgate = back(
-        own_tiles, dy, w_out, w_out_other, w_in, w_in_other, act, der, gate, tile_count
+    act, der, out_all = forward(
+        places, own_tiles, empty, x_all, w_in, w_in_other, w_out, w_out_other, gate, tile_count
     )
-    out_rows = rows_out(act, w_out, w_out_other, gate)
-
-    dx = lax.psum_scatter(dx_all, "tok", scatter_dimension=0)
-
-    parts = exchange(out_rows).reshape(experts * OWN, BLK, WIDTH)
-    mixed_all = merge(parts, own_rows.reshape(-1), tile_count * blocks)
-    mixed = lax.psum_scatter(
-        mixed_all.reshape(tile_count, blocks * BLK, WIDTH), "tok", scatter_dimension=0
+    dx_rows, dgate = back(dy, w_out, w_out_other, w_in, w_in_other, act, der, gate)
+
+    out_mine = lax.psum_scatter(out_all, "tok", scatter_dimension=0)
+    parts = exchange(dx_rows).reshape(experts * OWN, BLK, WIDTH)
+    grad_all = merge(parts, own_rows.reshape(-1), tile_count * blocks)
+    d_tokens = lax.psum_scatter(
+        grad_all.reshape(tile_count, blocks * BLK, WIDTH), "tok", scatter_dimension=0
     )
-    dx = exchange(dx)
-    d_tokens = merge(dx, tile_picks, blocks)
+    out_mine = exchange(out_mine)
+    mixed = merge(out_mine, tile_picks, blocks)
 
     dgate = dgate.reshape(OWN, BLK)
     dgate += sum(along_z(dgate, k, chips) for k in (1, 2, 3))
@@ -427,7 +460,7 @@
     low = jnp.where(core == 0, dgate, theirs)
     high = jnp.where(core == 0, theirs, dgate)
     both = jnp.concatenate([low, high])
-    both, _ = lax.optimization_barrier((both, dx))
+    both, _ = lax.optimization_barrier((both, out_mine))
     grads = exchange(jnp.broadcast_to(both[None], (experts, CAP, BLK)))
     taken = lax.dynamic_index_in_dim(chosen, my_tile, 0, False)
     here = (slot_tile == my_tile) & taken[:, None]
@@ -435,8 +468,8 @@
     at_block = tile_picks[None, :] == jnp.arange(blocks, dtype=jnp.int32)[:, None]
     d_gates = jnp.where(at_block[:, None, :], mine.T[None], 0.0)
     return (
-        mixed,
-        d_tokens.reshape(blocks * BLK, WIDTH),
+        mixed.reshape(blocks * BLK, WIDTH),
+        d_tokens,
         d_gates.reshape(blocks * BLK, experts),
     )
 

time: 240 us -> 229 us (0.954)
  blocking collectives: 67.4 us -> 44.9 us
  waiting for transfers between devices: 44.8 us -> 59.9 us
  local copies, waits for them, and re-layouts: 9.69 us -> 5.26 us
  Pallas kernels: 67.4 us -> 65 us
    all_gather x1 -> x0, blocking collectives: 20.4 us -> none  [on_device(): gate_all = lax.all_gather(gate_mine, 'tok', tiled=True)]
    all_to_all x4, waiting for transfers between devices: 10.6 us -> 20.6 us  [exchange(): return lax.all_to_all(value, 'exp', split_axis=0, concat_axis=0, tiled=True)]
    ppermute x7 -> x10, waiting for transfers between devices: 25.2 us -> 30.5 us  [along_z(): return lax.ppermute(value, 'tok', pairs)]
    reduce_scatter x2, waiting for transfers between devices: 4.76 us -> 0.6 us  [the longest x1 0.58 us: on_device(): lax.psum_scatter(grad_all.reshape(tile_count, blocks * BLK, WIDTH), 'tok'...]
    ppermute x8 -> x9, waiting for transfers between devices: 3.55 us -> 7.48 us  [other_core(): return lax.ppermute(value, 'tok', [(i, i ^ 1) for i in range(2 * chips)])]
    ppermute x7 -> x10, starting transfers between devices: 11.2 us -> 14.1 us  [along_z(): return lax.ppermute(value, 'tok', pairs)]
    pallas_call x2 -> x1, Pallas kernels: 26.8 us -> 25.1 us  [forward(): pl.pallas_call(functools.partial(forward_body, len(srcs), feats), grid=(S...]
  transfers between devices with their start and end apart: 22 -> 26, of which waited for: 12 -> 12; matrix products, arithmetic and copies ran while one was open for 4% -> 3% of each run, Pallas kernels for 18% -> 29%
where the time goes in v4:
time: 229 us; the launch traced here: 228 us
  Pallas kernels  65 us (28%)
  waiting for transfers between devices  59.9 us (26%)
  blocking collectives  44.9 us (20%)
  starting transfers between devices  35.7 us (16%)
  between operations  14.2 us (6%)
  local copies, waits for them, and re-layouts  5.26 us (2%)
  other arithmetic  3.13 us (1%)
    all_to_all x1, blocking collectives, exchange(): return lax.all_to_all(value, 'exp', split_axis=0, concat_axis=0, tiled=True)  44.9 us
    ppermute x10, waiting for transfers between devices, along_z(): return lax.ppermute(value, 'tok', pairs)  30.5 us
    pallas_call x1, Pallas kernels, forward(): pl.pallas_call(functools.partial(forward_body, len(srcs), feats), grid=(S...  25.1 us
    pallas_call x1, Pallas kernels, back(): pl.pallas_call(functools.partial(back_body, feats), grid=(STEPS + SLICES...  23.9 us
    all_to_all x4, waiting for transfers between devices, exchange(): return lax.all_to_all(value, 'exp', split_axis=0, concat_axis=0, tiled=True)  20.6 us
    all_to_all x4, starting transfers between devices, exchange(): return lax.all_to_all(value, 'exp', split_axis=0, concat_axis=0, tiled=True)  20.1 us
    ppermute x10, starting transfers between devices, along_z(): return lax.ppermute(value, 'tok', pairs)  14.1 us
    pallas_call x2, Pallas kernels, pick_blocks(): pl.pallas_call(functools.partial(pick_body, count), out_shape=jax.ShapeDt...  8.06 us
  transfers between devices with their start and end apart: 26, of which 12 were waited for; matrix products, arithmetic and copies ran while one was open for 3% of the time, Pallas kernels for 29%

profile of v4, /device:TPU:0, one launch (start us, length us, event | category | flops | bytes accessed | tf_op | source)
XLA Modules:
  0.0 228.0 jit_solution(16125420454802631964)
XLA Ops:
  7.2 0.7 all-gather.2.cloned.1.call-update
  8.5 4.2 %collective-permute-start = (f32[8,128]{1,0:T(8,128)S(1)}, f32[8,128]{1,0:T(8,128)S(1)}, u32[]{:S(2)}, u32[]{:S(2)}) collective-permute-start(f32[8,128]{1,0:T(8,128)S(1)} %bitcast.40), channel_id=1, source_target_pairs={{32,0},{48,16},{64,32},{80,48},{96,64},{112,80},{0,96},{16,112},{3... | collective-permute-start | bytes 12296 | tf_op jit(solution)/shard_map/ppermute | solution.py:382
  12.7 1.3 collective-permute-start.2
  14.0 1.2 broadcast_minimum_fusion
  15.2 3.3 %pick_blocks.2 = bf16[16,128,256]{2,1,0:T(8,128)(2,1)} custom-call(s32[16]{0:T(128)} %get-tuple-element.27.ids, bf16[8,128,256]{2,1,0:T(8,128)(2,1)} %bitcast.35), custom_call_target="tpu_custom_call" | custom-call | bytes 2097152 | tf_op jit(solution)/shard_map/pick_blocks/pallas_call | solution.py:49
  18.5 7.0 %all-to-all-start = ((bf16[16,128,256]{2,1,0:T(8,128)(2,1)}), bf16[16,128,256]{2,1,0:T(8,128)(2,1)S(1)}, u32[]{:S(2)}, u32[]{:S(2)}) async-start(bf16[16,128,256]{2,1,0:T(8,128)(2,1)} %pick_blocks.2), calls=%async_computation | async-start | bytes 2097152 | tf_op jit(solution)/shard_map/all_to_all | solution.py:375
  27.9 5.3 %collective-permute-done.3 = f32[32,128]{1,0:T(8,128)S(1)} collective-permute-done((f32[32,128]{1,0:T(8,128)S(1)}, f32[32,128]{1,0:T(8,128)S(1)}, u32[]{:S(2)}, u32[]{:S(2)}) %collective-permute-start.3) | collective-permute-done | bytes 16416 | tf_op jit(solution)/shard_map/ppermute | solution.py:386
  33.8 8.5 %all-to-all-done.refs_0_ = bf16[16,128,256]{2,1,0:T(8,128)(2,1)S(1)} async-done(((bf16[16,128,256]{2,1,0:T(8,128)(2,1)}), bf16[16,128,256]{2,1,0:T(8,128)(2,1)S(1)}, u32[]{:S(2)}, u32[]{:S(2)}) %all-to-all-start) | async-done | bytes 1048608 | tf_op jit(solution)/shard_map/all_to_all | solution.py:375
  42.3 2.7 %collective-permute-start.4 = (bf16[16,128,256]{2,1,0:T(8,128)(2,1)S(1)}, bf16[16,128,256]{2,1,0:T(8,128)(2,1)S(1)}, u32[]{:S(2)}, u32[]{:S(2)}) collective-permute-start(bf16[16,128,256]{2,1,0:T(8,128)(2,1)S(1)} %all-to-all-done.refs_0_), channel_id=1, source_target_pairs={{32,0},{48,16},{64,32},{80,48},{96,64},{112,80},{0,96},{16,112},{3... | collective-permute-start | bytes 3145736 | tf_op jit(solution)/shard_map/ppermute | solution.py:382
  45.7 4.8 %pick_blocks.3 = bf16[48,128,256]{2,1,0:T(8,128)(2,1)} custom-call(s32[48]{0:T(128)} %reshape.111.ids, bf16[64,128,256]{2,1,0:T(8,128)(2,1)} %all-gather.2.cloned.1.call-done.src), custom_call_target="tpu_custom_call" | custom-call | bytes 6291456 | tf_op jit(solution)/shard_map/pick_blocks/pallas_call | solution.py:49
  50.5 5.8 %all-to-all-start.2 = ((bf16[16,384,256]{2,1,0:T(8,128)(2,1)}), bf16[16,384,256]{2,1,0:T(8,128)(2,1)}, u32[]{:S(2)}, u32[]{:S(2)}) async-start(bf16[16,384,256]{2,1,0:T(8,128)(2,1)} %bitcast.32), calls=%async_computation.3 | async-start | bytes 6291456 | tf_op jit(solution)/shard_map/all_to_all | solution.py:375
  56.3 9.7 %collective-permute-done.4.refs_1_ = bf16[16,128,256]{2,1,0:T(8,128)(2,1)S(1)} collective-permute-done((bf16[16,128,256]{2,1,0:T(8,128)(2,1)S(1)}, bf16[16,128,256]{2,1,0:T(8,128)(2,1)S(1)}, u32[]{:S(2)}, u32[]{:S(2)}) %collective-permute-start.4) | collective-permute-done | bytes 1048608 | tf_op jit(solution)/shard_map/ppermute | solution.py:382
  66.0 2.6 %collective-permute-start.6 = (bf16[8,128,256]{2,1,0:T(8,128)(2,1)S(1)}, bf16[8,128,256]{2,1,0:T(8,128)(2,1)}, u32[]{:S(2)}, u32[]{:S(2)}) collective-permute-start(bf16[8,128,256]{2,1,0:T(8,128)(2,1)S(1)} %slice.10), channel_id=1, source_target_pairs={{32,0},{48,16},{64,32},{80,48},{96,64},{112,80},{0,96},{16,112},{3... | collective-permute-start | bytes 1572872 | tf_op jit(solution)/shard_map/ppermute | solution.py:382
  68.8 8.1 %collective-permute-done.6.refs_3_ = bf16[8,128,256]{2,1,0:T(8,128)(2,1)} collective-permute-done((bf16[8,128,256]{2,1,0:T(8,128)(2,1)S(1)}, bf16[8,128,256]{2,1,0:T(8,128)(2,1)}, u32[]{:S(2)}, u32[]{:S(2)}) %collective-permute-start.6) | collective-permute-done | bytes 524320 | tf_op jit(solution)/shard_map/ppermute | solution.py:382
  76.9 7.5 %collective-permute-done.7.refs_4_ = bf16[8,128,256]{2,1,0:T(8,128)(2,1)} collective-permute-done((bf16[8,128,256]{2,1,0:T(8,128)(2,1)S(1)}, bf16[8,128,256]{2,1,0:T(8,128)(2,1)}, u32[]{:S(2)}, u32[]{:S(2)}) %collective-permute-start.7) | collective-permute-done | bytes 524320 | tf_op jit(solution)/shard_map/ppermute | solution.py:382
  84.4 1.0 copy-done.14
  85.9 0.8 copy.19.refs_14_.gate
  86.7 1.0 collective-permute-done.12.refs_9_
  87.8 25.1 %forward.1 = (bf16[384,2048]{1,0:T(8,128)(2,1)}, f32[384,2048]{1,0:T(8,128)}, bf16[8,16,128,256]{3,2,1,0:T(8,128)(2,1)}) custom-call(s32[3]{0:T(128)} %and_select_fusion.picked, s32[3]{0:T(128)} %copy-done.13, s32[5]{0:T(128)} %select_reduce_fusion.3.empty, bf16[16,128,256]{2,1,0:T(8,128)(2,1)} %copy-done.3, bf16[16,128,256]{2,1,0:T(8,128)(2,1)} %copy-done.4, ...), custom_call_target="tpu_custom_call" | custom-call | flops 12884901888 | bytes 25165824 | tf_op jit(solution)/shard_map/forward/pallas_call | solution.py:209
  113.1 23.9 %back.1 = (bf16[16,384,256]{2,1,0:T(8,128)(2,1)}, f32[384,1]{1,0:T(8,128)}) custom-call(bf16[16,384,256]{2,1,0:T(8,128)(2,1)} %all-to-all-done.2.dy, bf16[1024,4096]{1,0:T(8,128)(2,1)} %bitcast.56, bf16[1024,4096]{1,0:T(8,128)(2,1)} %collective-permute-done.14.refs_13_.ob, bf16[4096,1024]{1,0:T(8,128)(2,1)} %bitcast.53, ...), custom_call_target="tpu_custom_call" | custom-call | flops 206158430208 | bytes 52428800 | tf_op jit(solution)/shard_map/back/pallas_call | solution.py:321
  137.1 44.9 %all_to_all.25 = bf16[16,384,256]{2,1,0:T(8,128)(2,1)} all-to-all(bf16[16,384,256]{2,1,0:T(8,128)(2,1)} %get-tuple-element.22), channel_id=1, replica_groups=mesh['tok'=8,'exp'=16] {'exp'}, dimensions={0} | all-to-all | bytes 6291456 | tf_op jit(solution)/shard_map/all_to_all | solution.py:375
  182.0 5.5 %merge.3 = bf16[64,128,256]{2,1,0:T(8,128)(2,1)} custom-call(s32[48]{0:T(128)} %reshape.111.ids, bf16[48,128,256]{2,1,0:T(8,128)(2,1)} %bitcast.33), custom_call_target="tpu_custom_call" | custom-call | bytes 14680064 | tf_op jit(solution)/shard_map/merge/pallas_call | solution.py:362
  187.5 3.8 %all-to-all-start.1 = ((bf16[16,128,256]{2,1,0:T(8,128)(2,1)}), bf16[16,128,256]{2,1,0:T(8,128)(2,1)S(1)}, u32[]{:S(2)}, u32[]{:S(2)}) async-start(bf16[16,128,256]{2,1,0:T(8,128)(2,1)} %bitcast.34), calls=%async_computation.2 | async-start | bytes 2097152 | tf_op jit(solution)/shard_map/all_to_all | solution.py:375
  191.6 3.2 %collective-permute-start.15 = (f32[3,128]{1,0:T(4,128)S(1)}, f32[3,128]{1,0:T(4,128)S(1)}, u32[]{:S(2)}, u32[]{:S(2)}) collective-permute-start(f32[3,128]{1,0:T(4,128)S(1)} %bitcast.47), channel_id=1, source_target_pairs={{32,0},{48,16},{64,32},{80,48},{96,64},{112,80},{0,96},{16,112},{3... | collective-permute-start | bytes 4616 | tf_op jit(solution)/shard_map/ppermute | solution.py:382
  194.8 1.5 collective-permute-done.17
  196.4 3.6 %collective-permute-done.16 = f32[3,128]{1,0:T(4,128)S(1)} collective-permute-done((f32[3,128]{1,0:T(4,128)S(1)}, f32[3,128]{1,0:T(4,128)S(1)}, u32[]{:S(2)}, u32[]{:S(2)}) %collective-permute-start.16) | collective-permute-done | bytes 1568 | tf_op jit(solution)/shard_map/ppermute | solution.py:382
  200.0 1.1 collective-permute-done.18
  201.2 7.1 %all-to-all-done.1.parts = bf16[16,128,256]{2,1,0:T(8,128)(2,1)S(1)} async-done(((bf16[16,128,256]{2,1,0:T(8,128)(2,1)}), bf16[16,128,256]{2,1,0:T(8,128)(2,1)S(1)}, u32[]{:S(2)}, u32[]{:S(2)}) %all-to-all-start.1) | async-done | bytes 1048608 | tf_op jit(solution)/shard_map/all_to_all | solution.py:375
  208.3 0.7 broadcast_in_dim.103
  209.0 3.5 %all-to-all-start.4 = ((f32[16,6,128]{2,1,0:T(8,128)}), f32[16,6,128]{2,1,0:T(8,128)S(1)}, u32[]{:S(2)}, u32[]{:S(2)}) async-start(f32[16,6,128]{2,1,0:T(8,128)} %broadcast_in_dim.103), calls=%async_computation.6 | async-start | bytes 131072 | tf_op jit(solution)/shard_map/all_to_all | solution.py:375
  212.7 2.4 %merge.2 = bf16[8,128,256]{2,1,0:T(8,128)(2,1)} custom-call(s32[16]{0:T(128)} %get-tuple-element.28.ids, bf16[16,128,256]{2,1,0:T(8,128)(2,1)} %copy-done.2), custom_call_target="tpu_custom_call" | custom-call | bytes 3145728 | tf_op jit(solution)/shard_map/merge/pallas_call | solution.py:362
  215.1 5.0 %all-to-all-done.4 = f32[16,6,128]{2,1,0:T(8,128)S(1)} async-done(((f32[16,6,128]{2,1,0:T(8,128)}), f32[16,6,128]{2,1,0:T(8,128)S(1)}, u32[]{:S(2)}, u32[]{:S(2)}) %all-to-all-start.4) | async-done | bytes 49184 | tf_op jit(solution)/shard_map/all_to_all | solution.py:375
  (102 shorter events, 7.0 us)
Async XLA Ops:
  7.2 38.5 %all-gather.2.cloned.1.call-start = ((), (), s32[]{:S(2)}) async-start(), calls=%async_computation.8 | async-start | bytes 4718592 | tf_op jit(solution)/shard_map/all_gather | solution.py:399
  7.9 79.8 %collective-permute-start.13 = (bf16[4096,1024]{1,0:T(8,128)(2,1)}, bf16[4096,1024]{1,0:T(8,128)(2,1)}, u32[]{:S(2)}, u32[]{:S(2)}) collective-permute-start(bf16[4096,1024]{1,0:T(8,128)(2,1)} %bitcast.51), channel_id=1, source_target_pairs={{0,16},{16,0},{32,48},{48,32},{64,80},{80,64},{96,112},{112,96},{1... | collective-permute-start | bytes 25165832 | tf_op jit(solution)/shard_map/ppermute | solution.py:386
  8.0 79.7 %collective-permute-start.14 = (bf16[1024,4096]{1,0:T(8,128)(2,1)}, bf16[1024,4096]{1,0:T(8,128)(2,1)}, u32[]{:S(2)}, u32[]{:S(2)}) collective-permute-start(bf16[1024,4096]{1,0:T(8,128)(2,1)} %bitcast.54), channel_id=1, source_target_pairs={{0,16},{16,0},{32,48},{48,32},{64,80},{80,64},{96,112},{112,96},{1... | collective-permute-start | bytes 25165832 | tf_op jit(solution)/shard_map/ppermute | solution.py:386
  8.5 19.2 %collective-permute-start = (f32[8,128]{1,0:T(8,128)S(1)}, f32[8,128]{1,0:T(8,128)S(1)}, u32[]{:S(2)}, u32[]{:S(2)}) collective-permute-start(f32[8,128]{1,0:T(8,128)S(1)} %bitcast.40), channel_id=1, source_target_pairs={{32,0},{48,16},{64,32},{80,48},{96,64},{112,80},{0,96},{16,112},{3... | collective-permute-start | bytes 12296 | tf_op jit(solution)/shard_map/ppermute | solution.py:382
  12.7 15.0 %collective-permute-start.1 = (f32[8,128]{1,0:T(8,128)S(1)}, f32[8,128]{1,0:T(8,128)S(1)}, u32[]{:S(2)}, u32[]{:S(2)}) collective-permute-start(f32[8,128]{1,0:T(8,128)S(1)} %bitcast.41), channel_id=1, source_target_pairs={{64,0},{80,16},{96,32},{112,48},{0,64},{16,80},{32,96},{48,112},{6... | collective-permute-start | bytes 12296 | tf_op jit(solution)/shard_map/ppermute | solution.py:382
  12.7 15.0 %collective-permute-start.2 = (f32[8,128]{1,0:T(8,128)S(1)}, f32[8,128]{1,0:T(8,128)S(1)}, u32[]{:S(2)}, u32[]{:S(2)}) collective-permute-start(f32[8,128]{1,0:T(8,128)S(1)} %bitcast.42), channel_id=1, source_target_pairs={{96,0},{112,16},{0,32},{16,48},{32,64},{48,80},{64,96},{80,112},{9... | collective-permute-start | bytes 12296 | tf_op jit(solution)/shard_map/ppermute | solution.py:382
  18.5 23.8 %all-to-all-start = ((bf16[16,128,256]{2,1,0:T(8,128)(2,1)}), bf16[16,128,256]{2,1,0:T(8,128)(2,1)S(1)}, u32[]{:S(2)}, u32[]{:S(2)}) async-start(bf16[16,128,256]{2,1,0:T(8,128)(2,1)} %pick_blocks.2), calls=%async_computation | async-start | bytes 2097152 | tf_op jit(solution)/shard_map/all_to_all | solution.py:375
  25.8 24.7 %copy-start.7 = (s32[16,6]{0,1:T(8,128)}, s32[16,6]{0,1:T(8,128)S(1)}, u32[]{:S(2)}) copy-start(s32[16,6]{0,1:T(8,128)S(1)} %get-tuple-element.25) | copy-start | bytes 1156
  26.2 24.3 %copy-start.13 = (s32[3]{0:T(128)}, s32[3]{0:T(128)S(1)}, u32[]{:S(2)}) copy-start(s32[3]{0:T(128)S(1)} %dynamic-slice_reduce_fusion.tiles) | copy-start | bytes 40
  27.8 5.4 %collective-permute-start.3 = (f32[32,128]{1,0:T(8,128)S(1)}, f32[32,128]{1,0:T(8,128)S(1)}, u32[]{:S(2)}, u32[]{:S(2)}) collective-permute-start(f32[32,128]{1,0:T(8,128)S(1)} %pad_maximum_fusion), channel_id=1, source_target_pairs={{0,16},{16,0},{32,48},{48,32},{64,80},{80,64},{96,112},{112,96},{1... | collective-permute-start | bytes 49160 | tf_op jit(solution)/shard_map/ppermute | solution.py:386
  42.3 23.7 %collective-permute-start.4 = (bf16[16,128,256]{2,1,0:T(8,128)(2,1)S(1)}, bf16[16,128,256]{2,1,0:T(8,128)(2,1)S(1)}, u32[]{:S(2)}, u32[]{:S(2)}) collective-permute-start(bf16[16,128,256]{2,1,0:T(8,128)(2,1)S(1)} %all-to-all-done.refs_0_), channel_id=1, source_target_pairs={{32,0},{48,16},{64,32},{80,48},{96,64},{112,80},{0,96},{16,112},{3... | collective-permute-start | bytes 3145736 | tf_op jit(solution)/shard_map/ppermute | solution.py:382
  44.9 23.7 %collective-permute-start.5 = (bf16[16,128,256]{2,1,0:T(8,128)(2,1)S(1)}, bf16[16,128,256]{2,1,0:T(8,128)(2,1)S(1)}, u32[]{:S(2)}, u32[]{:S(2)}) collective-permute-start(bf16[16,128,256]{2,1,0:T(8,128)(2,1)S(1)} %all-to-all-done.refs_0_), channel_id=1, source_target_pairs={{96,0},{112,16},{0,32},{16,48},{32,64},{48,80},{64,96},{80,112},{9... | collective-permute-start | bytes 3145736 | tf_op jit(solution)/shard_map/ppermute | solution.py:382
  44.9 23.7 %collective-permute-start.8 = (bf16[16,128,256]{2,1,0:T(8,128)(2,1)S(1)}, bf16[16,128,256]{2,1,0:T(8,128)(2,1)}, u32[]{:S(2)}, u32[]{:S(2)}) collective-permute-start(bf16[16,128,256]{2,1,0:T(8,128)(2,1)S(1)} %all-to-all-done.refs_0_), channel_id=1, source_target_pairs={{0,16},{16,0},{32,48},{48,32},{64,80},{80,64},{96,112},{112,96},{1... | collective-permute-start | bytes 3145736 | tf_op jit(solution)/shard_map/ppermute | solution.py:386
  50.5 62.6 %all-to-all-start.2 = ((bf16[16,384,256]{2,1,0:T(8,128)(2,1)}), bf16[16,384,256]{2,1,0:T(8,128)(2,1)}, u32[]{:S(2)}, u32[]{:S(2)}) async-start(bf16[16,384,256]{2,1,0:T(8,128)(2,1)} %bitcast.32), calls=%async_computation.3 | async-start | bytes 6291456 | tf_op jit(solution)/shard_map/all_to_all | solution.py:375
  56.3 131.3 %reduce-scatter.3.cloned.1.call-start = ((), (), s32[]{:S(2)}) async-start(), calls=%async_computation.7 | async-start | bytes 9437184 | tf_op jit(solution)/shard_map/reduce_scatter | solution.py:448
  66.0 21.8 %copy-start.4 = (bf16[16,128,256]{2,1,0:T(8,128)(2,1)}, bf16[16,128,256]{2,1,0:T(8,128)(2,1)S(1)}, u32[]{:S(2)}) copy-start(bf16[16,128,256]{2,1,0:T(8,128)(2,1)S(1)} %collective-permute-done.4.refs_1_) | copy-start | bytes 3145732
  66.0 10.8 %collective-permute-start.6 = (bf16[8,128,256]{2,1,0:T(8,128)(2,1)S(1)}, bf16[8,128,256]{2,1,0:T(8,128)(2,1)}, u32[]{:S(2)}, u32[]{:S(2)}) collective-permute-start(bf16[8,128,256]{2,1,0:T(8,128)(2,1)S(1)} %slice.10), channel_id=1, source_target_pairs={{32,0},{48,16},{64,32},{80,48},{96,64},{112,80},{0,96},{16,112},{3... | collective-permute-start | bytes 1572872 | tf_op jit(solution)/shard_map/ppermute | solution.py:382
  68.6 19.2 %copy-start.5 = (bf16[16,128,256]{2,1,0:T(8,128)(2,1)}, bf16[16,128,256]{2,1,0:T(8,128)(2,1)S(1)}, u32[]{:S(2)}) copy-start(bf16[16,128,256]{2,1,0:T(8,128)(2,1)S(1)} %collective-permute-done.5.refs_2_) | copy-start | bytes 3145732
  68.6 15.8 %collective-permute-start.9 = (bf16[16,128,256]{2,1,0:T(8,128)(2,1)S(1)}, bf16[16,128,256]{2,1,0:T(8,128)(2,1)S(1)}, u32[]{:S(2)}, u32[]{:S(2)}) collective-permute-start(bf16[16,128,256]{2,1,0:T(8,128)(2,1)S(1)} %collective-permute-done.4.refs_1_), channel_id=1, source_target_pairs={{0,16},{16,0},{32,48},{48,32},{64,80},{80,64},{96,112},{112,96},{1... | collective-permute-start | bytes 3145736 | tf_op jit(solution)/shard_map/ppermute | solution.py:386
  68.7 15.7 %collective-permute-start.7 = (bf16[8,128,256]{2,1,0:T(8,128)(2,1)S(1)}, bf16[8,128,256]{2,1,0:T(8,128)(2,1)}, u32[]{:S(2)}, u32[]{:S(2)}) collective-permute-start(bf16[8,128,256]{2,1,0:T(8,128)(2,1)S(1)} %slice.11), channel_id=1, source_target_pairs={{96,0},{112,16},{0,32},{16,48},{32,64},{48,80},{64,96},{80,112},{9... | collective-permute-start | bytes 1572872 | tf_op jit(solution)/shard_map/ppermute | solution.py:382
  76.8 9.8 %collective-permute-start.10 = (bf16[16,128,256]{2,1,0:T(8,128)(2,1)S(1)}, bf16[16,128,256]{2,1,0:T(8,128)(2,1)S(1)}, u32[]{:S(2)}, u32[]{:S(2)}) collective-permute-start(bf16[16,128,256]{2,1,0:T(8,128)(2,1)S(1)} %collective-permute-done.5.refs_2_), channel_id=1, source_target_pairs={{0,16},{16,0},{32,48},{48,32},{64,80},{80,64},{96,112},{112,96},{1... | collective-permute-start | bytes 3145736 | tf_op jit(solution)/shard_map/ppermute | solution.py:386
  84.4 2.3 %collective-permute-start.11 = (bf16[8,128,256]{2,1,0:T(8,128)(2,1)}, bf16[8,128,256]{2,1,0:T(8,128)(2,1)}, u32[]{:S(2)}, u32[]{:S(2)}) collective-permute-start(bf16[8,128,256]{2,1,0:T(8,128)(2,1)} %collective-permute-done.6.refs_3_), channel_id=1, source_target_pairs={{0,16},{16,0},{32,48},{48,32},{64,80},{80,64},{96,112},{112,96},{1... | collective-permute-start | bytes 1572872 | tf_op jit(solution)/shard_map/ppermute | solution.py:386
  85.4 2.4 %collective-permute-start.12 = (bf16[8,128,256]{2,1,0:T(8,128)(2,1)}, bf16[8,128,256]{2,1,0:T(8,128)(2,1)}, u32[]{:S(2)}, u32[]{:S(2)}) collective-permute-start(bf16[8,128,256]{2,1,0:T(8,128)(2,1)} %collective-permute-done.7.refs_4_), channel_id=1, source_target_pairs={{0,16},{16,0},{32,48},{48,32},{64,80},{80,64},{96,112},{112,96},{1... | collective-permute-start | bytes 1572872 | tf_op jit(solution)/shard_map/ppermute | solution.py:386
  112.9 108.6 %reduce-scatter.5.cloned.1.call-start = ((), (), s32[]{:S(2)}) async-start(), calls=%async_computation.9 | async-start | bytes 4718592 | tf_op jit(solution)/shard_map/reduce_scatter | solution.py:451
  187.5 25.0 %copy-start.12 = (s32[16]{0:T(128)S(1)}, s32[16]{0:T(128)}, u32[]{:S(2)}) copy-start(s32[16]{0:T(128)} %get-tuple-element.28.ids) | copy-start | bytes 196
  187.5 34.0 %copy-start.1 = (f32[1024,16]{0,1:T(8,128)S(1)}, f32[1024,16]{0,1:T(8,128)}, u32[]{:S(2)}) copy-start(f32[1024,16]{0,1:T(8,128)} %param.8) | copy-start | bytes 196612
  187.5 20.8 %all-to-all-start.1 = ((bf16[16,128,256]{2,1,0:T(8,128)(2,1)}), bf16[16,128,256]{2,1,0:T(8,128)(2,1)S(1)}, u32[]{:S(2)}, u32[]{:S(2)}) async-start(bf16[16,128,256]{2,1,0:T(8,128)(2,1)} %bitcast.34), calls=%async_computation.2 | async-start | bytes 2097152 | tf_op jit(solution)/shard_map/all_to_all | solution.py:375
  191.5 4.9 %collective-permute-start.17 = (f32[3,128]{1,0:T(4,128)S(1)}, f32[3,128]{1,0:T(4,128)S(1)}, u32[]{:S(2)}, u32[]{:S(2)}) collective-permute-start(f32[3,128]{1,0:T(4,128)S(1)} %bitcast.46), channel_id=1, source_target_pairs={{96,0},{112,16},{0,32},{16,48},{32,64},{48,80},{64,96},{80,112},{9... | collective-permute-start | bytes 4616 | tf_op jit(solution)/shard_map/ppermute | solution.py:382
  191.6 4.8 %collective-permute-start.15 = (f32[3,128]{1,0:T(4,128)S(1)}, f32[3,128]{1,0:T(4,128)S(1)}, u32[]{:S(2)}, u32[]{:S(2)}) collective-permute-start(f32[3,128]{1,0:T(4,128)S(1)} %bitcast.47), channel_id=1, source_target_pairs={{32,0},{48,16},{64,32},{80,48},{96,64},{112,80},{0,96},{16,112},{3... | collective-permute-start | bytes 4616 | tf_op jit(solution)/shard_map/ppermute | solution.py:382
  194.8 5.2 %collective-permute-start.16 = (f32[3,128]{1,0:T(4,128)S(1)}, f32[3,128]{1,0:T(4,128)S(1)}, u32[]{:S(2)}, u32[]{:S(2)}) collective-permute-start(f32[3,128]{1,0:T(4,128)S(1)} %bitcast.48), channel_id=1, source_target_pairs={{64,0},{80,16},{96,32},{112,48},{0,64},{16,80},{32,96},{48,112},{6... | collective-permute-start | bytes 4616 | tf_op jit(solution)/shard_map/ppermute | solution.py:382
  200.0 1.2 collective-permute-start.18
  209.0 11.1 %all-to-all-start.4 = ((f32[16,6,128]{2,1,0:T(8,128)}), f32[16,6,128]{2,1,0:T(8,128)S(1)}, u32[]{:S(2)}, u32[]{:S(2)}) async-start(f32[16,6,128]{2,1,0:T(8,128)} %broadcast_in_dim.103), calls=%async_computation.6 | async-start | bytes 131072 | tf_op jit(solution)/shard_map/all_to_all | solution.py:375
  (10 other events, 58.7 us)
Sparse Core Ops, SparseCore 0:
  9.7 34.7 all-gather.1
  113.0 49.0 reduce-scatter.2
  187.6 33.8 reduce-scatter.4

commit v5 on v4

--- a/solution.py
+++ b/solution.py
@@ -58,6 +58,16 @@
     )(ids, src)
 
 
+def as_column(rows):
+    shape = (BLK, BLK)
+    same = lax.broadcasted_iota(jnp.int32, shape, 0) == lax.broadcasted_iota(jnp.int32, shape, 1)
+    parts = [
+        jnp.sum(jnp.where(same, rows[s : s + 1, :], 0.0), axis=1, keepdims=True)
+        for s in range(OWN)
+    ]
+    return jnp.concatenate(parts, axis=0)
+
+
 def start(copies):
     for copy in copies:
         copy.start()
@@ -189,7 +199,7 @@
             wait(results(i - 2))
 
         o = jnp.dot(act_v[...], o_v[i % 2], preferred_element_type=jnp.float32)
-        o = (o * gate[...]).astype(out.dtype)
+        o = (o * as_column(gate[...])).astype(out.dtype)
         for s in range(OWN):
             for f in range(per):
                 r_v[i % 2, s, f] = o[s * BLK : (s + 1) * BLK, f * WIDTH : (f + 1) * WIDTH]
@@ -216,7 +226,7 @@
         ),
         in_specs=[SMEM] * 3
         + [ANY] * (len(srcs) + 4)
-        + [pl.BlockSpec((ROWS, 1), lambda i: (0, 0))],
+        + [pl.BlockSpec((OWN, BLK), lambda i: (0, 0))],
         out_specs=(o_spec, o_spec, ANY),
         scratch_shapes=[
             pltpu.VMEM((OWN, SLICES, BLK, WIDTH), jnp.bfloat16),
@@ -275,7 +285,7 @@
         whole.start()
         start(out_weights(0))
         whole.wait()
-        scale = gate[...]
+        scale = as_column(gate[...])
         for f in range(SLICES):
             g = scale * dy_v[f].astype(jnp.float32)
             g_v[:, f * WIDTH : (f + 1) * WIDTH] = g.astype(g_v.dtype)
@@ -296,7 +306,7 @@
         here = pl.ds(pl.multiple_of(step * GROUP, GROUP), GROUP)
         dh[:, here] = (u * der[...]).astype(dh.dtype)
         total = dgate[...] + jnp.sum(act[...].astype(jnp.float32) * u, axis=1, keepdims=True)
-        dgate[...] = jnp.where(step == STEPS - 1, total / gate[...], total)
+        dgate[...] = jnp.where(step == STEPS - 1, total / as_column(gate[...]), total)
 
     @pl.when(step >= STEPS)
     def _():
@@ -325,7 +335,7 @@
             jax.ShapeDtypeStruct((SLICES, ROWS, WIDTH), jnp.bfloat16),
             jax.ShapeDtypeStruct((ROWS, 1), jnp.float32),
         ),
-        in_specs=[ANY, ANY, ANY, ANY, ANY, h_spec, h_spec, g_spec],
+        in_specs=[ANY] * 5 + [h_spec, h_spec, pl.BlockSpec((OWN, BLK), lambda i: (0, 0))],
         out_specs=(
             pl.BlockSpec((per, ROWS, WIDTH), lambda i: (jnp.maximum(i - STEPS, 0), 0, 0)),
             g_spec,
@@ -424,12 +434,15 @@
     my_places = lax.dynamic_index_in_dim(own_places, my_expert, 0, False)
 
     gate_mine = lax.dynamic_index_in_dim(gates, my_expert, 1, False).reshape(blocks, BLK)
+    gate_mine, _ = lax.optimization_barrier((gate_mine, x_slot))
     gate_near = jnp.concatenate([gate_mine] + [along_z(gate_mine, k, chips) for k in (1, 2, 3)])
     gate_all = jnp.concatenate([gate_near, other_core(gate_near, chips)])
-    gate = jnp.take(gate_all, my_places, axis=0, mode="clip").reshape(ROWS, 1)
+    gate = jnp.take(gate_all, my_places, axis=0, mode="clip")
     places = my_places // blocks
-    x_mine, gate, places, own_tiles, empty = lax.optimization_barrier(
-        (x_mine, gate, places, own_tiles, empty)
+    w_in_other = other_core(w_in, chips)
+    w_out_other = other_core(w_out, chips)
+    x_mine, gate, places, own_tiles, empty, w_in_other, w_out_other = lax.optimization_barrier(
+        (x_mine, gate, places, own_tiles, empty, w_in_other, w_out_other)
     )
     above, below = along_z(x_mine, 1, chips), along_z(x_mine, 3, chips)
     far = [along_z(above[:PART], 1, chips), along_z(below[PART:], 3, chips)]
@@ -437,8 +450,6 @@
     send_dy = pick_blocks(cot_all, own_rows.reshape(-1))
     dy = exchange(send_dy.reshape(experts, ROWS, WIDTH))
     x_all = x_near + [other_core(piece, chips) for piece in x_near]
-    w_in_other = other_core(w_in, chips)
-    w_out_other = other_core(w_out, chips)
 
     act, der, out_all = forward(
         places, own_tiles, empty, x_all, w_in, w_in_other, w_out, w_out_other, gate, tile_count

time: 229 us -> 228 us (level)
  waiting for transfers between devices: 59.9 us -> 51.5 us
  starting transfers between devices: 35.7 us -> 39.7 us
  blocking collectives: 44.9 us -> 47.3 us
    ppermute x10, waiting for transfers between devices: 30.5 us -> 25.7 us  [along_z(): return lax.ppermute(value, 'tok', pairs)]
    all_to_all x4, waiting for transfers between devices: 20.6 us -> 16 us  [exchange(): return lax.all_to_all(value, 'exp', split_axis=0, concat_axis=0, tiled=True)]
    all_gather x1, waiting for transfers between devices: 0.01 us -> 4.17 us  [on_device(): lax.all_gather(cotangent.reshape(blocks, BLK, WIDTH), 'tok', tiled=True)]
    ppermute x9, waiting for transfers between devices: 7.48 us -> 4.54 us  [other_core(): return lax.ppermute(value, 'tok', [(i, i ^ 1) for i in range(2 * chips)])]
    all_to_all x4, starting transfers between devices: 20.1 us -> 23 us  [exchange(): return lax.all_to_all(value, 'exp', split_axis=0, concat_axis=0, tiled=True)]
    all_to_all x1, blocking collectives: 44.9 us -> 47.3 us  [exchange(): return lax.all_to_all(value, 'exp', split_axis=0, concat_axis=0, tiled=True)]
  transfers between devices with their start and end apart: 26 -> 26, of which waited for: 12 -> 13; matrix products, arithmetic and copies ran while one was open for 3% -> 3% of each run, Pallas kernels for 29% -> 29%
where the time goes in v5:
time: 228 us
  Pallas kernels  64.9 us (28%)
  waiting for transfers between devices  51.5 us (23%)
  blocking collectives  47.3 us (21%)
  starting transfers between devices  39.7 us (17%)
  between operations  14.1 us (6%)
  local copies, waits for them, and re-layouts  6.79 us (3%)
  other arithmetic  3.31 us (1%)
    all_to_all x1, blocking collectives, exchange(): return lax.all_to_all(value, 'exp', split_axis=0, concat_axis=0, tiled=True)  47.3 us
    ppermute x10, waiting for transfers between devices, along_z(): return lax.ppermute(value, 'tok', pairs)  25.7 us
    pallas_call x1, Pallas kernels, forward(): pl.pallas_call(functools.partial(forward_body, len(srcs), feats), grid=(S...  25 us
    pallas_call x1, Pallas kernels, back(): pl.pallas_call(functools.partial(back_body, feats), grid=(STEPS + SLICES...  24 us
    all_to_all x4, starting transfers between devices, exchange(): return lax.all_to_all(value, 'exp', split_axis=0, concat_axis=0, tiled=True)  23 us
    all_to_all x4, waiting for transfers between devices, exchange(): return lax.all_to_all(value, 'exp', split_axis=0, concat_axis=0, tiled=True)  16 us
    ppermute x10, starting transfers between devices, along_z(): return lax.ppermute(value, 'tok', pairs)  15.1 us
    pallas_call x2, Pallas kernels, pick_blocks(): pl.pallas_call(functools.partial(pick_body, count), out_shape=jax.ShapeDt...  7.94 us
  transfers between devices with their start and end apart: 26, of which 13 were waited for; matrix products, arithmetic and copies ran while one was open for 3% of the time, Pallas kernels for 29%

profile of v5, /device:TPU:0, one launch (start us, length us, event | category | flops | bytes accessed | tf_op | source)
XLA Modules:
  0.0 227.6 jit_solution(9278257085176120789)
XLA Ops:
  7.9 1.3 broadcast_minimum_fusion
  9.2 3.2 %pick_blocks.2 = bf16[16,128,256]{2,1,0:T(8,128)(2,1)} custom-call(s32[16]{0:T(128)} %get-tuple-element.33.ids, bf16[8,128,256]{2,1,0:T(8,128)(2,1)} %bitcast.29), custom_call_target="tpu_custom_call" | custom-call | bytes 2097152 | tf_op jit(solution)/shard_map/pick_blocks/pallas_call | solution.py:49
  12.4 7.1 %all-to-all-start = ((bf16[16,128,256]{2,1,0:T(8,128)(2,1)}), bf16[16,128,256]{2,1,0:T(8,128)(2,1)S(1)}, u32[]{:S(2)}, u32[]{:S(2)}) async-start(bf16[16,128,256]{2,1,0:T(8,128)(2,1)} %pick_blocks.2), calls=%async_computation | async-start | bytes 2097152 | tf_op jit(solution)/shard_map/all_to_all | solution.py:385
  19.6 4.3 %collective-permute-start = (f32[8,128]{1,0:T(8,128)S(1)}, f32[8,128]{1,0:T(8,128)S(1)}, u32[]{:S(2)}, u32[]{:S(2)}) collective-permute-start(f32[8,128]{1,0:T(8,128)S(1)} %bitcast.34), channel_id=1, source_target_pairs={{32,0},{48,16},{64,32},{80,48},{96,64},{112,80},{0,96},{16,112},{3... | collective-permute-start | bytes 12296 | tf_op jit(solution)/shard_map/ppermute | solution.py:392
  23.9 1.3 collective-permute-start.2
  27.5 1.6 collective-permute-done.1
  29.1 3.4 %collective-permute-done.3 = f32[32,128]{1,0:T(8,128)S(1)} collective-permute-done((f32[32,128]{1,0:T(8,128)S(1)}, f32[32,128]{1,0:T(8,128)S(1)}, u32[]{:S(2)}, u32[]{:S(2)}) %collective-permute-start.3) | collective-permute-done | bytes 16416 | tf_op jit(solution)/shard_map/ppermute | solution.py:396
  32.5 1.1 gather_fusion
  33.6 4.0 %all-to-all-done.refs_0_ = bf16[16,128,256]{2,1,0:T(8,128)(2,1)S(1)} async-done(((bf16[16,128,256]{2,1,0:T(8,128)(2,1)}), bf16[16,128,256]{2,1,0:T(8,128)(2,1)S(1)}, u32[]{:S(2)}, u32[]{:S(2)}) %all-to-all-start) | async-done | bytes 1048608 | tf_op jit(solution)/shard_map/all_to_all | solution.py:385
  37.7 4.1 %collective-permute-start.6 = (bf16[16,128,256]{2,1,0:T(8,128)(2,1)S(1)}, bf16[16,128,256]{2,1,0:T(8,128)(2,1)S(1)}, u32[]{:S(2)}, u32[]{:S(2)}) collective-permute-start(bf16[16,128,256]{2,1,0:T(8,128)(2,1)S(1)} %all-to-all-done.refs_0_), channel_id=1, source_target_pairs={{32,0},{48,16},{64,32},{80,48},{96,64},{112,80},{0,96},{16,112},{3... | collective-permute-start | bytes 3145736 | tf_op jit(solution)/shard_map/ppermute | solution.py:392
  42.5 4.2 %all-gather.2.cloned.1.call-done.src = bf16[64,128,256]{2,1,0:T(8,128)(2,1)} async-done(((bf16[8,128,256]{2,1,0:T(8,128)(2,1)}), bf16[64,128,256]{2,1,0:T(8,128)(2,1)}) %all-gather.2.cloned.1.call-update) | async-done | bytes 4194320 | tf_op jit(solution)/shard_map/all_gather | solution.py:409
  46.6 4.8 %pick_blocks.3 = bf16[48,128,256]{2,1,0:T(8,128)(2,1)} custom-call(s32[48]{0:T(128)} %reshape.107.ids, bf16[64,128,256]{2,1,0:T(8,128)(2,1)} %all-gather.2.cloned.1.call-done.src), custom_call_target="tpu_custom_call" | custom-call | bytes 6291456 | tf_op jit(solution)/shard_map/pick_blocks/pallas_call | solution.py:49
  51.4 8.5 %all-to-all-start.2 = ((bf16[16,384,256]{2,1,0:T(8,128)(2,1)}), bf16[16,384,256]{2,1,0:T(8,128)(2,1)}, u32[]{:S(2)}, u32[]{:S(2)}) async-start(bf16[16,384,256]{2,1,0:T(8,128)(2,1)} %bitcast.26), calls=%async_computation.3 | async-start | bytes 6291456 | tf_op jit(solution)/shard_map/all_to_all | solution.py:385
  60.1 4.3 %collective-permute-done.6.refs_1_ = bf16[16,128,256]{2,1,0:T(8,128)(2,1)S(1)} collective-permute-done((bf16[16,128,256]{2,1,0:T(8,128)(2,1)S(1)}, bf16[16,128,256]{2,1,0:T(8,128)(2,1)S(1)}, u32[]{:S(2)}, u32[]{:S(2)}) %collective-permute-start.6) | collective-permute-done | bytes 1048608 | tf_op jit(solution)/shard_map/ppermute | solution.py:392
  64.4 1.7 collective-permute-start.8
  67.2 10.1 %collective-permute-done.8.refs_3_ = bf16[8,128,256]{2,1,0:T(8,128)(2,1)S(1)} collective-permute-done((bf16[8,128,256]{2,1,0:T(8,128)(2,1)S(1)}, bf16[8,128,256]{2,1,0:T(8,128)(2,1)S(1)}, u32[]{:S(2)}, u32[]{:S(2)}) %collective-permute-start.8) | collective-permute-done | bytes 524320 | tf_op jit(solution)/shard_map/ppermute | solution.py:392
  77.3 4.6 %collective-permute-done.9.refs_4_ = bf16[8,128,256]{2,1,0:T(8,128)(2,1)S(1)} collective-permute-done((bf16[8,128,256]{2,1,0:T(8,128)(2,1)S(1)}, bf16[8,128,256]{2,1,0:T(8,128)(2,1)S(1)}, u32[]{:S(2)}, u32[]{:S(2)}) %collective-permute-start.9) | collective-permute-done | bytes 524320 | tf_op jit(solution)/shard_map/ppermute | solution.py:392
  81.9 1.0 copy-done.14
  84.7 25.0 %forward.1 = (bf16[384,2048]{1,0:T(8,128)(2,1)}, f32[384,2048]{1,0:T(8,128)}, bf16[8,16,128,256]{3,2,1,0:T(8,128)(2,1)}) custom-call(s32[3]{0:T(128)} %and_select_fusion.picked, s32[3]{0:T(128)} %copy-done.13, s32[5]{0:T(128)} %select_reduce_fusion.3.empty, bf16[16,128,256]{2,1,0:T(8,128)(2,1)} %copy-done.3, bf16[16,128,256]{2,1,0:T(8,128)(2,1)} %copy-done.4, ...), custom_call_target="tpu_custom_call" | custom-call | flops 12884901888 | bytes 25165824 | tf_op jit(solution)/shard_map/forward/pallas_call | solution.py:219
  110.0 24.0 %back.1 = (bf16[16,384,256]{2,1,0:T(8,128)(2,1)}, f32[384,1]{1,0:T(8,128)}) custom-call(bf16[16,384,256]{2,1,0:T(8,128)(2,1)} %all-to-all-done.2.dy, bf16[1024,4096]{1,0:T(8,128)(2,1)} %bitcast.48, bf16[1024,4096]{1,0:T(8,128)(2,1)} %collective-permute-done.5.refs_13_.ob, bf16[4096,1024]{1,0:T(8,128)(2,1)} %bitcast.45, ...), custom_call_target="tpu_custom_call" | custom-call | flops 206158430208 | bytes 52428800 | tf_op jit(solution)/shard_map/back/pallas_call | solution.py:331
  134.0 47.3 %all_to_all.25 = bf16[16,384,256]{2,1,0:T(8,128)(2,1)} all-to-all(bf16[16,384,256]{2,1,0:T(8,128)(2,1)} %get-tuple-element.28), channel_id=1, replica_groups=mesh['tok'=8,'exp'=16] {'exp'}, dimensions={0} | all-to-all | bytes 6291456 | tf_op jit(solution)/shard_map/all_to_all | solution.py:385
  181.3 5.5 %merge.3 = bf16[64,128,256]{2,1,0:T(8,128)(2,1)} custom-call(s32[48]{0:T(128)} %reshape.107.ids, bf16[48,128,256]{2,1,0:T(8,128)(2,1)} %bitcast.27), custom_call_target="tpu_custom_call" | custom-call | bytes 14680064 | tf_op jit(solution)/shard_map/merge/pallas_call | solution.py:372
  186.9 3.8 %all-to-all-start.1 = ((bf16[16,128,256]{2,1,0:T(8,128)(2,1)}), bf16[16,128,256]{2,1,0:T(8,128)(2,1)S(1)}, u32[]{:S(2)}, u32[]{:S(2)}) async-start(bf16[16,128,256]{2,1,0:T(8,128)(2,1)} %bitcast.28), calls=%async_computation.2 | async-start | bytes 2097152 | tf_op jit(solution)/shard_map/all_to_all | solution.py:385
  190.9 3.2 %collective-permute-start.15 = (f32[3,128]{1,0:T(4,128)S(1)}, f32[3,128]{1,0:T(4,128)S(1)}, u32[]{:S(2)}, u32[]{:S(2)}) collective-permute-start(f32[3,128]{1,0:T(4,128)S(1)} %bitcast.41), channel_id=1, source_target_pairs={{32,0},{48,16},{64,32},{80,48},{96,64},{112,80},{0,96},{16,112},{3... | collective-permute-start | bytes 4616 | tf_op jit(solution)/shard_map/ppermute | solution.py:392
  194.2 1.5 collective-permute-done.17
  195.7 3.6 %collective-permute-done.16 = f32[3,128]{1,0:T(4,128)S(1)} collective-permute-done((f32[3,128]{1,0:T(4,128)S(1)}, f32[3,128]{1,0:T(4,128)S(1)}, u32[]{:S(2)}, u32[]{:S(2)}) %collective-permute-start.16) | collective-permute-done | bytes 1568 | tf_op jit(solution)/shard_map/ppermute | solution.py:392
  199.4 1.1 collective-permute-done.18
  200.5 6.9 %all-to-all-done.1.parts = bf16[16,128,256]{2,1,0:T(8,128)(2,1)S(1)} async-done(((bf16[16,128,256]{2,1,0:T(8,128)(2,1)}), bf16[16,128,256]{2,1,0:T(8,128)(2,1)S(1)}, u32[]{:S(2)}, u32[]{:S(2)}) %all-to-all-start.1) | async-done | bytes 1048608 | tf_op jit(solution)/shard_map/all_to_all | solution.py:385
  208.1 3.5 %all-to-all-start.4 = ((f32[16,6,128]{2,1,0:T(8,128)}), f32[16,6,128]{2,1,0:T(8,128)S(1)}, u32[]{:S(2)}, u32[]{:S(2)}) async-start(f32[16,6,128]{2,1,0:T(8,128)} %broadcast_in_dim.103), calls=%async_computation.6 | async-start | bytes 131072 | tf_op jit(solution)/shard_map/all_to_all | solution.py:385
  211.8 2.4 %merge.2 = bf16[8,128,256]{2,1,0:T(8,128)(2,1)} custom-call(s32[16]{0:T(128)} %get-tuple-element.34.ids, bf16[16,128,256]{2,1,0:T(8,128)(2,1)} %copy-done.2), custom_call_target="tpu_custom_call" | custom-call | bytes 3145728 | tf_op jit(solution)/shard_map/merge/pallas_call | solution.py:372
  214.2 5.0 %all-to-all-done.4 = f32[16,6,128]{2,1,0:T(8,128)S(1)} async-done(((f32[16,6,128]{2,1,0:T(8,128)}), f32[16,6,128]{2,1,0:T(8,128)S(1)}, u32[]{:S(2)}, u32[]{:S(2)}) %all-to-all-start.4) | async-done | bytes 49184 | tf_op jit(solution)/shard_map/all_to_all | solution.py:385
  220.1 1.0 reduce-scatter.5.cloned.1.call-done
  (108 shorter events, 9.0 us)
Async XLA Ops:
  7.2 39.4 %all-gather.2.cloned.1.call-start = ((), (), s32[]{:S(2)}) async-start(), calls=%async_computation.8 | async-start | bytes 4718592 | tf_op jit(solution)/shard_map/all_gather | solution.py:409
  7.2 30.4 %collective-permute-start.4 = (bf16[4096,1024]{1,0:T(8,128)(2,1)}, bf16[4096,1024]{1,0:T(8,128)(2,1)}, u32[]{:S(2)}, u32[]{:S(2)}) collective-permute-start(bf16[4096,1024]{1,0:T(8,128)(2,1)} %bitcast.43), channel_id=1, source_target_pairs={{0,16},{16,0},{32,48},{48,32},{64,80},{80,64},{96,112},{112,96},{1... | collective-permute-start | bytes 25165832 | tf_op jit(solution)/shard_map/ppermute | solution.py:396
  7.3 30.4 %collective-permute-start.5 = (bf16[1024,4096]{1,0:T(8,128)(2,1)}, bf16[1024,4096]{1,0:T(8,128)(2,1)}, u32[]{:S(2)}, u32[]{:S(2)}) collective-permute-start(bf16[1024,4096]{1,0:T(8,128)(2,1)} %bitcast.46), channel_id=1, source_target_pairs={{0,16},{16,0},{32,48},{48,32},{64,80},{80,64},{96,112},{112,96},{1... | collective-permute-start | bytes 25165832 | tf_op jit(solution)/shard_map/ppermute | solution.py:396
  12.4 25.3 %all-to-all-start = ((bf16[16,128,256]{2,1,0:T(8,128)(2,1)}), bf16[16,128,256]{2,1,0:T(8,128)(2,1)S(1)}, u32[]{:S(2)}, u32[]{:S(2)}) async-start(bf16[16,128,256]{2,1,0:T(8,128)(2,1)} %pick_blocks.2), calls=%async_computation | async-start | bytes 2097152 | tf_op jit(solution)/shard_map/all_to_all | solution.py:385
  19.6 7.9 %collective-permute-start = (f32[8,128]{1,0:T(8,128)S(1)}, f32[8,128]{1,0:T(8,128)S(1)}, u32[]{:S(2)}, u32[]{:S(2)}) collective-permute-start(f32[8,128]{1,0:T(8,128)S(1)} %bitcast.34), channel_id=1, source_target_pairs={{32,0},{48,16},{64,32},{80,48},{96,64},{112,80},{0,96},{16,112},{3... | collective-permute-start | bytes 12296 | tf_op jit(solution)/shard_map/ppermute | solution.py:392
  23.9 5.2 %collective-permute-start.1 = (f32[8,128]{1,0:T(8,128)S(1)}, f32[8,128]{1,0:T(8,128)S(1)}, u32[]{:S(2)}, u32[]{:S(2)}) collective-permute-start(f32[8,128]{1,0:T(8,128)S(1)} %bitcast.35), channel_id=1, source_target_pairs={{64,0},{80,16},{96,32},{112,48},{0,64},{16,80},{32,96},{48,112},{6... | collective-permute-start | bytes 12296 | tf_op jit(solution)/shard_map/ppermute | solution.py:392
  23.9 5.2 %collective-permute-start.2 = (f32[8,128]{1,0:T(8,128)S(1)}, f32[8,128]{1,0:T(8,128)S(1)}, u32[]{:S(2)}, u32[]{:S(2)}) collective-permute-start(f32[8,128]{1,0:T(8,128)S(1)} %bitcast.36), channel_id=1, source_target_pairs={{96,0},{112,16},{0,32},{16,48},{32,64},{48,80},{64,96},{80,112},{9... | collective-permute-start | bytes 12296 | tf_op jit(solution)/shard_map/ppermute | solution.py:392
  25.4 26.0 %copy-start.7 = (s32[16,6]{0,1:T(8,128)}, s32[16,6]{0,1:T(8,128)S(1)}, u32[]{:S(2)}) copy-start(s32[16,6]{0,1:T(8,128)S(1)} %get-tuple-element.31) | copy-start | bytes 1156
  25.8 25.6 %copy-start.13 = (s32[3]{0:T(128)}, s32[3]{0:T(128)S(1)}, u32[]{:S(2)}) copy-start(s32[3]{0:T(128)S(1)} %dynamic-slice_reduce_fusion.tiles) | copy-start | bytes 40
  29.1 3.4 %collective-permute-start.3 = (f32[32,128]{1,0:T(8,128)S(1)}, f32[32,128]{1,0:T(8,128)S(1)}, u32[]{:S(2)}, u32[]{:S(2)}) collective-permute-start(f32[32,128]{1,0:T(8,128)S(1)} %pad_maximum_fusion), channel_id=1, source_target_pairs={{0,16},{16,0},{32,48},{48,32},{64,80},{80,64},{96,112},{112,96},{1... | collective-permute-start | bytes 49160 | tf_op jit(solution)/shard_map/ppermute | solution.py:396
  37.7 22.3 %copy-start.3 = (bf16[16,128,256]{2,1,0:T(8,128)(2,1)}, bf16[16,128,256]{2,1,0:T(8,128)(2,1)S(1)}, u32[]{:S(2)}) copy-start(bf16[16,128,256]{2,1,0:T(8,128)(2,1)S(1)} %all-to-all-done.refs_0_) | copy-start | bytes 3145732
  37.7 26.7 %collective-permute-start.6 = (bf16[16,128,256]{2,1,0:T(8,128)(2,1)S(1)}, bf16[16,128,256]{2,1,0:T(8,128)(2,1)S(1)}, u32[]{:S(2)}, u32[]{:S(2)}) collective-permute-start(bf16[16,128,256]{2,1,0:T(8,128)(2,1)S(1)} %all-to-all-done.refs_0_), channel_id=1, source_target_pairs={{32,0},{48,16},{64,32},{80,48},{96,64},{112,80},{0,96},{16,112},{3... | collective-permute-start | bytes 3145736 | tf_op jit(solution)/shard_map/ppermute | solution.py:392
  41.8 24.3 %collective-permute-start.7 = (bf16[16,128,256]{2,1,0:T(8,128)(2,1)S(1)}, bf16[16,128,256]{2,1,0:T(8,128)(2,1)S(1)}, u32[]{:S(2)}, u32[]{:S(2)}) collective-permute-start(bf16[16,128,256]{2,1,0:T(8,128)(2,1)S(1)} %all-to-all-done.refs_0_), channel_id=1, source_target_pairs={{96,0},{112,16},{0,32},{16,48},{32,64},{48,80},{64,96},{80,112},{9... | collective-permute-start | bytes 3145736 | tf_op jit(solution)/shard_map/ppermute | solution.py:392
  51.4 58.6 %all-to-all-start.2 = ((bf16[16,384,256]{2,1,0:T(8,128)(2,1)}), bf16[16,384,256]{2,1,0:T(8,128)(2,1)}, u32[]{:S(2)}, u32[]{:S(2)}) async-start(bf16[16,384,256]{2,1,0:T(8,128)(2,1)} %bitcast.26), calls=%async_computation.3 | async-start | bytes 6291456 | tf_op jit(solution)/shard_map/all_to_all | solution.py:385
  60.0 126.9 %reduce-scatter.3.cloned.1.call-start = ((), (), s32[]{:S(2)}) async-start(), calls=%async_computation.7 | async-start | bytes 9437184 | tf_op jit(solution)/shard_map/reduce_scatter | solution.py:459
  60.0 21.8 %collective-permute-start.10 = (bf16[16,128,256]{2,1,0:T(8,128)(2,1)S(1)}, bf16[16,128,256]{2,1,0:T(8,128)(2,1)S(1)}, u32[]{:S(2)}, u32[]{:S(2)}) collective-permute-start(bf16[16,128,256]{2,1,0:T(8,128)(2,1)S(1)} %all-to-all-done.refs_0_), channel_id=1, source_target_pairs={{0,16},{16,0},{32,48},{48,32},{64,80},{80,64},{96,112},{112,96},{1... | collective-permute-start | bytes 3145736 | tf_op jit(solution)/shard_map/ppermute | solution.py:396
  64.4 20.3 %copy-start.4 = (bf16[16,128,256]{2,1,0:T(8,128)(2,1)}, bf16[16,128,256]{2,1,0:T(8,128)(2,1)S(1)}, u32[]{:S(2)}) copy-start(bf16[16,128,256]{2,1,0:T(8,128)(2,1)S(1)} %collective-permute-done.6.refs_1_) | copy-start | bytes 3145732
  64.4 12.8 %collective-permute-start.8 = (bf16[8,128,256]{2,1,0:T(8,128)(2,1)S(1)}, bf16[8,128,256]{2,1,0:T(8,128)(2,1)S(1)}, u32[]{:S(2)}, u32[]{:S(2)}) collective-permute-start(bf16[8,128,256]{2,1,0:T(8,128)(2,1)S(1)} %slice.10), channel_id=1, source_target_pairs={{32,0},{48,16},{64,32},{80,48},{96,64},{112,80},{0,96},{16,112},{3... | collective-permute-start | bytes 1572872 | tf_op jit(solution)/shard_map/ppermute | solution.py:392
  66.1 15.8 %collective-permute-start.11 = (bf16[16,128,256]{2,1,0:T(8,128)(2,1)S(1)}, bf16[16,128,256]{2,1,0:T(8,128)(2,1)S(1)}, u32[]{:S(2)}, u32[]{:S(2)}) collective-permute-start(bf16[16,128,256]{2,1,0:T(8,128)(2,1)S(1)} %collective-permute-done.6.refs_1_), channel_id=1, source_target_pairs={{0,16},{16,0},{32,48},{48,32},{64,80},{80,64},{96,112},{112,96},{1... | collective-permute-start | bytes 3145736 | tf_op jit(solution)/shard_map/ppermute | solution.py:396
  66.1 15.7 %collective-permute-start.12 = (bf16[16,128,256]{2,1,0:T(8,128)(2,1)S(1)}, bf16[16,128,256]{2,1,0:T(8,128)(2,1)S(1)}, u32[]{:S(2)}, u32[]{:S(2)}) collective-permute-start(bf16[16,128,256]{2,1,0:T(8,128)(2,1)S(1)} %collective-permute-done.7.refs_2_), channel_id=1, source_target_pairs={{0,16},{16,0},{32,48},{48,32},{64,80},{80,64},{96,112},{112,96},{1... | collective-permute-start | bytes 3145736 | tf_op jit(solution)/shard_map/ppermute | solution.py:396
  66.7 15.1 %collective-permute-start.9 = (bf16[8,128,256]{2,1,0:T(8,128)(2,1)S(1)}, bf16[8,128,256]{2,1,0:T(8,128)(2,1)S(1)}, u32[]{:S(2)}, u32[]{:S(2)}) collective-permute-start(bf16[8,128,256]{2,1,0:T(8,128)(2,1)S(1)} %slice.11), channel_id=1, source_target_pairs={{96,0},{112,16},{0,32},{16,48},{32,64},{48,80},{64,96},{80,112},{9... | collective-permute-start | bytes 1572872 | tf_op jit(solution)/shard_map/ppermute | solution.py:392
  77.3 5.7 %collective-permute-start.13 = (bf16[8,128,256]{2,1,0:T(8,128)(2,1)S(1)}, bf16[8,128,256]{2,1,0:T(8,128)(2,1)S(1)}, u32[]{:S(2)}, u32[]{:S(2)}) collective-permute-start(bf16[8,128,256]{2,1,0:T(8,128)(2,1)S(1)} %collective-permute-done.8.refs_3_), channel_id=1, source_target_pairs={{0,16},{16,0},{32,48},{48,32},{64,80},{80,64},{96,112},{112,96},{1... | collective-permute-start | bytes 1572872 | tf_op jit(solution)/shard_map/ppermute | solution.py:396
  81.9 2.8 %collective-permute-start.14 = (bf16[8,128,256]{2,1,0:T(8,128)(2,1)S(1)}, bf16[8,128,256]{2,1,0:T(8,128)(2,1)}, u32[]{:S(2)}, u32[]{:S(2)}) collective-permute-start(bf16[8,128,256]{2,1,0:T(8,128)(2,1)S(1)} %collective-permute-done.9.refs_4_), channel_id=1, source_target_pairs={{0,16},{16,0},{32,48},{48,32},{64,80},{80,64},{96,112},{112,96},{1... | collective-permute-start | bytes 1572872 | tf_op jit(solution)/shard_map/ppermute | solution.py:396
  109.8 111.3 %reduce-scatter.5.cloned.1.call-start = ((), (), s32[]{:S(2)}) async-start(), calls=%async_computation.9 | async-start | bytes 4718592 | tf_op jit(solution)/shard_map/reduce_scatter | solution.py:462
  186.8 24.8 %copy-start.12 = (s32[16]{0:T(128)S(1)}, s32[16]{0:T(128)}, u32[]{:S(2)}) copy-start(s32[16]{0:T(128)} %get-tuple-element.34.ids) | copy-start | bytes 196
  186.8 34.2 %copy-start.1 = (f32[1024,16]{0,1:T(8,128)S(1)}, f32[1024,16]{0,1:T(8,128)}, u32[]{:S(2)}) copy-start(f32[1024,16]{0,1:T(8,128)} %param.8) | copy-start | bytes 196612
  186.9 20.5 %all-to-all-start.1 = ((bf16[16,128,256]{2,1,0:T(8,128)(2,1)}), bf16[16,128,256]{2,1,0:T(8,128)(2,1)S(1)}, u32[]{:S(2)}, u32[]{:S(2)}) async-start(bf16[16,128,256]{2,1,0:T(8,128)(2,1)} %bitcast.28), calls=%async_computation.2 | async-start | bytes 2097152 | tf_op jit(solution)/shard_map/all_to_all | solution.py:385
  190.9 4.9 %collective-permute-start.17 = (f32[3,128]{1,0:T(4,128)S(1)}, f32[3,128]{1,0:T(4,128)S(1)}, u32[]{:S(2)}, u32[]{:S(2)}) collective-permute-start(f32[3,128]{1,0:T(4,128)S(1)} %bitcast.40), channel_id=1, source_target_pairs={{96,0},{112,16},{0,32},{16,48},{32,64},{48,80},{64,96},{80,112},{9... | collective-permute-start | bytes 4616 | tf_op jit(solution)/shard_map/ppermute | solution.py:392
  190.9 4.8 %collective-permute-start.15 = (f32[3,128]{1,0:T(4,128)S(1)}, f32[3,128]{1,0:T(4,128)S(1)}, u32[]{:S(2)}, u32[]{:S(2)}) collective-permute-start(f32[3,128]{1,0:T(4,128)S(1)} %bitcast.41), channel_id=1, source_target_pairs={{32,0},{48,16},{64,32},{80,48},{96,64},{112,80},{0,96},{16,112},{3... | collective-permute-start | bytes 4616 | tf_op jit(solution)/shard_map/ppermute | solution.py:392
  194.2 5.2 %collective-permute-start.16 = (f32[3,128]{1,0:T(4,128)S(1)}, f32[3,128]{1,0:T(4,128)S(1)}, u32[]{:S(2)}, u32[]{:S(2)}) collective-permute-start(f32[3,128]{1,0:T(4,128)S(1)} %bitcast.42), channel_id=1, source_target_pairs={{64,0},{80,16},{96,32},{112,48},{0,64},{16,80},{32,96},{48,112},{6... | collective-permute-start | bytes 4616 | tf_op jit(solution)/shard_map/ppermute | solution.py:392
  199.4 1.2 collective-permute-start.18
  208.1 11.1 %all-to-all-start.4 = ((f32[16,6,128]{2,1,0:T(8,128)}), f32[16,6,128]{2,1,0:T(8,128)S(1)}, u32[]{:S(2)}, u32[]{:S(2)}) async-start(f32[16,6,128]{2,1,0:T(8,128)} %broadcast_in_dim.103), calls=%async_computation.6 | async-start | bytes 131072 | tf_op jit(solution)/shard_map/all_to_all | solution.py:385
  (14 other events, 90.6 us)
Sparse Core Ops, SparseCore 0:
  9.7 36.8 all-gather.1
  109.9 51.7 reduce-scatter.2
  187.0 34.0 reduce-scatter.4
